TPU v7x, 32 devices: a whole 2x2x4 slice. The times are simulated.
32 devices in a mesh: groups: 2 (over y), row: 4 (over z), col: 4 (over x, core).
Axes of the slice: x: 2, y: 2, z: 4, core: 2. Of those that a mesh axis runs over, the one named last changes fastest.
Arguments:
- activations: bfloat16 [4096, 8192], P('groups', ('row', 'col')), parts along dimension 0, may hold values from -6 to 6
- basis_in: bfloat16 [16384, 512], P(('groups', 'row', 'col')), parts along dimension 0, may hold values from -0.09375 to 0.09375
- gradients: bfloat16 [4096, 28672], P('groups', 'row'), parts along dimension 0, may hold values from -6 to 6
- basis_out: bfloat16 [57344, 1536], P(('groups', 'row'), 'col'), parts along dimension 0, may hold values from -0.03125 to 0.03125
- token_ids: int32 [4, 512], replicated, may hold values from 0 to 31999, as said below
Outputs:
- correction: float32 [1024, 1536], P(('groups', 'row'), 'col'), parts along dimension 0
There are 2 independent parts, one for each index of `groups`. A program takes and returns all parts, laid end to end along the dimension named above; an argument that names none is the same for every part. Nothing has to cross between parts.
Inputs may be any that keep to these rules, and one draw needn't show every extreme that they name: `token_ids`: 0 marks padding and fills only the tail of a sequence; the first sequence has no padding and every sequence has 256 or more tokens that are not padding.
All inputs are finite; a program needn't handle non-finite values.
Results may differ from a plain program's by a relative error of at most 0.0034.
Values may be sent and summed in bfloat16 or wider, within the bound.
No kernel may reach another device: no remote copies, remote signals or barrier semaphores. Data moves between devices by JAX's collectives and lax.ppermute only.
A program may use at most 128 MiB of HBM per device.

v0:
```python
import jax
import jax.numpy as jnp
from jax import lax
from jax.sharding import PartitionSpec as P


def shards(activations, basis_in, gradients, basis_out, token_ids):
    sequences = token_ids.shape[0]
    keep_mask = (token_ids != 0).astype(jnp.float32)
    counts = jnp.sum(keep_mask, axis=1)
    scales = 1.0 / jnp.sqrt(counts)
    flat_keep = keep_mask.reshape(1, -1).astype(jnp.bfloat16)
    act_share = lax.psum_scatter(
        lax.dot_general(
            basis_in, activations, (((0,), (1,)), ((), ())), preferred_element_type=jnp.float32
        ),
        ("row", "col"),
        scatter_dimension=0,
        tiled=True,
    ).astype(jnp.bfloat16)
    act_local = lax.all_gather(act_share, "col", axis=0, tiled=True) * flat_keep
    partial_value = jnp.dot(gradients, basis_out, preferred_element_type=jnp.float32)
    rot_grad = lax.psum(partial_value, "row").astype(jnp.bfloat16)
    height = act_local.shape[0]
    width = rot_grad.shape[1]
    act_blocks = act_local.reshape(height, sequences, -1)
    grad_blocks = rot_grad.reshape(sequences, -1, width)
    products = jnp.einsum(
        "rsl,slc->rsc", act_blocks, grad_blocks, preferred_element_type=jnp.float32
    )
    products = products * scales[None, :, None]
    return jnp.mean(products * products, axis=1)


def solution(mesh):
    in_specs = (
        P("groups", ("row", "col")),
        P(("groups", "row", "col"), None),
        P("groups", "row"),
        P(("groups", "row"), "col"),
        P(),
    )
    out_specs = P(("groups", "row"), "col")
    return jax.shard_map(shards, mesh=mesh, in_specs=in_specs, out_specs=out_specs, check_vma=False)
```

profile of v0, /device:TPU:0, one launch (start us, length us, event | category | flops | bytes accessed | tf_op | source)
XLA Modules:
  0.0 193.2 jit_solution(9197925553515451777)
XLA Ops:
  6.5 0.0 copy-start
  6.5 0.0 reduce-scatter.2.cloned.1.call-start
  6.5 1.6 copy-done
  8.1 4.3 %fusion.6 = f32[512,2048]{1,0:T(8,128)} fusion(bf16[512,512]{1,0:T(8,128)(2,1)} %param.6, bf16[2048,512]{1,0:T(8,128)(2,1)S(1)} %copy-done), kind=kOutput, calls=%fused_computation.12 | convolution fusion | flops 1073741824 | bytes 6815744 | tf_op jit(solution)/shard_map/dot_general | solution.py:14
  12.4 0.0 copy-start.1
  12.4 0.0 reduce-scatter.2.cloned.1.call-update
  12.4 0.7 copy-done.1
  13.1 0.1 convert_reduce_fusion
  13.2 22.1 %fusion.5 = f32[2048,384]{1,0:T(8,128)} fusion(bf16[2048,7168]{1,0:T(8,128)(2,1)} %param.7, bf16[7168,384]{1,0:T(8,128)(2,1)} %param.8), kind=kOutput, calls=%fused_computation.11 | convolution fusion | flops 11274289152 | bytes 38010880 | tf_op jit(solution)/shard_map/dot_general | solution.py:22
  35.4 139.8 %all-reduce.1 = bf16[2048,384]{1,0:T(8,128)(2,1)} all-reduce(f32[2048,384]{1,0:T(8,128)} %fusion.5), channel_id=1, replica_groups=mesh['groups'=2,'row'=4,'col'=4] {'row'}, use_global_device_ids=true, to_apply=%region_0.0 | all-reduce | flops 786432 | bytes 4718592 | tf_op jit(solution)/shard_map/psum | solution.py:23
  175.2 0.0 reduce-scatter.2.cloned.1.call-done
  175.2 1.0 convert_element_type.21
  176.2 7.1 %all_gather.3 = bf16[128,2048]{1,0:T(8,128)(2,1)S(1)} all-gather(bf16[32,2048]{1,0:T(8,128)(2,1)S(1)} %convert_element_type.21), channel_id=1, replica_groups=mesh['groups'=2,'row'=4,'col'=4] {'col'}, dimensions={0}, use_global_device_ids=true | all-gather | bytes 655360 | tf_op jit(solution)/shard_map/all_gather | solution.py:21
  183.4 2.1 %fusion.1 = f32[384,128]{1,0:T(8,128)S(1)} fusion(bf16[4,512,384]{2,1,0:T(8,128)(2,1)} %bitcast.15, bf16[16,4,8,512]{3,2,1,0:T(8,128)(2,1)S(1)} %bitcast.16, f32[4]{0:T(128)S(1)} %sqrt.3), kind=kOutput, calls=%fused_computation.2 | convolution fusion | flops 201867264 | bytes 2293776 | tf_op jit(solution)/shard_map/rsl,slc->rsc/dot_general | solution.py:28
  185.5 0.8 copy.10
  (5 shorter events, 0.1 us)
Async XLA Ops:
  6.5 1.6 copy-start
  6.5 168.7 %reduce-scatter.2.cloned.1.call-start = ((), (), s32[]{:S(2)}) async-start(), calls=%async_computation.1 | async-start | bytes 4456448 | tf_op jit(solution)/shard_map/reduce_scatter | solution.py:13
  12.4 0.7 copy-start.1
Sparse Core Ops, SparseCore 0:
  12.5 95.6 reduce-scatter.1
where the time goes:
time: 194 us; the launch traced here: 193 us
  blocking collectives  147 us (76%)
  matrix products  28.5 us (15%)
  between operations  13.4 us (7%)
  local copies, waits for them, and re-layouts  3.08 us (2%)
    psum x1, blocking collectives, shards(): rot_grad = lax.psum(partial_value, 'row').astype(jnp.bfloat16)  140 us
    dot_general x1, matrix products, shards(): jnp.dot(gradients, basis_out, preferred_element_type=jnp.float32)  22.1 us
    all_gather x1, blocking collectives, shards(): act_local = lax.all_gather(act_share, 'col', axis=0, tiled=True) * flat_keep  7.15 us
    dot_general x1, matrix products, shards(): lax.dot_general(basis_in, activations, (((0,), (1,)), ((), ())), preferre...  4.27 us
  transfers between devices with their start and end apart: 1, of which 0 were waited for; matrix products, arithmetic and copies ran while one was open for 12% of the time, Pallas kernels for 0%

commit v1 on v0

--- a/solution.py
+++ b/solution.py
@@ -1,10 +1,21 @@
+import functools
+
 import jax
 import jax.numpy as jnp
 from jax import lax
+from jax.experimental import pallas as pl
+from jax.experimental.pallas import tpu as pltpu
 from jax.sharding import PartitionSpec as P
 
-
-def shards(activations, basis_in, gradients, basis_out, token_ids):
+VMEM = pl.BlockSpec(memory_space=pltpu.VMEM)
+SMEM = pl.BlockSpec(memory_space=pltpu.SMEM)
+ANY = pl.BlockSpec(memory_space=pl.ANY)
+ACT_UP = 4.0
+GRAD_UP = 8.0
+CUTS = 4
+
+
+def plain_shards(activations, basis_in, gradients, basis_out, token_ids):
     sequences = token_ids.shape[0]
     keep_mask = (token_ids != 0).astype(jnp.float32)
     counts = jnp.sum(keep_mask, axis=1)
@@ -32,6 +43,173 @@
     return jnp.mean(products * products, axis=1)
 
 
+def act_kernel(where, act, basis, send_far, send_near, keep_far, keep_near):
+    length = send_far.shape[2]
+    half = send_far.shape[1]
+    z, core = where[0], where[1]
+    for mine, far, near in ((False, send_far, send_near), (True, keep_far, keep_near)):
+        which = core if mine else 1 - core
+        weights = basis[:, pl.ds(pl.multiple_of(which * half, half), half)]
+        for slot, step in ((0, 1), (1, 3)):
+            rows = act[pl.ds(pl.multiple_of((z ^ step) * length, length), length), :]
+            far[slot] = lax.dot_general(
+                weights, rows, (((0,), (1,)), ((), ())), preferred_element_type=jnp.float32
+            )
+        for slot, step in ((0, 0), (1, 2)):
+            rows = act[pl.ds(pl.multiple_of((z ^ step) * length, length), length), :]
+            near[slot] = lax.dot_general(
+                weights, rows, (((0,), (1,)), ((), ())), preferred_element_type=jnp.float32
+            )
+
+
+def rotate_act(where, activations, basis_in, length):
+    half = basis_in.shape[1] // 2
+    shape = jax.ShapeDtypeStruct((2, half, length), jnp.float32)
+    return pl.pallas_call(
+        act_kernel,
+        in_specs=[SMEM, VMEM, VMEM],
+        out_specs=[VMEM] * 4,
+        out_shape=[shape] * 4,
+        compiler_params=pltpu.CompilerParams(vmem_limit_bytes=24 * 2**20),
+    )(where, activations, basis_in)
+
+
+def grad_kernel(block, gradients, basis, out, buffer, total, sems):
+    length, depth = buffer.shape
+    cut = depth // CUTS
+    start = pl.multiple_of(block[0] * length, length)
+    copies = []
+    for i in range(CUTS):
+        copy = pltpu.make_async_copy(
+            gradients.at[pl.ds(start, length), pl.ds(i * cut, cut)],
+            buffer.at[:, pl.ds(i * cut, cut)],
+            sems.at[i],
+        )
+        copy.start()
+        copies.append(copy)
+    for i in range(CUTS):
+        copies[i].wait()
+        part = lax.dot_general(
+            basis[i * cut : (i + 1) * cut, :],
+            buffer[:, i * cut : (i + 1) * cut],
+            (((0,), (1,)), ((), ())),
+            preferred_element_type=jnp.float32,
+        )
+        if i == 0:
+            total[...] = part
+        elif i < CUTS - 1:
+            total[...] += part
+        else:
+            out[...] = total[...] + part
+
+
+def rotate_grad(block, gradients, basis_out, length):
+    depth, width = basis_out.shape
+    return pl.pallas_call(
+        grad_kernel,
+        in_specs=[SMEM, ANY, VMEM],
+        out_specs=VMEM,
+        out_shape=jax.ShapeDtypeStruct((width, length), jnp.float32),
+        scratch_shapes=[
+            pltpu.VMEM((length, depth), jnp.bfloat16),
+            pltpu.VMEM((width, length), jnp.float32),
+            pltpu.SemaphoreType.DMA((CUTS,)),
+        ],
+        compiler_params=pltpu.CompilerParams(vmem_limit_bytes=24 * 2**20),
+        cost_estimate=pl.CostEstimate(
+            flops=2 * length * depth * width, bytes_accessed=2 * length * depth, transcendentals=0
+        ),
+    )(jnp.reshape(block, (1,)), gradients, basis_out)
+
+
+def tile_kernel(share, order, scale, act, grad, own, *sends):
+    weight = scale[0]
+    rows = own.shape[0]
+    for slot, out in enumerate((own, *sends)):
+        piece = act[pl.ds(pl.multiple_of(order[slot] * rows, rows), rows), :]
+        product = lax.dot_general(
+            piece, grad[...], (((1,), (1,)), ((), ())), preferred_element_type=jnp.float32
+        )
+        product = product * weight
+        out[...] = (product * product * share).astype(out.dtype)
+
+
+def make_tile(order, scale, act, grad, sequences):
+    rows, width = act.shape[0] // sequences, grad.shape[0]
+    return pl.pallas_call(
+        functools.partial(tile_kernel, 1.0 / sequences),
+        in_specs=[SMEM, SMEM, VMEM, VMEM],
+        out_specs=[VMEM] * sequences,
+        out_shape=[jax.ShapeDtypeStruct((rows, width), jnp.float32)]
+        + [jax.ShapeDtypeStruct((rows, width), jnp.bfloat16)] * (sequences - 1),
+        compiler_params=pltpu.CompilerParams(vmem_limit_bytes=16 * 2**20),
+    )(order, scale, act, grad)
+
+
+def swap(value, axis, step, size=4):
+    return lax.ppermute(value, axis, [(i, i ^ step) for i in range(size)])
+
+
+def pack(value, up):
+    return (value * up).astype(jnp.float16)
+
+
+def unpack(value, up):
+    return value.astype(jnp.float32) * (1.0 / up)
+
+
+def line_shards(activations, basis_in, gradients, basis_out, token_ids):
+    sequences, length = token_ids.shape
+    z = lax.axis_index("row").astype(jnp.int32)
+    place = lax.axis_index("col").astype(jnp.int32)
+    core, x = place & 1, place >> 1
+    quarter = basis_in.shape[1] // 4
+
+    send_far, send_near, keep_far, keep_near = rotate_act(
+        jnp.stack([z, core]), activations, basis_in, length
+    )
+    far = keep_far + unpack(swap(pack(send_far, ACT_UP), "col", 1), ACT_UP)
+    near = keep_near + unpack(swap(pack(send_near, ACT_UP), "col", 1), ACT_UP)
+
+    def over_x(value):
+        mine = lax.dynamic_slice_in_dim(value, x * quarter, quarter, 1)
+        other = lax.dynamic_slice_in_dim(value, (1 - x) * quarter, quarter, 1)
+        return mine + unpack(swap(pack(other, ACT_UP), "col", 2), ACT_UP)
+
+    far, near = over_x(far), over_x(near)
+
+    third = rotate_grad(z ^ 3, gradients, basis_out, length)
+    got_third = unpack(swap(pack(third, GRAD_UP), "row", 1), GRAD_UP)
+    second = rotate_grad(z ^ 2, gradients, basis_out, length)
+    first = rotate_grad(z ^ 1, gradients, basis_out, length)
+    got_first = unpack(swap(pack(first, GRAD_UP), "row", 1), GRAD_UP)
+    got_second = unpack(swap(pack(second + got_third, GRAD_UP), "row", 2), GRAD_UP)
+    own = rotate_grad(z, gradients, basis_out, length)
+
+    near = near + unpack(swap(pack(far, ACT_UP), "row", 1), ACT_UP)
+    act = near[0] + unpack(swap(pack(near[1], ACT_UP), "row", 2), ACT_UP)
+    keep_mask = (lax.dynamic_slice_in_dim(token_ids, z, 1, 0) != 0).astype(jnp.float32)
+    scale = 1.0 / jnp.sqrt(jnp.sum(keep_mask, axis=1))
+    act = act.astype(jnp.bfloat16) * keep_mask.astype(jnp.bfloat16)
+    across = swap(act, "col", 2)
+    pair = jnp.where(x == 0, jnp.stack([act, across]), jnp.stack([across, act]))
+    pair = pair.reshape(2 * quarter, length)
+    other = swap(pair, "col", 1)
+    whole = jnp.where(core == 0, jnp.stack([pair, other]), jnp.stack([other, pair]))
+    whole = whole.reshape(4 * quarter, length)
+
+    grad = (own + got_first + got_second).astype(jnp.bfloat16)
+    order = jnp.stack([z, z ^ 3, z ^ 2, z ^ 1])
+    tile, to_3, to_2, to_1 = make_tile(order, scale, whole, grad, sequences)
+    from_3, from_2, from_1 = swap(to_3, "row", 3), swap(to_2, "row", 2), swap(to_1, "row", 1)
+    return (
+        tile
+        + from_3.astype(jnp.float32)
+        + from_2.astype(jnp.float32)
+        + from_1.astype(jnp.float32)
+    )
+
+
 def solution(mesh):
     in_specs = (
         P("groups", ("row", "col")),
@@ -41,4 +219,10 @@
         P(),
     )
     out_specs = P(("groups", "row"), "col")
+    rows, columns = mesh.shape["row"], mesh.shape["col"]
+
+    def shards(*arrays):
+        fits = rows == 4 and columns == 4 and arrays[4].shape[0] == rows
+        return (line_shards if fits else plain_shards)(*arrays)
+
     return jax.shard_map(shards, mesh=mesh, in_specs=in_specs, out_specs=out_specs, check_vma=False)

time: 194 us -> 85.2 us (0.44)
  blocking collectives: 147 us -> 0 us
  matrix products: 28.5 us -> 0 us
  waiting for transfers between devices: 0.02 us -> 26 us
  Pallas kernels: 0 us -> 22.8 us
  starting transfers between devices: 0.01 us -> 17 us
  between operations: 13.4 us -> 0.85 us
  local copies, waits for them, and re-layouts: 3.08 us -> 10.3 us
  other arithmetic: 1.14 us -> 7.84 us
    psum x1 -> x0, blocking collectives: 140 us -> none  [shards(): rot_grad = lax.psum(partial_value, 'row').astype(jnp.bfloat16)]
    dot_general x3 -> x0, matrix products: 28.5 us -> none  [the longest x1 22.1 us: shards(): jnp.dot(gradients, basis_out, preferred_element_type=jnp.float32)]
    ppermute x0 -> x14, waiting for transfers between devices: none -> 26 us  [swap(): return lax.ppermute(value, axis, [(i, i ^ step) for i in range(size)])]
    pallas_call x0 -> x6, Pallas kernels: none -> 22.8 us  [the longest x4 19.9 us: rotate_grad(): pl.pallas_call(grad_kernel, in_specs=[SMEM, ANY, VMEM], out_specs=VMEM, o...]
    ppermute x0 -> x14, starting transfers between devices: none -> 17 us  [swap(): return lax.ppermute(value, axis, [(i, i ^ step) for i in range(size)])]
    unnamed x5 -> x16, local copies, waits for them, and re-layouts: 2.27 us -> 10.3 us
    all_gather x1 -> x0, blocking collectives: 7.15 us -> none  [shards(): act_local = lax.all_gather(act_share, 'col', axis=0, tiled=True) * flat_keep]
    convert_element_type x1 -> x11, other arithmetic: 0.97 us -> 4.55 us  [the longest x9 3.34 us: pack(): return (value * up).astype(jnp.float16)]
  transfers between devices with their start and end apart: 1 -> 14, of which waited for: 0 -> 5; matrix products, arithmetic and copies ran while one was open for 12% -> 7% of each run, Pallas kernels for 0% -> 23%
where the time goes in v1:
time: 85.2 us; the launch traced here: 84.9 us
  waiting for transfers between devices  26 us (31%)
  Pallas kernels  22.8 us (27%)
  starting transfers between devices  17 us (20%)
  local copies, waits for them, and re-layouts  10.3 us (12%)
  other arithmetic  7.84 us (9%)
    ppermute x14, waiting for transfers between devices, swap(): return lax.ppermute(value, axis, [(i, i ^ step) for i in range(size)])  26 us
    pallas_call x4, Pallas kernels, rotate_grad(): pl.pallas_call(grad_kernel, in_specs=[SMEM, ANY, VMEM], out_specs=VMEM, o...  19.9 us
    ppermute x14, starting transfers between devices, swap(): return lax.ppermute(value, axis, [(i, i ^ step) for i in range(size)])  17 us
    unnamed x16, local copies, waits for them, and re-layouts  10.3 us
    convert_element_type x9, other arithmetic, pack(): return (value * up).astype(jnp.float16)  3.34 us
    pallas_call x1, Pallas kernels, rotate_act(): pl.pallas_call(act_kernel, in_specs=[SMEM, VMEM, VMEM], out_specs=[VMEM]...  1.83 us
  transfers between devices with their start and end apart: 14, of which 5 were waited for; matrix products, arithmetic and copies ran while one was open for 7% of the time, Pallas kernels for 23%

profile of v1, /device:TPU:0, one launch (start us, length us, event | category | flops | bytes accessed | tf_op | source)
XLA Modules:
  0.0 84.9 jit_solution(17187064751745956291)
XLA Ops:
  0.1 1.6 %copy-done.3 = bf16[2048,512]{1,0:T(8,128)(2,1)S(1)} copy-done((bf16[2048,512]{1,0:T(8,128)(2,1)S(1)}, bf16[2048,512]{1,0:T(8,128)(2,1)}, u32[]{:S(2)}) %copy-start.3) | copy-done | bytes 2097176
  1.7 1.0 %copy-done.4 = bf16[512,512]{1,0:T(8,128)(2,1)S(1)} copy-done((bf16[512,512]{1,0:T(8,128)(2,1)S(1)}, bf16[512,512]{1,0:T(8,128)(2,1)}, u32[]{:S(2)}) %copy-start.4) | copy-done | bytes 524312
  2.7 1.8 %shard_map.55 = (f32[2,256,512]{2,1,0:T(8,128)S(1)}, f32[2,256,512]{2,1,0:T(8,128)S(1)}, f32[2,256,512]{2,1,0:T(8,128)S(1)}, f32[2,256,512]{2,1,0:T(8,128)S(1)}) custom-call(s32[2]{0:T(128)S(1)} %pad_add_fusion.1.where, bf16[2048,512]{1,0:T(8,128)(2,1)S(1)} %copy-done.3, bf16[512,512]{1,0:T(8,128)(2,1)S(1)} %copy-done.4), custom_call_target="tpu_custom_call" | custom-call | tf_op jit(solution)/shard_map/pallas_call | solution.py:68
  4.6 0.9 %multiply_convert_fusion = f16[2,256,512]{2,1,0:T(8,128)(2,1)} fusion(f32[2,256,512]{2,1,0:T(8,128)S(1)} %get-tuple-element.16), kind=kLoop, calls=%fused_computation.1 | loop fusion | flops 524288 | bytes 1572864 | tf_op jit(solution)/shard_map/convert_element_type | solution.py:154
  5.5 0.5 collective-permute-start.2
  6.2 2.6 %copy-done = bf16[7168,384]{1,0:T(8,128)(2,1)S(1)} copy-done((bf16[7168,384]{1,0:T(8,128)(2,1)S(1)}, bf16[7168,384]{1,0:T(8,128)(2,1)}, u32[]{:S(2)}) %copy-start) | copy-done | bytes 5505048
  8.7 4.9 %shard_map.59 = f32[384,512]{1,0:T(8,128)S(1)} custom-call(s32[1]{0:T(128)} %bitcast.1.block, bf16[2048,7168]{1,0:T(8,128)(2,1)} %gradients.7, bf16[7168,384]{1,0:T(8,128)(2,1)S(1)} %copy-done), custom_call_target="tpu_custom_call" | custom-call | flops 2818572288 | bytes 7340032 | tf_op jit(solution)/shard_map/pallas_call | solution.py:108
  13.6 0.8 multiply_convert_fusion.3
  14.4 3.0 %collective-permute-start.9 = (f16[384,512]{1,0:T(8,128)(2,1)}, f16[384,512]{1,0:T(8,128)(2,1)}, u32[]{:S(2)}, u32[]{:S(2)}) collective-permute-start(f16[384,512]{1,0:T(8,128)(2,1)} %multiply_convert_fusion.3), channel_id=1, source_target_pairs={{0,4},{4,0},{8,12},{12,8},{1,5},{5,1},{9,13},{13,9},{2,6},{6,2},{1... | collective-permute-start | bytes 1179656 | tf_op jit(solution)/shard_map/ppermute | solution.py:150
  17.4 2.6 %copy-done.1 = bf16[7168,384]{1,0:T(8,128)(2,1)S(1)} copy-done((bf16[7168,384]{1,0:T(8,128)(2,1)S(1)}, bf16[7168,384]{1,0:T(8,128)(2,1)}, u32[]{:S(2)}) %copy-start.1) | copy-done | bytes 5505048
  20.0 4.9 %shard_map.57 = f32[384,512]{1,0:T(8,128)S(1)} custom-call(s32[1]{0:T(128)} %bitcast.3.block, bf16[2048,7168]{1,0:T(8,128)(2,1)} %gradients.7, bf16[7168,384]{1,0:T(8,128)(2,1)S(1)} %copy-done.1), custom_call_target="tpu_custom_call" | custom-call | flops 2818572288 | bytes 7340032 | tf_op jit(solution)/shard_map/pallas_call | solution.py:108
  25.1 1.4 %multiply_add_fusion = f32[2,256,512]{2,1,0:T(8,128)S(1)} fusion(f32[2,256,512]{2,1,0:T(8,128)S(1)} %get-tuple-element.15, f16[2,256,512]{2,1,0:T(8,128)(2,1)} %collective-permute-done.2), kind=kLoop, calls=%fused_computation | loop fusion | flops 786432 | bytes 2621440 | tf_op jit(solution)/shard_map/add | solution.py:171
  26.5 2.0 %collective-permute-start.3 = (f16[2,128,512]{2,1,0:T(8,128)(2,1)S(1)}, f16[2,128,512]{2,1,0:T(8,128)(2,1)S(1)}, u32[]{:S(2)}, u32[]{:S(2)}) collective-permute-start(f16[2,128,512]{2,1,0:T(8,128)(2,1)S(1)} %multiply_convert_fusion.6), channel_id=1, source_target_pairs={{0,2},{1,3},{2,0},{3,1},{4,6},{5,7},{6,4},{7,5},{8,10},{9,11},{10,... | collective-permute-start | bytes 786440 | tf_op jit(solution)/shard_map/ppermute | solution.py:150
  28.9 6.9 %collective-permute-done.3 = f16[2,128,512]{2,1,0:T(8,128)(2,1)S(1)} collective-permute-done((f16[2,128,512]{2,1,0:T(8,128)(2,1)S(1)}, f16[2,128,512]{2,1,0:T(8,128)(2,1)S(1)}, u32[]{:S(2)}, u32[]{:S(2)}) %collective-permute-start.3) | collective-permute-done | bytes 262176 | tf_op jit(solution)/shard_map/ppermute | solution.py:150
  35.9 2.1 %collective-permute-start.4 = (f16[2,128,512]{2,1,0:T(8,128)(2,1)S(1)}, f16[2,128,512]{2,1,0:T(8,128)(2,1)S(1)}, u32[]{:S(2)}, u32[]{:S(2)}) collective-permute-start(f16[2,128,512]{2,1,0:T(8,128)(2,1)S(1)} %multiply_convert_fusion.5), channel_id=1, source_target_pairs={{0,4},{4,0},{8,12},{12,8},{1,5},{5,1},{9,13},{13,9},{2,6},{6,2},{1... | collective-permute-start | bytes 786440 | tf_op jit(solution)/shard_map/ppermute | solution.py:150
  38.0 2.6 %copy-done.2 = bf16[7168,384]{1,0:T(8,128)(2,1)S(1)} copy-done((bf16[7168,384]{1,0:T(8,128)(2,1)S(1)}, bf16[7168,384]{1,0:T(8,128)(2,1)}, u32[]{:S(2)}) %copy-start.2) | copy-done | bytes 5505048
  40.5 5.0 %shard_map.58 = f32[384,512]{1,0:T(8,128)S(1)} custom-call(s32[1]{0:T(128)} %bitcast.2.block, bf16[2048,7168]{1,0:T(8,128)(2,1)} %gradients.7, bf16[7168,384]{1,0:T(8,128)(2,1)S(1)} %copy-done.2), custom_call_target="tpu_custom_call" | custom-call | flops 2818572288 | bytes 7340032 | tf_op jit(solution)/shard_map/pallas_call | solution.py:108
  45.8 2.7 %collective-permute-start.5 = (f16[128,512]{1,0:T(8,128)(2,1)S(1)}, f16[128,512]{1,0:T(8,128)(2,1)S(1)}, u32[]{:S(2)}, u32[]{:S(2)}) collective-permute-start(f16[128,512]{1,0:T(8,128)(2,1)S(1)} %fusion.4), channel_id=1, source_target_pairs={{0,8},{4,12},{8,0},{12,4},{1,9},{5,13},{9,1},{13,5},{2,10},{6,14},... | collective-permute-start | bytes 393224 | tf_op jit(solution)/shard_map/ppermute | solution.py:150
  48.4 1.2 %multiply_convert_fusion.2 = f16[384,512]{1,0:T(8,128)(2,1)S(1)} fusion(f32[384,512]{1,0:T(8,128)S(1)} %shard_map.58, f16[384,512]{1,0:T(8,128)(2,1)} %collective-permute-done.9), kind=kLoop, calls=%fused_computation.5 | loop fusion | flops 983040 | bytes 1572864 | tf_op jit(solution)/shard_map/convert_element_type | solution.py:154
  49.6 0.4 collective-permute-start.10
  50.0 12.2 %collective-permute-done.5 = f16[128,512]{1,0:T(8,128)(2,1)S(1)} collective-permute-done((f16[128,512]{1,0:T(8,128)(2,1)S(1)}, f16[128,512]{1,0:T(8,128)(2,1)S(1)}, u32[]{:S(2)}, u32[]{:S(2)}) %collective-permute-start.5) | collective-permute-done | bytes 131104 | tf_op jit(solution)/shard_map/ppermute | solution.py:150
  62.3 1.6 %collective-permute-start.6 = (bf16[128,512]{1,0:T(8,128)(2,1)S(1)}, bf16[128,512]{1,0:T(8,128)(2,1)S(1)}, u32[]{:S(2)}, u32[]{:S(2)}) collective-permute-start(bf16[128,512]{1,0:T(8,128)(2,1)S(1)} %fusion.3), channel_id=1, source_target_pairs={{0,2},{1,3},{2,0},{3,1},{4,6},{5,7},{6,4},{7,5},{8,10},{9,11},{10,... | collective-permute-start | bytes 393224 | tf_op jit(solution)/shard_map/ppermute | solution.py:150
  63.9 5.1 %shard_map.56 = f32[384,512]{1,0:T(8,128)S(1)} custom-call(s32[1]{0:T(128)} %bitcast.block, bf16[2048,7168]{1,0:T(8,128)(2,1)} %gradients.7, bf16[7168,384]{1,0:T(8,128)(2,1)S(1)} %bitcast.23), custom_call_target="tpu_custom_call" | custom-call | flops 2818572288 | bytes 7340032 | tf_op jit(solution)/shard_map/pallas_call | solution.py:108
  69.0 0.6 fusion.5
  70.4 1.2 %add_convert_fusion.grad = bf16[384,512]{1,0:T(8,128)(2,1)S(1)} fusion(f16[384,512]{1,0:T(8,128)(2,1)S(1)} %collective-permute-done.10, f32[384,512]{1,0:T(8,128)S(1)} %shard_map.56, f16[384,512]{1,0:T(8,128)(2,1)} %collective-permute-done.8), kind=kLoop, calls=%fused_computation.4 | loop fusion | flops 1376256 | bytes 1966080 | tf_op jit(solution)/shard_map/convert_element_type | solution.py:201
  71.6 0.3 collective-permute-done.7
  72.0 1.1 %shard_map.60 = (f32[128,384]{1,0:T(8,128)S(1)}, bf16[128,384]{1,0:T(8,128)(2,1)S(1)}, bf16[128,384]{1,0:T(8,128)(2,1)S(1)}, bf16[128,384]{1,0:T(8,128)(2,1)S(1)}) custom-call(s32[4]{0:T(128)S(1)} %pad_add_fusion.order, f32[1]{0:T(128)} %bitcast.4.scale, bf16[512,512]{1,0:T(8,128)(2,1)S(1)} %bitcast.24, bf16[384,512]{1,0:T(8,128)(2,1)S(1)} %add_convert_fusion.grad), custom_call_target="tpu_custom_call" | custom-call | tf_op jit(solution)/shard_map/pallas_call | solution.py:139
  73.2 1.7 %collective-permute-start.11 = (bf16[128,384]{1,0:T(8,128)(2,1)S(1)}, bf16[128,384]{1,0:T(8,128)(2,1)S(1)}, u32[]{:S(2)}, u32[]{:S(2)}) collective-permute-start(bf16[128,384]{1,0:T(8,128)(2,1)S(1)} %get-tuple-element.18), channel_id=1, source_target_pairs={{0,12},{4,8},{8,4},{12,0},{1,13},{5,9},{9,5},{13,1},{2,14},{6,10},... | collective-permute-start | bytes 294920 | tf_op jit(solution)/shard_map/ppermute | solution.py:150
  74.8 2.8 %collective-permute-start.13 = (bf16[128,384]{1,0:T(8,128)(2,1)S(1)}, bf16[128,384]{1,0:T(8,128)(2,1)S(1)}, u32[]{:S(2)}, u32[]{:S(2)}) collective-permute-start(bf16[128,384]{1,0:T(8,128)(2,1)S(1)} %get-tuple-element.20), channel_id=1, source_target_pairs={{0,4},{4,0},{8,12},{12,8},{1,5},{5,1},{9,13},{13,9},{2,6},{6,2},{1... | collective-permute-start | bytes 294920 | tf_op jit(solution)/shard_map/ppermute | solution.py:150
  77.6 3.1 %collective-permute-done.11 = bf16[128,384]{1,0:T(8,128)(2,1)S(1)} collective-permute-done((bf16[128,384]{1,0:T(8,128)(2,1)S(1)}, bf16[128,384]{1,0:T(8,128)(2,1)S(1)}, u32[]{:S(2)}, u32[]{:S(2)}) %collective-permute-start.11) | collective-permute-done | bytes 98336 | tf_op jit(solution)/shard_map/ppermute | solution.py:150
  80.8 3.4 %collective-permute-done.12 = bf16[128,384]{1,0:T(8,128)(2,1)S(1)} collective-permute-done((bf16[128,384]{1,0:T(8,128)(2,1)S(1)}, bf16[128,384]{1,0:T(8,128)(2,1)S(1)}, u32[]{:S(2)}, u32[]{:S(2)}) %collective-permute-start.12) | collective-permute-done | bytes 98336 | tf_op jit(solution)/shard_map/ppermute | solution.py:150
  84.1 0.7 convert_add_fusion
  (40 shorter events, 1.5 us)
Async XLA Ops:
  0.1 1.6 %copy-start.3 = (bf16[2048,512]{1,0:T(8,128)(2,1)S(1)}, bf16[2048,512]{1,0:T(8,128)(2,1)}, u32[]{:S(2)}) copy-start(bf16[2048,512]{1,0:T(8,128)(2,1)} %act.1) | copy-start | bytes 6291460
  1.7 1.0 %copy-start.4 = (bf16[512,512]{1,0:T(8,128)(2,1)S(1)}, bf16[512,512]{1,0:T(8,128)(2,1)}, u32[]{:S(2)}) copy-start(bf16[512,512]{1,0:T(8,128)(2,1)} %basis.5) | copy-start | bytes 1572868
  5.5 19.6 %collective-permute-start.2 = (f16[2,256,512]{2,1,0:T(8,128)(2,1)}, f16[2,256,512]{2,1,0:T(8,128)(2,1)}, u32[]{:S(2)}, u32[]{:S(2)}) collective-permute-start(f16[2,256,512]{2,1,0:T(8,128)(2,1)} %multiply_convert_fusion), channel_id=1, source_target_pairs={{0,1},{1,0},{2,3},{3,2},{4,5},{5,4},{6,7},{7,6},{8,9},{9,8},{10,11... | collective-permute-start | bytes 1572872 | tf_op jit(solution)/shard_map/ppermute | solution.py:150
  6.1 22.4 %collective-permute-start = (f16[2,256,512]{2,1,0:T(8,128)(2,1)S(1)}, f16[2,256,512]{2,1,0:T(8,128)(2,1)S(1)}, u32[]{:S(2)}, u32[]{:S(2)}) collective-permute-start(f16[2,256,512]{2,1,0:T(8,128)(2,1)S(1)} %multiply_convert_fusion.1), channel_id=1, source_target_pairs={{0,1},{1,0},{2,3},{3,2},{4,5},{5,4},{6,7},{7,6},{8,9},{9,8},{10,11... | collective-permute-start | bytes 1572872 | tf_op jit(solution)/shard_map/ppermute | solution.py:150
  6.2 2.6 %copy-start = (bf16[7168,384]{1,0:T(8,128)(2,1)S(1)}, bf16[7168,384]{1,0:T(8,128)(2,1)}, u32[]{:S(2)}) copy-start(bf16[7168,384]{1,0:T(8,128)(2,1)} %basis.9) | copy-start | bytes 16515076
  14.4 34.0 %collective-permute-start.9 = (f16[384,512]{1,0:T(8,128)(2,1)}, f16[384,512]{1,0:T(8,128)(2,1)}, u32[]{:S(2)}, u32[]{:S(2)}) collective-permute-start(f16[384,512]{1,0:T(8,128)(2,1)} %multiply_convert_fusion.3), channel_id=1, source_target_pairs={{0,4},{4,0},{8,12},{12,8},{1,5},{5,1},{9,13},{13,9},{2,6},{6,2},{1... | collective-permute-start | bytes 1179656 | tf_op jit(solution)/shard_map/ppermute | solution.py:150
  17.4 2.6 %copy-start.1 = (bf16[7168,384]{1,0:T(8,128)(2,1)S(1)}, bf16[7168,384]{1,0:T(8,128)(2,1)}, u32[]{:S(2)}) copy-start(bf16[7168,384]{1,0:T(8,128)(2,1)} %basis.9) | copy-start | bytes 16515076
  20.0 5.0 %copy-start.5 = (s32[4,512]{1,0:T(4,128)S(1)}, s32[4,512]{1,0:T(4,128)}, u32[]{:S(2)}) copy-start(s32[4,512]{1,0:T(4,128)} %param.9) | copy-start | bytes 24580
  24.9 45.5 %collective-permute-start.8 = (f16[384,512]{1,0:T(8,128)(2,1)S(1)}, f16[384,512]{1,0:T(8,128)(2,1)}, u32[]{:S(2)}, u32[]{:S(2)}) collective-permute-start(f16[384,512]{1,0:T(8,128)(2,1)S(1)} %multiply_convert_fusion.4), channel_id=1, source_target_pairs={{0,4},{4,0},{8,12},{12,8},{1,5},{5,1},{9,13},{13,9},{2,6},{6,2},{1... | collective-permute-start | bytes 1179656 | tf_op jit(solution)/shard_map/ppermute | solution.py:150
  25.1 38.8 %slice-start = ((s8[5505024]{0:T(1024)(128)(4,1)}), s8[4194304]{0:T(1024)(128)(4,1)S(1)}, s32[]{:S(2)}) async-start(s8[5505024]{0:T(1024)(128)(4,1)} %bitcast.22), calls=%async_computation | async-start | bytes 8388608
  26.5 9.3 %collective-permute-start.3 = (f16[2,128,512]{2,1,0:T(8,128)(2,1)S(1)}, f16[2,128,512]{2,1,0:T(8,128)(2,1)S(1)}, u32[]{:S(2)}, u32[]{:S(2)}) collective-permute-start(f16[2,128,512]{2,1,0:T(8,128)(2,1)S(1)} %multiply_convert_fusion.6), channel_id=1, source_target_pairs={{0,2},{1,3},{2,0},{3,1},{4,6},{5,7},{6,4},{7,5},{8,10},{9,11},{10,... | collective-permute-start | bytes 786440 | tf_op jit(solution)/shard_map/ppermute | solution.py:150
  28.7 16.9 %collective-permute-start.1 = (f16[2,128,512]{2,1,0:T(8,128)(2,1)S(1)}, f16[2,128,512]{2,1,0:T(8,128)(2,1)S(1)}, u32[]{:S(2)}, u32[]{:S(2)}) collective-permute-start(f16[2,128,512]{2,1,0:T(8,128)(2,1)S(1)} %multiply_convert_fusion.7), channel_id=1, source_target_pairs={{0,2},{1,3},{2,0},{3,1},{4,6},{5,7},{6,4},{7,5},{8,10},{9,11},{10,... | collective-permute-start | bytes 786440 | tf_op jit(solution)/shard_map/ppermute | solution.py:150
  35.9 9.7 %collective-permute-start.4 = (f16[2,128,512]{2,1,0:T(8,128)(2,1)S(1)}, f16[2,128,512]{2,1,0:T(8,128)(2,1)S(1)}, u32[]{:S(2)}, u32[]{:S(2)}) collective-permute-start(f16[2,128,512]{2,1,0:T(8,128)(2,1)S(1)} %multiply_convert_fusion.5), channel_id=1, source_target_pairs={{0,4},{4,0},{8,12},{12,8},{1,5},{5,1},{9,13},{13,9},{2,6},{6,2},{1... | collective-permute-start | bytes 786440 | tf_op jit(solution)/shard_map/ppermute | solution.py:150
  38.0 2.6 %copy-start.2 = (bf16[7168,384]{1,0:T(8,128)(2,1)S(1)}, bf16[7168,384]{1,0:T(8,128)(2,1)}, u32[]{:S(2)}) copy-start(bf16[7168,384]{1,0:T(8,128)(2,1)} %basis.9) | copy-start | bytes 16515076
  40.5 23.3 %slice-start.1 = ((s8[5505024]{0:T(1024)(128)(4,1)}), s8[1310720]{0:T(1024)(128)(4,1)S(1)}, s32[]{:S(2)}) async-start(s8[5505024]{0:T(1024)(128)(4,1)} %bitcast.22), calls=%async_computation.1 | async-start | bytes 2621440
  45.8 16.5 %collective-permute-start.5 = (f16[128,512]{1,0:T(8,128)(2,1)S(1)}, f16[128,512]{1,0:T(8,128)(2,1)S(1)}, u32[]{:S(2)}, u32[]{:S(2)}) collective-permute-start(f16[128,512]{1,0:T(8,128)(2,1)S(1)} %fusion.4), channel_id=1, source_target_pairs={{0,8},{4,12},{8,0},{12,4},{1,9},{5,13},{9,1},{13,5},{2,10},{6,14},... | collective-permute-start | bytes 393224 | tf_op jit(solution)/shard_map/ppermute | solution.py:150
  49.6 20.8 %collective-permute-start.10 = (f16[384,512]{1,0:T(8,128)(2,1)S(1)}, f16[384,512]{1,0:T(8,128)(2,1)S(1)}, u32[]{:S(2)}, u32[]{:S(2)}) collective-permute-start(f16[384,512]{1,0:T(8,128)(2,1)S(1)} %multiply_convert_fusion.2), channel_id=1, source_target_pairs={{0,8},{4,12},{8,0},{12,4},{1,9},{5,13},{9,1},{13,5},{2,10},{6,14},... | collective-permute-start | bytes 1179656 | tf_op jit(solution)/shard_map/ppermute | solution.py:150
  62.3 8.0 %collective-permute-start.6 = (bf16[128,512]{1,0:T(8,128)(2,1)S(1)}, bf16[128,512]{1,0:T(8,128)(2,1)S(1)}, u32[]{:S(2)}, u32[]{:S(2)}) collective-permute-start(bf16[128,512]{1,0:T(8,128)(2,1)S(1)} %fusion.3), channel_id=1, source_target_pairs={{0,2},{1,3},{2,0},{3,1},{4,6},{5,7},{6,4},{7,5},{8,10},{9,11},{10,... | collective-permute-start | bytes 393224 | tf_op jit(solution)/shard_map/ppermute | solution.py:150
  70.3 1.6 %collective-permute-start.7 = (bf16[256,512]{1,0:T(8,128)(2,1)S(1)}, bf16[256,512]{1,0:T(8,128)(2,1)S(1)}, u32[]{:S(2)}, u32[]{:S(2)}) collective-permute-start(bf16[256,512]{1,0:T(8,128)(2,1)S(1)} %bitcast.25), channel_id=1, source_target_pairs={{0,1},{1,0},{2,3},{3,2},{4,5},{5,4},{6,7},{7,6},{8,9},{9,8},{10,11... | collective-permute-start | bytes 786440 | tf_op jit(solution)/shard_map/ppermute | solution.py:150
  73.2 7.6 %collective-permute-start.11 = (bf16[128,384]{1,0:T(8,128)(2,1)S(1)}, bf16[128,384]{1,0:T(8,128)(2,1)S(1)}, u32[]{:S(2)}, u32[]{:S(2)}) collective-permute-start(bf16[128,384]{1,0:T(8,128)(2,1)S(1)} %get-tuple-element.18), channel_id=1, source_target_pairs={{0,12},{4,8},{8,4},{12,0},{1,13},{5,9},{9,5},{13,1},{2,14},{6,10},... | collective-permute-start | bytes 294920 | tf_op jit(solution)/shard_map/ppermute | solution.py:150
  74.8 9.3 %collective-permute-start.12 = (bf16[128,384]{1,0:T(8,128)(2,1)S(1)}, bf16[128,384]{1,0:T(8,128)(2,1)S(1)}, u32[]{:S(2)}, u32[]{:S(2)}) collective-permute-start(bf16[128,384]{1,0:T(8,128)(2,1)S(1)} %get-tuple-element.19), channel_id=1, source_target_pairs={{0,8},{4,12},{8,0},{12,4},{1,9},{5,13},{9,1},{13,5},{2,10},{6,14},... | collective-permute-start | bytes 294920 | tf_op jit(solution)/shard_map/ppermute | solution.py:150
  74.8 9.3 %collective-permute-start.13 = (bf16[128,384]{1,0:T(8,128)(2,1)S(1)}, bf16[128,384]{1,0:T(8,128)(2,1)S(1)}, u32[]{:S(2)}, u32[]{:S(2)}) collective-permute-start(bf16[128,384]{1,0:T(8,128)(2,1)S(1)} %get-tuple-element.20), channel_id=1, source_target_pairs={{0,4},{4,0},{8,12},{12,8},{1,5},{5,1},{9,13},{13,9},{2,6},{6,2},{1... | collective-permute-start | bytes 294920 | tf_op jit(solution)/shard_map/ppermute | solution.py:150

commit v2 on v0

--- a/solution.py
+++ b/solution.py
@@ -1,10 +1,19 @@
 import jax
 import jax.numpy as jnp
 from jax import lax
+from jax.experimental import pallas as pl
+from jax.experimental.pallas import tpu as pltpu
 from jax.sharding import PartitionSpec as P
 
-
-def shards(activations, basis_in, gradients, basis_out, token_ids):
+VMEM = pl.BlockSpec(memory_space=pltpu.VMEM)
+SMEM = pl.BlockSpec(memory_space=pltpu.SMEM)
+HBM = pl.BlockSpec(memory_space=pltpu.HBM)
+ACT_UP = 4.0
+GRAD_UP = 8.0
+CUT = 1024
+
+
+def plain_shards(activations, basis_in, gradients, basis_out, token_ids):
     sequences = token_ids.shape[0]
     keep_mask = (token_ids != 0).astype(jnp.float32)
     counts = jnp.sum(keep_mask, axis=1)
@@ -32,6 +41,252 @@
     return jnp.mean(products * products, axis=1)
 
 
+def in_hbm(value):
+    return pltpu.with_memory_space_constraint(value, pltpu.HBM)
+
+
+def columns_by_rows(weights, rows):
+    return lax.dot_general(
+        weights, rows, (((0,), (1,)), ((), ())), preferred_element_type=jnp.float32
+    )
+
+
+def pieces(depth):
+    return [(at, min(CUT, depth - at)) for at in range(0, depth, CUT)]
+
+
+def fetch_block(block, gradients, buffer, sems):
+    length, depth = buffer.shape
+    start = pl.multiple_of(block * length, length)
+    return [
+        pltpu.make_async_copy(
+            gradients.at[pl.ds(start, length), pl.ds(at, size)],
+            buffer.at[:, pl.ds(at, size)],
+            sems.at[i],
+        )
+        for i, (at, size) in enumerate(pieces(depth))
+    ]
+
+
+def rotate_block(copies, weights, buffer, total, out):
+    edges = pieces(buffer.shape[1])
+    for i, (at, size) in enumerate(edges):
+        for copy in copies[i]:
+            copy.wait()
+        part = columns_by_rows(weights[at : at + size, :], buffer[:, at : at + size])
+        if i == 0:
+            total[...] = part
+        elif i < len(edges) - 1:
+            total[...] += part
+        else:
+            out[...] = total[...] + part
+
+
+def first_kernel(block, gradients, basis, out, weights, buffer, total, grad_sems, basis_sems):
+    copies = []
+    edges = pieces(buffer.shape[1])
+    for i, copy in enumerate(fetch_block(block[0], gradients, buffer, grad_sems)):
+        at, size = edges[i]
+        part = pltpu.make_async_copy(
+            basis.at[pl.ds(at, size), :], weights.at[pl.ds(at, size), :], basis_sems.at[i]
+        )
+        part.start()
+        copy.start()
+        copies.append((part, copy))
+    rotate_block(copies, weights, buffer, total, out)
+
+
+def rotate_first(block, gradients, basis_out, length):
+    depth, width = basis_out.shape
+    steps = len(pieces(depth))
+    return pl.pallas_call(
+        first_kernel,
+        in_specs=[SMEM, HBM, HBM],
+        out_specs=VMEM,
+        out_shape=jax.ShapeDtypeStruct((width, length), jnp.float32),
+        scratch_shapes=[
+            pltpu.VMEM((depth, width), basis_out.dtype),
+            pltpu.VMEM((length, depth), jnp.bfloat16),
+            pltpu.VMEM((width, length), jnp.float32),
+            pltpu.SemaphoreType.DMA((steps,)),
+            pltpu.SemaphoreType.DMA((steps,)),
+        ],
+        compiler_params=pltpu.CompilerParams(vmem_limit_bytes=18 * 2**20),
+        cost_estimate=pl.CostEstimate(
+            flops=2 * length * depth * width,
+            bytes_accessed=2 * depth * (length + width),
+            transcendentals=0,
+        ),
+    )(jnp.reshape(block, (1,)), in_hbm(gradients), in_hbm(basis_out))
+
+
+def grad_kernel(block, gradients, basis, out, buffer, total, sems):
+    copies = fetch_block(block[0], gradients, buffer, sems)
+    for copy in copies:
+        copy.start()
+    rotate_block([(copy,) for copy in copies], basis, buffer, total, out)
+
+
+def rotate_grad(block, gradients, basis, length):
+    depth, width = basis.shape
+    return pl.pallas_call(
+        grad_kernel,
+        in_specs=[SMEM, HBM, VMEM],
+        out_specs=VMEM,
+        out_shape=jax.ShapeDtypeStruct((width, length), jnp.float32),
+        scratch_shapes=[
+            pltpu.VMEM((length, depth), jnp.bfloat16),
+            pltpu.VMEM((width, length), jnp.float32),
+            pltpu.SemaphoreType.DMA((len(pieces(depth)),)),
+        ],
+        compiler_params=pltpu.CompilerParams(vmem_limit_bytes=12 * 2**20),
+        cost_estimate=pl.CostEstimate(flops=1, bytes_accessed=1, transcendentals=0),
+    )(jnp.reshape(block, (1,)), in_hbm(gradients), pltpu.with_memory_space_constraint(basis, pltpu.VMEM))
+
+
+def act_kernel(where, act, basis, far_act, far_basis, *outs):
+    quarter, length = outs[0].shape
+    z, core, x = where[0], where[1], where[2]
+    span = pl.ds(pl.multiple_of(core * 2 * quarter, 2 * quarter), 2 * quarter)
+    near = basis[:, span]
+    far = far_basis[:, span]
+    for i, step in enumerate((3, 2, 1, 0)):
+        rows = pl.ds(pl.multiple_of((z ^ step) * length, length), length)
+        product = columns_by_rows(near, act[rows, :]) + columns_by_rows(far, far_act[rows, :])
+        low, high = product[:quarter], product[quarter:]
+        outs[2 * i][...] = jnp.where(x == 0, low, high)
+        outs[2 * i + 1][...] = jnp.where(x == 0, high, low)
+
+
+def rotate_act(where, activations, basis_in, far_act, far_basis, length):
+    shape = jax.ShapeDtypeStruct((basis_in.shape[1] // 4, length), jnp.float32)
+    return pl.pallas_call(
+        act_kernel,
+        in_specs=[SMEM, VMEM, VMEM, VMEM, VMEM],
+        out_specs=[VMEM] * 8,
+        out_shape=[shape] * 8,
+        compiler_params=pltpu.CompilerParams(vmem_limit_bytes=12 * 2**20),
+        cost_estimate=pl.CostEstimate(
+            flops=2 * activations.size * basis_in.shape[1],
+            bytes_accessed=4 * activations.size,
+            transcendentals=0,
+        ),
+    )(where, activations, basis_in, far_act, far_basis)
+
+
+def tile_kernel(order, ids, act, grad, own, *sends):
+    sequences, rows = ids.shape[0], own.shape[0]
+    keep = (ids[pl.ds(order[0], 1), :] != 0).astype(jnp.float32)
+    weight = 1.0 / jnp.sqrt(jnp.sum(keep, axis=1, keepdims=True))
+    keep = keep.astype(jnp.bfloat16)
+    for slot, out in enumerate((own, *sends)):
+        piece = act[pl.ds(pl.multiple_of(order[slot] * rows, rows), rows), :] * keep
+        product = lax.dot_general(
+            piece, grad[...], (((1,), (1,)), ((), ())), preferred_element_type=jnp.float32
+        )
+        product = product * weight
+        out[...] = (product * product * (1.0 / sequences)).astype(out.dtype)
+
+
+def make_tile(order, token_ids, act, grad):
+    sequences = token_ids.shape[0]
+    rows, width = act.shape[0] // sequences, grad.shape[0]
+    return pl.pallas_call(
+        tile_kernel,
+        in_specs=[SMEM, VMEM, VMEM, VMEM],
+        out_specs=[VMEM] * sequences,
+        out_shape=[jax.ShapeDtypeStruct((rows, width), jnp.float32)]
+        + [jax.ShapeDtypeStruct((rows, width), jnp.bfloat16)] * (sequences - 1),
+        compiler_params=pltpu.CompilerParams(vmem_limit_bytes=16 * 2**20),
+    )(order, token_ids, act, grad)
+
+
+def swap(value, axis, step, size=4):
+    return lax.ppermute(value, axis, [(i, i ^ step) for i in range(size)])
+
+
+def pack(value, up):
+    return (value * up).astype(jnp.float16)
+
+
+def unpack(value, up):
+    return value.astype(jnp.float32) * (1.0 / up)
+
+
+def line_shards(activations, basis_in, gradients, basis_out, token_ids):
+    length = token_ids.shape[1]
+    z = lax.axis_index("row").astype(jnp.int32)
+    place = lax.axis_index("col").astype(jnp.int32)
+    core, x = place & 1, place >> 1
+    quarter = basis_in.shape[1] // 4
+    middle = basis_out.shape[1] // 3 * 2
+    tie = lax.optimization_barrier
+    order = jnp.stack([z, z ^ 3, z ^ 2, z ^ 1])
+    where = jnp.stack([z, core, x])
+
+    far_act, far_basis = swap(activations, "col", 1), swap(basis_in, "col", 1)
+    third = rotate_first(z ^ 3, gradients, basis_out, length)
+    third = pack(third, GRAD_UP)
+    got_third = swap(third, "row", 1)
+
+    far_act, far_basis, third, order = tie((far_act, far_basis, third, order))
+    mine_3, other_3, mine_2, other_2, mine_1, other_1, mine_0, other_0 = rotate_act(
+        where, activations, basis_in, far_act, far_basis, length
+    )
+    other_a = pack(jnp.stack([other_3, other_2]), ACT_UP)
+    other_b = pack(jnp.stack([other_1, other_0]), ACT_UP)
+    got_a, got_b = swap(other_a, "col", 2), swap(other_b, "col", 2)
+
+    block, other_a, other_b = tie((z ^ 2, other_a, other_b))
+    second = rotate_first(block, gradients, basis_out, length)
+    got_third, second = tie((got_third, second))
+    second = second + unpack(got_third, GRAD_UP)
+    upper_2, lower_2 = pack(second[:middle], GRAD_UP), pack(second[middle:], GRAD_UP)
+    got_upper_2 = swap(upper_2, "row", 2)
+    got_a, upper_2 = tie((got_a, upper_2))
+    got_a = unpack(got_a, ACT_UP)
+    act_3 = pack(mine_3 + got_a[0], ACT_UP)
+    over_3 = swap(act_3, "row", 1)
+
+    block, act_3, upper_2 = tie((z ^ 1, act_3, upper_2))
+    first = rotate_grad(block, gradients, basis_out, length)
+    first_out = pack(first, GRAD_UP)
+    got_b, over_3, first_out = tie((got_b, over_3, first_out))
+    got_b = unpack(got_b, ACT_UP)
+    act_2 = mine_2 + got_a[1] + unpack(over_3, ACT_UP)
+    act_2 = pack(act_2, ACT_UP)
+    over_2 = swap(act_2, "row", 2)
+    act_1 = pack(mine_1 + got_b[0], ACT_UP)
+    over_1 = swap(act_1, "row", 1)
+    act_0 = mine_0 + got_b[1]
+    lower_2, act_2, act_0 = tie((lower_2, act_2, act_0))
+    got_lower_2 = swap(lower_2, "row", 2)
+    got_first = swap(first_out, "row", 1)
+
+    block, act_2, act_1, lower_2, first_out = tie((z, act_2, act_1, lower_2, first_out))
+    own = rotate_grad(block, gradients, basis_out, length)
+    over_1, over_2, got_upper_2, own = tie((over_1, over_2, got_upper_2, own))
+    act = act_0 + unpack(over_1, ACT_UP) + unpack(over_2, ACT_UP)
+    act = act.astype(jnp.bfloat16)
+    across = swap(act, "col", 2)
+    pair = jnp.where(x == 0, jnp.stack([act, across]), jnp.stack([across, act]))
+    pair = pair.reshape(2 * quarter, length)
+    other = swap(pair, "col", 1)
+    whole = jnp.where(core == 0, jnp.stack([pair, other]), jnp.stack([other, pair]))
+    whole = whole.reshape(4 * quarter, length)
+
+    got_second = jnp.concatenate([got_upper_2, got_lower_2])
+    grad = own + unpack(got_first, GRAD_UP) + unpack(got_second, GRAD_UP)
+    tile, to_3, to_2, to_1 = make_tile(order, token_ids, whole, grad.astype(jnp.bfloat16))
+    from_3, from_2, from_1 = swap(to_3, "row", 3), swap(to_2, "row", 2), swap(to_1, "row", 1)
+    return (
+        tile
+        + from_3.astype(jnp.float32)
+        + from_2.astype(jnp.float32)
+        + from_1.astype(jnp.float32)
+    )
+
+
 def solution(mesh):
     in_specs = (
         P("groups", ("row", "col")),
@@ -41,4 +296,10 @@
         P(),
     )
     out_specs = P(("groups", "row"), "col")
+    rows, columns = mesh.shape["row"], mesh.shape["col"]
+
+    def shards(*arrays):
+        fits = rows == 4 and columns == 4 and arrays[4].shape[0] == rows
+        return (line_shards if fits else plain_shards)(*arrays)
+
     return jax.shard_map(shards, mesh=mesh, in_specs=in_specs, out_specs=out_specs, check_vma=False)

time: 194 us -> 64.8 us (0.33)
  blocking collectives: 147 us -> 0 us
  matrix products: 28.5 us -> 0 us
  Pallas kernels: 0 us -> 25.3 us
  starting transfers between devices: 0.01 us -> 20.8 us
  waiting for transfers between devices: 0.02 us -> 15.2 us
  between operations: 13.4 us -> 0.22 us
  local copies, waits for them, and re-layouts: 3.08 us -> 0.02 us
  other arithmetic: 1.14 us -> 3.1 us
    psum x1 -> x0, blocking collectives: 140 us -> none  [shards(): rot_grad = lax.psum(partial_value, 'row').astype(jnp.bfloat16)]
    dot_general x3 -> x0, matrix products: 28.5 us -> none  [the longest x1 22.1 us: shards(): jnp.dot(gradients, basis_out, preferred_element_type=jnp.float32)]
    pallas_call x0 -> x6, Pallas kernels: none -> 25.3 us  [the longest x2 11.1 us: rotate_first(): pl.pallas_call(first_kernel, in_specs=[SMEM, HBM, HBM], out_specs=VMEM, o...]
    ppermute x0 -> x16, starting transfers between devices: none -> 20.8 us  [swap(): return lax.ppermute(value, axis, [(i, i ^ step) for i in range(size)])]
    ppermute x0 -> x16, waiting for transfers between devices: none -> 15.2 us  [swap(): return lax.ppermute(value, axis, [(i, i ^ step) for i in range(size)])]
    all_gather x1 -> x0, blocking collectives: 7.15 us -> none  [shards(): act_local = lax.all_gather(act_share, 'col', axis=0, tiled=True) * flat_keep]
    unnamed x5 -> x10, local copies, waits for them, and re-layouts: 2.27 us -> 0.02 us
    add x0 -> x3, other arithmetic: none -> 1.95 us  [the longest x1 1.13 us: line_shards(): second = second + unpack(got_third, GRAD_UP)]
  transfers between devices with their start and end apart: 1 -> 16, of which waited for: 0 -> 7; matrix products, arithmetic and copies ran while one was open for 12% -> 4% of each run, Pallas kernels for 0% -> 37%
where the time goes in v2:
time: 64.8 us; the launch traced here: 64.6 us
  Pallas kernels  25.3 us (39%)
  starting transfers between devices  20.8 us (32%)
  waiting for transfers between devices  15.2 us (23%)
  other arithmetic  3.1 us (5%)
    ppermute x16, starting transfers between devices, swap(): return lax.ppermute(value, axis, [(i, i ^ step) for i in range(size)])  20.8 us
    ppermute x16, waiting for transfers between devices, swap(): return lax.ppermute(value, axis, [(i, i ^ step) for i in range(size)])  15.2 us
    pallas_call x2, Pallas kernels, rotate_first(): pl.pallas_call(first_kernel, in_specs=[SMEM, HBM, HBM], out_specs=VMEM, o...  11.1 us
    pallas_call x2, Pallas kernels, rotate_grad(): pl.pallas_call(grad_kernel, in_specs=[SMEM, HBM, VMEM], out_specs=VMEM, o...  10.1 us
    pallas_call x1, Pallas kernels, rotate_act(): pl.pallas_call(act_kernel, in_specs=[SMEM, VMEM, VMEM, VMEM, VMEM], out_s...  2.9 us
  transfers between devices with their start and end apart: 16, of which 7 were waited for; matrix products, arithmetic and copies ran while one was open for 4% of the time, Pallas kernels for 37%

profile of v2, /device:TPU:0, one launch (start us, length us, event | category | flops | bytes accessed | tf_op | source)
XLA Modules:
  0.0 64.6 jit_solution(10903270977597124107)
XLA Ops:
  0.0 0.5 collective-permute-start
  0.5 5.6 %shard_map.55 = f32[384,512]{1,0:T(8,128)S(1)} custom-call(s32[1]{0:T(128)} %bitcast.block, bf16[2048,7168]{1,0:T(8,128)(2,1)} %gradients.7, bf16[7168,384]{1,0:T(8,128)(2,1)} %basis.9), custom_call_target="tpu_custom_call" | custom-call | flops 2818572288 | bytes 12845056 | tf_op jit(solution)/shard_map/pallas_call | solution.py:102
  6.2 3.1 %collective-permute-start.2 = (f16[384,512]{1,0:T(8,128)(2,1)S(1)}, f16[384,512]{1,0:T(8,128)(2,1)}, u32[]{:S(2)}, u32[]{:S(2)}) collective-permute-start(f16[384,512]{1,0:T(8,128)(2,1)S(1)} %multiply_convert_fusion.1), channel_id=1, source_target_pairs={{0,4},{4,0},{8,12},{12,8},{1,5},{5,1},{9,13},{13,9},{2,6},{6,2},{1... | collective-permute-start | bytes 1179656 | tf_op jit(solution)/shard_map/ppermute | solution.py:205
  9.4 2.9 %shard_map.56 = (f32[128,512]{1,0:T(8,128)S(1)}, f32[128,512]{1,0:T(8,128)S(1)}, f32[128,512]{1,0:T(8,128)S(1)}, f32[128,512]{1,0:T(8,128)S(1)}, f32[128,512]{1,...) custom-call(s32[3]{0:T(128)S(1)} %pad_add_fusion.1.where, ...), custom_call_target="tpu_custom_call" | custom-call | flops 1073741824 | bytes 4194304 | tf_op jit(solution)/shard_map/pallas_call | solution.py:163
  12.3 0.1 fusion.1
  12.5 1.6 %collective-permute-start.3 = (f16[2,128,512]{2,1,0:T(8,128)(2,1)S(1)}, f16[2,128,512]{2,1,0:T(8,128)(2,1)S(1)}, u32[]{:S(2)}, u32[]{:S(2)}) collective-permute-start(f16[2,128,512]{2,1,0:T(8,128)(2,1)S(1)} %get-tuple-element.67), channel_id=1, source_target_pairs={{0,2},{1,3},{2,0},{3,1},{4,6},{5,7},{6,4},{7,5},{8,10},{9,11},{10,... | collective-permute-start | bytes 786440 | tf_op jit(solution)/shard_map/ppermute | solution.py:205
  14.0 0.5 collective-permute-start.4
  14.6 5.6 %shard_map.57 = f32[384,512]{1,0:T(8,128)S(1)} custom-call(s32[1]{0:T(128)} %bitcast.10.block, bf16[2048,7168]{1,0:T(8,128)(2,1)} %gradients.7, bf16[7168,384]{1,0:T(8,128)(2,1)} %basis.9), custom_call_target="tpu_custom_call" | custom-call | flops 2818572288 | bytes 12845056 | tf_op jit(solution)/shard_map/pallas_call | solution.py:102
  20.2 1.1 %multiply_add_fusion = f32[384,512]{1,0:T(8,128)S(1)} fusion(f32[384,512]{1,0:T(8,128)S(1)} %shard_map.57, f16[384,512]{1,0:T(8,128)(2,1)} %collective-permute-done.2), kind=kLoop, calls=%fused_computation.2 | loop fusion | flops 589824 | bytes 1966080 | tf_op jit(solution)/shard_map/add | solution.py:243
  21.4 2.7 %collective-permute-start.8 = (f16[256,512]{1,0:T(8,128)(2,1)S(1)}, f16[256,512]{1,0:T(8,128)(2,1)S(1)}, u32[]{:S(2)}, u32[]{:S(2)}) collective-permute-start(f16[256,512]{1,0:T(8,128)(2,1)S(1)} %fusion), channel_id=1, source_target_pairs={{0,8},{4,12},{8,0},{12,4},{1,9},{5,13},{9,1},{13,5},{2,10},{6,14},... | collective-permute-start | bytes 786440 | tf_op jit(solution)/shard_map/ppermute | solution.py:205
  24.1 0.5 collective-permute-start.5
  24.7 5.0 %shard_map.58 = f32[384,512]{1,0:T(8,128)S(1)} custom-call(s32[1]{0:T(128)} %bitcast.13.block, bf16[2048,7168]{1,0:T(8,128)(2,1)} %gradients.7, bf16[7168,384]{1,0:T(8,128)(2,1)S(1)} %bitcast.50), custom_call_target="tpu_custom_call" | custom-call | flops 1 | bytes 1 | tf_op jit(solution)/shard_map/pallas_call | solution.py:132
  29.7 2.0 %collective-permute-done.5 = f16[128,512]{1,0:T(8,128)(2,1)S(1)} collective-permute-done((f16[128,512]{1,0:T(8,128)(2,1)S(1)}, f16[128,512]{1,0:T(8,128)(2,1)S(1)}, u32[]{:S(2)}, u32[]{:S(2)}) %collective-permute-start.5) | collective-permute-done | bytes 131104 | tf_op jit(solution)/shard_map/ppermute | solution.py:205
  31.8 1.3 %collective-permute-start.7 = (f16[128,512]{1,0:T(8,128)(2,1)S(1)}, f16[128,512]{1,0:T(8,128)(2,1)S(1)}, u32[]{:S(2)}, u32[]{:S(2)}) collective-permute-start(f16[128,512]{1,0:T(8,128)(2,1)S(1)} %fusion.13), channel_id=1, source_target_pairs={{0,8},{4,12},{8,0},{12,4},{1,9},{5,13},{9,1},{13,5},{2,10},{6,14},... | collective-permute-start | bytes 393224 | tf_op jit(solution)/shard_map/ppermute | solution.py:205
  33.2 0.1 fusion.6
  33.3 1.4 %collective-permute-start.6 = (f16[128,512]{1,0:T(8,128)(2,1)S(1)}, f16[128,512]{1,0:T(8,128)(2,1)S(1)}, u32[]{:S(2)}, u32[]{:S(2)}) collective-permute-start(f16[128,512]{1,0:T(8,128)(2,1)S(1)} %get-tuple-element.66), channel_id=1, source_target_pairs={{0,4},{4,0},{8,12},{12,8},{1,5},{5,1},{9,13},{13,9},{2,6},{6,2},{1... | collective-permute-start | bytes 393224 | tf_op jit(solution)/shard_map/ppermute | solution.py:205
  34.7 0.7 %collective-permute-start.11 = (f16[384,512]{1,0:T(8,128)(2,1)S(1)}, f16[384,512]{1,0:T(8,128)(2,1)S(1)}, u32[]{:S(2)}, u32[]{:S(2)}) collective-permute-start(f16[384,512]{1,0:T(8,128)(2,1)S(1)} %multiply_convert_fusion), channel_id=1, source_target_pairs={{0,4},{4,0},{8,12},{12,8},{1,5},{5,1},{9,13},{13,9},{2,6},{6,2},{1... | collective-permute-start | bytes 1179656 | tf_op jit(solution)/shard_map/ppermute | solution.py:205
  35.4 5.2 %shard_map.59 = f32[384,512]{1,0:T(8,128)S(1)} custom-call(s32[1]{0:T(128)} %bitcast.16.block, bf16[2048,7168]{1,0:T(8,128)(2,1)} %gradients.7, bf16[7168,384]{1,0:T(8,128)(2,1)S(1)} %bitcast.50), custom_call_target="tpu_custom_call" | custom-call | flops 1 | bytes 1 | tf_op jit(solution)/shard_map/pallas_call | solution.py:132
  40.6 1.7 %collective-permute-done.6 = f16[128,512]{1,0:T(8,128)(2,1)S(1)} collective-permute-done((f16[128,512]{1,0:T(8,128)(2,1)S(1)}, f16[128,512]{1,0:T(8,128)(2,1)S(1)}, u32[]{:S(2)}, u32[]{:S(2)}) %collective-permute-start.6) | collective-permute-done | bytes 131104 | tf_op jit(solution)/shard_map/ppermute | solution.py:205
  42.4 1.6 %collective-permute-start.9 = (bf16[128,512]{1,0:T(8,128)(2,1)S(1)}, bf16[128,512]{1,0:T(8,128)(2,1)S(1)}, u32[]{:S(2)}, u32[]{:S(2)}) collective-permute-start(bf16[128,512]{1,0:T(8,128)(2,1)S(1)} %add_convert_fusion.1), channel_id=1, source_target_pairs={{0,2},{1,3},{2,0},{3,1},{4,6},{5,7},{6,4},{7,5},{8,10},{9,11},{10,... | collective-permute-start | bytes 393224 | tf_op jit(solution)/shard_map/ppermute | solution.py:205
  44.0 2.3 %collective-permute-start.12 = (f16[128,512]{1,0:T(8,128)(2,1)S(1)}, f16[128,512]{1,0:T(8,128)(2,1)S(1)}, u32[]{:S(2)}, u32[]{:S(2)}) collective-permute-start(f16[128,512]{1,0:T(8,128)(2,1)S(1)} %fusion.14), channel_id=1, source_target_pairs={{0,8},{4,12},{8,0},{12,4},{1,9},{5,13},{9,1},{13,5},{2,10},{6,14},... | collective-permute-start | bytes 393224 | tf_op jit(solution)/shard_map/ppermute | solution.py:205
  46.3 1.1 %collective-permute-done.9 = bf16[128,512]{1,0:T(8,128)(2,1)S(1)} collective-permute-done((bf16[128,512]{1,0:T(8,128)(2,1)S(1)}, bf16[128,512]{1,0:T(8,128)(2,1)S(1)}, u32[]{:S(2)}, u32[]{:S(2)}) %collective-permute-start.9) | collective-permute-done | bytes 131104 | tf_op jit(solution)/shard_map/ppermute | solution.py:205
  47.5 2.8 %collective-permute-done.12 = f16[128,512]{1,0:T(8,128)(2,1)S(1)} collective-permute-done((f16[128,512]{1,0:T(8,128)(2,1)S(1)}, f16[128,512]{1,0:T(8,128)(2,1)S(1)}, u32[]{:S(2)}, u32[]{:S(2)}) %collective-permute-start.12) | collective-permute-done | bytes 131104 | tf_op jit(solution)/shard_map/ppermute | solution.py:205
  50.3 1.7 %collective-permute-done.11 = f16[384,512]{1,0:T(8,128)(2,1)S(1)} collective-permute-done((f16[384,512]{1,0:T(8,128)(2,1)S(1)}, f16[384,512]{1,0:T(8,128)(2,1)S(1)}, u32[]{:S(2)}, u32[]{:S(2)}) %collective-permute-start.11) | collective-permute-done | bytes 393248 | tf_op jit(solution)/shard_map/ppermute | solution.py:205
  52.0 0.2 add_convert_fusion.grad
  52.2 0.1 maximum_select_fusion
  52.3 1.1 %shard_map.60 = (f32[128,384]{1,0:T(8,128)S(1)}, bf16[128,384]{1,0:T(8,128)(2,1)S(1)}, bf16[128,384]{1,0:T(8,128)(2,1)S(1)}, bf16[128,384]{1,0:T(8,128)(2,1)S(1)}) custom-call(s32[4]{0:T(128)S(1)} %pad_add_fusion.order, s32[4,512]{1,0:T(4,128)S(1)} %copy-done.2, bf16[512,512]{1,0:T(8,128)(2,1)S(1)} %bitcast.51, bf16[384,512]{1,0:T(8,128)(2,1)S(1)} %add_convert_fusion.grad), custom_call_target="tpu_custom_call" | custom-call | tf_op jit(solution)/shard_map/pallas_call | solution.py:194
  53.5 3.9 %collective-permute-start.13 = (bf16[128,384]{1,0:T(8,128)(2,1)S(1)}, bf16[128,384]{1,0:T(8,128)(2,1)S(1)}, u32[]{:S(2)}, u32[]{:S(2)}) collective-permute-start(bf16[128,384]{1,0:T(8,128)(2,1)S(1)} %get-tuple-element.62), channel_id=1, source_target_pairs={{0,12},{4,8},{8,4},{12,0},{1,13},{5,9},{9,5},{13,1},{2,14},{6,10},... | collective-permute-start | bytes 294920 | tf_op jit(solution)/shard_map/ppermute | solution.py:205
  57.4 0.6 collective-permute-start.15
  58.0 2.8 %collective-permute-done.13 = bf16[128,384]{1,0:T(8,128)(2,1)S(1)} collective-permute-done((bf16[128,384]{1,0:T(8,128)(2,1)S(1)}, bf16[128,384]{1,0:T(8,128)(2,1)S(1)}, u32[]{:S(2)}, u32[]{:S(2)}) %collective-permute-start.13) | collective-permute-done | bytes 98336 | tf_op jit(solution)/shard_map/ppermute | solution.py:205
  60.8 3.1 %collective-permute-done.14 = bf16[128,384]{1,0:T(8,128)(2,1)S(1)} collective-permute-done((bf16[128,384]{1,0:T(8,128)(2,1)S(1)}, bf16[128,384]{1,0:T(8,128)(2,1)S(1)}, u32[]{:S(2)}, u32[]{:S(2)}) %collective-permute-start.14) | collective-permute-done | bytes 98336 | tf_op jit(solution)/shard_map/ppermute | solution.py:205
  63.9 0.7 %convert_add_fusion = f32[128,384]{1,0:T(8,128)} fusion(bf16[128,384]{1,0:T(8,128)(2,1)S(1)} %collective-permute-done.15, bf16[128,384]{1,0:T(8,128)(2,1)S(1)} %collective-permute-done.14, f32[128,384]{1,0:T(8,128)S(1)} %get-tuple-element.61, bf16[128,384]{1,0:T(8,128)(2,1)S(1)} %collective-permute-done.13), kind=kLoop, calls=%fused_computation.32 | loop fusion | flops 294912 | bytes 688128 | tf_op jit(solution)/shard_map/add | solution.py:283
  (35 shorter events, 0.9 us)
Async XLA Ops:
  0.0 9.4 %collective-permute-start = (bf16[2048,512]{1,0:T(8,128)(2,1)}, bf16[2048,512]{1,0:T(8,128)(2,1)}, u32[]{:S(2)}, u32[]{:S(2)}) collective-permute-start(bf16[2048,512]{1,0:T(8,128)(2,1)} %act.1), channel_id=1, source_target_pairs={{0,1},{1,0},{2,3},{3,2},{4,5},{5,4},{6,7},{7,6},{8,9},{9,8},{10,11... | collective-permute-start | bytes 6291464 | tf_op jit(solution)/shard_map/ppermute | solution.py:205
  0.5 9.0 %collective-permute-start.1 = (bf16[512,512]{1,0:T(8,128)(2,1)}, bf16[512,512]{1,0:T(8,128)(2,1)S(1)}, u32[]{:S(2)}, u32[]{:S(2)}) collective-permute-start(bf16[512,512]{1,0:T(8,128)(2,1)} %basis.6), channel_id=1, source_target_pairs={{0,1},{1,0},{2,3},{3,2},{4,5},{5,4},{6,7},{7,6},{8,9},{9,8},{10,11... | collective-permute-start | bytes 1572872 | tf_op jit(solution)/shard_map/ppermute | solution.py:205
  0.5 8.9 %copy-start = (bf16[2048,512]{1,0:T(8,128)(2,1)S(1)}, bf16[2048,512]{1,0:T(8,128)(2,1)}, u32[]{:S(2)}) copy-start(bf16[2048,512]{1,0:T(8,128)(2,1)} %act.1) | copy-start | bytes 6291460
  0.5 8.9 %copy-start.1 = (bf16[512,512]{1,0:T(8,128)(2,1)S(1)}, bf16[512,512]{1,0:T(8,128)(2,1)}, u32[]{:S(2)}) copy-start(bf16[512,512]{1,0:T(8,128)(2,1)} %basis.6) | copy-start | bytes 1572868
  6.2 14.0 %collective-permute-start.2 = (f16[384,512]{1,0:T(8,128)(2,1)S(1)}, f16[384,512]{1,0:T(8,128)(2,1)}, u32[]{:S(2)}, u32[]{:S(2)}) collective-permute-start(f16[384,512]{1,0:T(8,128)(2,1)S(1)} %multiply_convert_fusion.1), channel_id=1, source_target_pairs={{0,4},{4,0},{8,12},{12,8},{1,5},{5,1},{9,13},{13,9},{2,6},{6,2},{1... | collective-permute-start | bytes 1179656 | tf_op jit(solution)/shard_map/ppermute | solution.py:205
  12.5 11.5 %collective-permute-start.3 = (f16[2,128,512]{2,1,0:T(8,128)(2,1)S(1)}, f16[2,128,512]{2,1,0:T(8,128)(2,1)S(1)}, u32[]{:S(2)}, u32[]{:S(2)}) collective-permute-start(f16[2,128,512]{2,1,0:T(8,128)(2,1)S(1)} %get-tuple-element.67), channel_id=1, source_target_pairs={{0,2},{1,3},{2,0},{3,1},{4,6},{5,7},{6,4},{7,5},{8,10},{9,11},{10,... | collective-permute-start | bytes 786440 | tf_op jit(solution)/shard_map/ppermute | solution.py:205
  14.0 15.7 %collective-permute-start.4 = (f16[2,128,512]{2,1,0:T(8,128)(2,1)S(1)}, f16[2,128,512]{2,1,0:T(8,128)(2,1)S(1)}, u32[]{:S(2)}, u32[]{:S(2)}) collective-permute-start(f16[2,128,512]{2,1,0:T(8,128)(2,1)S(1)} %get-tuple-element.68), channel_id=1, source_target_pairs={{0,2},{1,3},{2,0},{3,1},{4,6},{5,7},{6,4},{7,5},{8,10},{9,11},{10,... | collective-permute-start | bytes 786440 | tf_op jit(solution)/shard_map/ppermute | solution.py:205
  14.6 10.1 %slice-start = ((s8[5505024]{0:T(1024)(128)(4,1)}), s8[4194304]{0:T(1024)(128)(4,1)S(1)}, s32[]{:S(2)}) async-start(s8[5505024]{0:T(1024)(128)(4,1)} %bitcast.49), calls=%async_computation | async-start | bytes 8388608
  14.6 10.1 %slice-start.1 = ((s8[5505024]{0:T(1024)(128)(4,1)}), s8[1310720]{0:T(1024)(128)(4,1)S(1)}, s32[]{:S(2)}) async-start(s8[5505024]{0:T(1024)(128)(4,1)} %bitcast.49), calls=%async_computation.1 | async-start | bytes 2621440
  21.4 19.3 %collective-permute-start.8 = (f16[256,512]{1,0:T(8,128)(2,1)S(1)}, f16[256,512]{1,0:T(8,128)(2,1)S(1)}, u32[]{:S(2)}, u32[]{:S(2)}) collective-permute-start(f16[256,512]{1,0:T(8,128)(2,1)S(1)} %fusion), channel_id=1, source_target_pairs={{0,8},{4,12},{8,0},{12,4},{1,9},{5,13},{9,1},{13,5},{2,10},{6,14},... | collective-permute-start | bytes 786440 | tf_op jit(solution)/shard_map/ppermute | solution.py:205
  24.1 7.6 %collective-permute-start.5 = (f16[128,512]{1,0:T(8,128)(2,1)S(1)}, f16[128,512]{1,0:T(8,128)(2,1)S(1)}, u32[]{:S(2)}, u32[]{:S(2)}) collective-permute-start(f16[128,512]{1,0:T(8,128)(2,1)S(1)} %fusion.9), channel_id=1, source_target_pairs={{0,4},{4,0},{8,12},{12,8},{1,5},{5,1},{9,13},{13,9},{2,6},{6,2},{1... | collective-permute-start | bytes 393224 | tf_op jit(solution)/shard_map/ppermute | solution.py:205
  31.8 8.8 %collective-permute-start.7 = (f16[128,512]{1,0:T(8,128)(2,1)S(1)}, f16[128,512]{1,0:T(8,128)(2,1)S(1)}, u32[]{:S(2)}, u32[]{:S(2)}) collective-permute-start(f16[128,512]{1,0:T(8,128)(2,1)S(1)} %fusion.13), channel_id=1, source_target_pairs={{0,8},{4,12},{8,0},{12,4},{1,9},{5,13},{9,1},{13,5},{2,10},{6,14},... | collective-permute-start | bytes 393224 | tf_op jit(solution)/shard_map/ppermute | solution.py:205
  33.3 9.1 %collective-permute-start.6 = (f16[128,512]{1,0:T(8,128)(2,1)S(1)}, f16[128,512]{1,0:T(8,128)(2,1)S(1)}, u32[]{:S(2)}, u32[]{:S(2)}) collective-permute-start(f16[128,512]{1,0:T(8,128)(2,1)S(1)} %get-tuple-element.66), channel_id=1, source_target_pairs={{0,4},{4,0},{8,12},{12,8},{1,5},{5,1},{9,13},{13,9},{2,6},{6,2},{1... | collective-permute-start | bytes 393224 | tf_op jit(solution)/shard_map/ppermute | solution.py:205
  34.7 17.3 %collective-permute-start.11 = (f16[384,512]{1,0:T(8,128)(2,1)S(1)}, f16[384,512]{1,0:T(8,128)(2,1)S(1)}, u32[]{:S(2)}, u32[]{:S(2)}) collective-permute-start(f16[384,512]{1,0:T(8,128)(2,1)S(1)} %multiply_convert_fusion), channel_id=1, source_target_pairs={{0,4},{4,0},{8,12},{12,8},{1,5},{5,1},{9,13},{13,9},{2,6},{6,2},{1... | collective-permute-start | bytes 1179656 | tf_op jit(solution)/shard_map/ppermute | solution.py:205
  35.4 16.9 %copy-start.2 = (s32[4,512]{1,0:T(4,128)S(1)}, s32[4,512]{1,0:T(4,128)}, u32[]{:S(2)}) copy-start(s32[4,512]{1,0:T(4,128)} %ids.1) | copy-start | bytes 24580
  42.4 5.0 %collective-permute-start.9 = (bf16[128,512]{1,0:T(8,128)(2,1)S(1)}, bf16[128,512]{1,0:T(8,128)(2,1)S(1)}, u32[]{:S(2)}, u32[]{:S(2)}) collective-permute-start(bf16[128,512]{1,0:T(8,128)(2,1)S(1)} %add_convert_fusion.1), channel_id=1, source_target_pairs={{0,2},{1,3},{2,0},{3,1},{4,6},{5,7},{6,4},{7,5},{8,10},{9,11},{10,... | collective-permute-start | bytes 393224 | tf_op jit(solution)/shard_map/ppermute | solution.py:205
  44.0 6.3 %collective-permute-start.12 = (f16[128,512]{1,0:T(8,128)(2,1)S(1)}, f16[128,512]{1,0:T(8,128)(2,1)S(1)}, u32[]{:S(2)}, u32[]{:S(2)}) collective-permute-start(f16[128,512]{1,0:T(8,128)(2,1)S(1)} %fusion.14), channel_id=1, source_target_pairs={{0,8},{4,12},{8,0},{12,4},{1,9},{5,13},{9,1},{13,5},{2,10},{6,14},... | collective-permute-start | bytes 393224 | tf_op jit(solution)/shard_map/ppermute | solution.py:205
  47.5 4.8 %collective-permute-start.10 = (bf16[256,512]{1,0:T(8,128)(2,1)S(1)}, bf16[256,512]{1,0:T(8,128)(2,1)S(1)}, u32[]{:S(2)}, u32[]{:S(2)}) collective-permute-start(bf16[256,512]{1,0:T(8,128)(2,1)S(1)} %bitcast.56), channel_id=1, source_target_pairs={{0,1},{1,0},{2,3},{3,2},{4,5},{5,4},{6,7},{7,6},{8,9},{9,8},{10,11... | collective-permute-start | bytes 786440 | tf_op jit(solution)/shard_map/ppermute | solution.py:205
  53.5 7.3 %collective-permute-start.13 = (bf16[128,384]{1,0:T(8,128)(2,1)S(1)}, bf16[128,384]{1,0:T(8,128)(2,1)S(1)}, u32[]{:S(2)}, u32[]{:S(2)}) collective-permute-start(bf16[128,384]{1,0:T(8,128)(2,1)S(1)} %get-tuple-element.62), channel_id=1, source_target_pairs={{0,12},{4,8},{8,4},{12,0},{1,13},{5,9},{9,5},{13,1},{2,14},{6,10},... | collective-permute-start | bytes 294920 | tf_op jit(solution)/shard_map/ppermute | solution.py:205
  57.4 6.5 %collective-permute-start.14 = (bf16[128,384]{1,0:T(8,128)(2,1)S(1)}, bf16[128,384]{1,0:T(8,128)(2,1)S(1)}, u32[]{:S(2)}, u32[]{:S(2)}) collective-permute-start(bf16[128,384]{1,0:T(8,128)(2,1)S(1)} %get-tuple-element.63), channel_id=1, source_target_pairs={{0,8},{4,12},{8,0},{12,4},{1,9},{5,13},{9,1},{13,5},{2,10},{6,14},... | collective-permute-start | bytes 294920 | tf_op jit(solution)/shard_map/ppermute | solution.py:205
  57.4 6.5 %collective-permute-start.15 = (bf16[128,384]{1,0:T(8,128)(2,1)S(1)}, bf16[128,384]{1,0:T(8,128)(2,1)S(1)}, u32[]{:S(2)}, u32[]{:S(2)}) collective-permute-start(bf16[128,384]{1,0:T(8,128)(2,1)S(1)} %get-tuple-element.64), channel_id=1, source_target_pairs={{0,4},{4,0},{8,12},{12,8},{1,5},{5,1},{9,13},{13,9},{2,6},{6,2},{1... | collective-permute-start | bytes 294920 | tf_op jit(solution)/shard_map/ppermute | solution.py:205

commit v3 on v2

--- a/solution.py
+++ b/solution.py
@@ -68,21 +68,19 @@
     ]
 
 
-def rotate_block(copies, weights, buffer, total, out):
+def rotate_block(copies, weights, buffer, out):
     edges = pieces(buffer.shape[1])
     for i, (at, size) in enumerate(edges):
         for copy in copies[i]:
             copy.wait()
         part = columns_by_rows(weights[at : at + size, :], buffer[:, at : at + size])
         if i == 0:
-            total[...] = part
-        elif i < len(edges) - 1:
-            total[...] += part
+            out[...] = part
         else:
-            out[...] = total[...] + part
-
-
-def first_kernel(block, gradients, basis, out, weights, buffer, total, grad_sems, basis_sems):
+            out[...] += part
+
+
+def grad_kernel(block, gradients, basis, out, weights, buffer, grad_sems, basis_sems):
     copies = []
     edges = pieces(buffer.shape[1])
     for i, copy in enumerate(fetch_block(block[0], gradients, buffer, grad_sems)):
@@ -93,55 +91,30 @@
         part.start()
         copy.start()
         copies.append((part, copy))
-    rotate_block(copies, weights, buffer, total, out)
-
-
-def rotate_first(block, gradients, basis_out, length):
+    rotate_block(copies, weights, buffer, out)
+
+
+def rotate_grad(block, gradients, basis_out, length):
     depth, width = basis_out.shape
     steps = len(pieces(depth))
     return pl.pallas_call(
-        first_kernel,
+        grad_kernel,
         in_specs=[SMEM, HBM, HBM],
         out_specs=VMEM,
         out_shape=jax.ShapeDtypeStruct((width, length), jnp.float32),
         scratch_shapes=[
             pltpu.VMEM((depth, width), basis_out.dtype),
             pltpu.VMEM((length, depth), jnp.bfloat16),
-            pltpu.VMEM((width, length), jnp.float32),
             pltpu.SemaphoreType.DMA((steps,)),
             pltpu.SemaphoreType.DMA((steps,)),
         ],
-        compiler_params=pltpu.CompilerParams(vmem_limit_bytes=18 * 2**20),
+        compiler_params=pltpu.CompilerParams(vmem_limit_bytes=14 * 2**20),
         cost_estimate=pl.CostEstimate(
             flops=2 * length * depth * width,
             bytes_accessed=2 * depth * (length + width),
             transcendentals=0,
         ),
     )(jnp.reshape(block, (1,)), in_hbm(gradients), in_hbm(basis_out))
-
-
-def grad_kernel(block, gradients, basis, out, buffer, total, sems):
-    copies = fetch_block(block[0], gradients, buffer, sems)
-    for copy in copies:
-        copy.start()
-    rotate_block([(copy,) for copy in copies], basis, buffer, total, out)
-
-
-def rotate_grad(block, gradients, basis, length):
-    depth, width = basis.shape
-    return pl.pallas_call(
-        grad_kernel,
-        in_specs=[SMEM, HBM, VMEM],
-        out_specs=VMEM,
-        out_shape=jax.ShapeDtypeStruct((width, length), jnp.float32),
-        scratch_shapes=[
-            pltpu.VMEM((length, depth), jnp.bfloat16),
-            pltpu.VMEM((width, length), jnp.float32),
-            pltpu.SemaphoreType.DMA((len(pieces(depth)),)),
-        ],
-        compiler_params=pltpu.CompilerParams(vmem_limit_bytes=12 * 2**20),
-        cost_estimate=pl.CostEstimate(flops=1, bytes_accessed=1, transcendentals=0),
-    )(jnp.reshape(block, (1,)), in_hbm(gradients), pltpu.with_memory_space_constraint(basis, pltpu.VMEM))
 
 
 def act_kernel(where, act, basis, far_act, far_basis, *outs):
@@ -165,7 +138,7 @@
         in_specs=[SMEM, VMEM, VMEM, VMEM, VMEM],
         out_specs=[VMEM] * 8,
         out_shape=[shape] * 8,
-        compiler_params=pltpu.CompilerParams(vmem_limit_bytes=12 * 2**20),
+        compiler_params=pltpu.CompilerParams(vmem_limit_bytes=6 * 2**20),
         cost_estimate=pl.CostEstimate(
             flops=2 * activations.size * basis_in.shape[1],
             bytes_accessed=4 * activations.size,
@@ -198,6 +171,7 @@
         out_shape=[jax.ShapeDtypeStruct((rows, width), jnp.float32)]
         + [jax.ShapeDtypeStruct((rows, width), jnp.bfloat16)] * (sequences - 1),
         compiler_params=pltpu.CompilerParams(vmem_limit_bytes=16 * 2**20),
+        cost_estimate=pl.CostEstimate(flops=1, bytes_accessed=1, transcendentals=0),
     )(order, token_ids, act, grad)
 
 
@@ -219,13 +193,13 @@
     place = lax.axis_index("col").astype(jnp.int32)
     core, x = place & 1, place >> 1
     quarter = basis_in.shape[1] // 4
-    middle = basis_out.shape[1] // 3 * 2
+    middle = basis_out.shape[1] // 2
     tie = lax.optimization_barrier
     order = jnp.stack([z, z ^ 3, z ^ 2, z ^ 1])
     where = jnp.stack([z, core, x])
 
     far_act, far_basis = swap(activations, "col", 1), swap(basis_in, "col", 1)
-    third = rotate_first(z ^ 3, gradients, basis_out, length)
+    third = rotate_grad(z ^ 3, gradients, basis_out, length)
     third = pack(third, GRAD_UP)
     got_third = swap(third, "row", 1)
 
@@ -233,48 +207,44 @@
     mine_3, other_3, mine_2, other_2, mine_1, other_1, mine_0, other_0 = rotate_act(
         where, activations, basis_in, far_act, far_basis, length
     )
-    other_a = pack(jnp.stack([other_3, other_2]), ACT_UP)
-    other_b = pack(jnp.stack([other_1, other_0]), ACT_UP)
-    got_a, got_b = swap(other_a, "col", 2), swap(other_b, "col", 2)
-
-    block, other_a, other_b = tie((z ^ 2, other_a, other_b))
-    second = rotate_first(block, gradients, basis_out, length)
+    out_3 = pack(other_3, ACT_UP)
+    out_210 = pack(jnp.stack([other_2, other_1, other_0]), ACT_UP)
+    got_3 = swap(out_3, "col", 2)
+    got_210 = swap(out_210, "col", 2)
+
+    block, out_3, out_210 = tie((z ^ 2, out_3, out_210))
+    second = rotate_grad(block, gradients, basis_out, length)
     got_third, second = tie((got_third, second))
     second = second + unpack(got_third, GRAD_UP)
     upper_2, lower_2 = pack(second[:middle], GRAD_UP), pack(second[middle:], GRAD_UP)
     got_upper_2 = swap(upper_2, "row", 2)
-    got_a, upper_2 = tie((got_a, upper_2))
-    got_a = unpack(got_a, ACT_UP)
-    act_3 = pack(mine_3 + got_a[0], ACT_UP)
+    got_3, upper_2 = tie((got_3, upper_2))
+    act_3 = pack(mine_3 + unpack(got_3, ACT_UP), ACT_UP)
     over_3 = swap(act_3, "row", 1)
 
     block, act_3, upper_2 = tie((z ^ 1, act_3, upper_2))
     first = rotate_grad(block, gradients, basis_out, length)
+    got_210, over_3, first = tie((got_210, over_3, first))
+    act_2 = pack(mine_2 + unpack(got_210[0], ACT_UP) + unpack(over_3, ACT_UP), ACT_UP)
+    over_2 = swap(act_2, "row", 2)
+    act_1 = pack(mine_1 + unpack(got_210[1], ACT_UP), ACT_UP)
+    act_0 = mine_0 + unpack(got_210[2], ACT_UP)
+    over_1 = swap(act_1, "row", 1)
+    first, act_2, act_1, act_0 = tie((first, act_2, act_1, act_0))
     first_out = pack(first, GRAD_UP)
-    got_b, over_3, first_out = tie((got_b, over_3, first_out))
-    got_b = unpack(got_b, ACT_UP)
-    act_2 = mine_2 + got_a[1] + unpack(over_3, ACT_UP)
-    act_2 = pack(act_2, ACT_UP)
-    over_2 = swap(act_2, "row", 2)
-    act_1 = pack(mine_1 + got_b[0], ACT_UP)
-    over_1 = swap(act_1, "row", 1)
-    act_0 = mine_0 + got_b[1]
-    lower_2, act_2, act_0 = tie((lower_2, act_2, act_0))
-    got_lower_2 = swap(lower_2, "row", 2)
     got_first = swap(first_out, "row", 1)
-
-    block, act_2, act_1, lower_2, first_out = tie((z, act_2, act_1, lower_2, first_out))
+    block, first_out = tie((z, first_out))
     own = rotate_grad(block, gradients, basis_out, length)
     over_1, over_2, got_upper_2, own = tie((over_1, over_2, got_upper_2, own))
     act = act_0 + unpack(over_1, ACT_UP) + unpack(over_2, ACT_UP)
     act = act.astype(jnp.bfloat16)
+    got_lower_2 = swap(lower_2, "row", 2)
     across = swap(act, "col", 2)
     pair = jnp.where(x == 0, jnp.stack([act, across]), jnp.stack([across, act]))
     pair = pair.reshape(2 * quarter, length)
     other = swap(pair, "col", 1)
     whole = jnp.where(core == 0, jnp.stack([pair, other]), jnp.stack([other, pair]))
     whole = whole.reshape(4 * quarter, length)
-
     got_second = jnp.concatenate([got_upper_2, got_lower_2])
     grad = own + unpack(got_first, GRAD_UP) + unpack(got_second, GRAD_UP)
     tile, to_3, to_2, to_1 = make_tile(order, token_ids, whole, grad.astype(jnp.bfloat16))

time: 64.8 us -> 62.9 us (0.971)
  starting transfers between devices: 20.8 us -> 19.4 us
  waiting for transfers between devices: 15.2 us -> 14.2 us
  Pallas kernels: 25.3 us -> 26 us
    ppermute x16, starting transfers between devices: 20.8 us -> 19.4 us  [swap(): return lax.ppermute(value, axis, [(i, i ^ step) for i in range(size)])]
    ppermute x16, waiting for transfers between devices: 15.2 us -> 14.2 us  [swap(): return lax.ppermute(value, axis, [(i, i ^ step) for i in range(size)])]
  transfers between devices with their start and end apart: 16 -> 16, of which waited for: 7 -> 6; matrix products, arithmetic and copies ran while one was open for 4% -> 3% of each run, Pallas kernels for 37% -> 40%
where the time goes in v3:
time: 62.9 us; the launch traced here: 62.8 us
  Pallas kernels  26 us (41%)
  starting transfers between devices  19.4 us (31%)
  waiting for transfers between devices  14.2 us (23%)
  other arithmetic  2.95 us (5%)
    pallas_call x4, Pallas kernels, rotate_grad(): pl.pallas_call(grad_kernel, in_specs=[SMEM, HBM, HBM], out_specs=VMEM, ou...  21.9 us
    ppermute x16, starting transfers between devices, swap(): return lax.ppermute(value, axis, [(i, i ^ step) for i in range(size)])  19.4 us
    ppermute x16, waiting for transfers between devices, swap(): return lax.ppermute(value, axis, [(i, i ^ step) for i in range(size)])  14.2 us
    pallas_call x1, Pallas kernels, rotate_act(): pl.pallas_call(act_kernel, in_specs=[SMEM, VMEM, VMEM, VMEM, VMEM], out_s...  2.9 us
  transfers between devices with their start and end apart: 16, of which 6 were waited for; matrix products, arithmetic and copies ran while one was open for 3% of the time, Pallas kernels for 40%

profile of v3, /device:TPU:0, one launch (start us, length us, event | category | flops | bytes accessed | tf_op | source)
XLA Modules:
  0.0 62.8 jit_solution(9021092089773002180)
XLA Ops:
  0.0 0.5 collective-permute-start
  0.5 5.6 %shard_map.55 = f32[384,512]{1,0:T(8,128)S(1)} custom-call(s32[1]{0:T(128)} %bitcast.block, bf16[2048,7168]{1,0:T(8,128)(2,1)} %gradients.7, bf16[7168,384]{1,0:T(8,128)(2,1)} %basis.9), custom_call_target="tpu_custom_call" | custom-call | flops 2818572288 | bytes 12845056 | tf_op jit(solution)/shard_map/pallas_call | solution.py:100
  6.2 3.1 %collective-permute-start.4 = (f16[384,512]{1,0:T(8,128)(2,1)S(1)}, f16[384,512]{1,0:T(8,128)(2,1)}, u32[]{:S(2)}, u32[]{:S(2)}) collective-permute-start(f16[384,512]{1,0:T(8,128)(2,1)S(1)} %multiply_convert_fusion.1), channel_id=1, source_target_pairs={{0,4},{4,0},{8,12},{12,8},{1,5},{5,1},{9,13},{13,9},{2,6},{6,2},{1... | collective-permute-start | bytes 1179656 | tf_op jit(solution)/shard_map/ppermute | solution.py:179
  9.3 0.1 pad_add_fusion.1.where
  9.3 0.1 pad_add_fusion.order
  9.4 2.9 %shard_map.56 = (f32[128,512]{1,0:T(8,128)S(1)}, f32[128,512]{1,0:T(8,128)S(1)}, f32[128,512]{1,0:T(8,128)S(1)}, f32[128,512]{1,0:T(8,128)S(1)}, f32[128,512]{1,...) custom-call(s32[3]{0:T(128)S(1)} %pad_add_fusion.1.where, ...), custom_call_target="tpu_custom_call" | custom-call | flops 1073741824 | bytes 4194304 | tf_op jit(solution)/shard_map/pallas_call | solution.py:136
  12.4 1.6 %collective-permute-start.3 = (f16[128,512]{1,0:T(8,128)(2,1)S(1)}, f16[128,512]{1,0:T(8,128)(2,1)S(1)}, u32[]{:S(2)}, u32[]{:S(2)}) collective-permute-start(f16[128,512]{1,0:T(8,128)(2,1)S(1)} %multiply_convert_fusion.3), channel_id=1, source_target_pairs={{0,2},{1,3},{2,0},{3,1},{4,6},{5,7},{6,4},{7,5},{8,10},{9,11},{10,... | collective-permute-start | bytes 393224 | tf_op jit(solution)/shard_map/ppermute | solution.py:179
  14.0 0.6 collective-permute-start.2
  14.6 5.4 %shard_map.57 = f32[384,512]{1,0:T(8,128)S(1)} custom-call(s32[1]{0:T(128)} %bitcast.9.block, bf16[2048,7168]{1,0:T(8,128)(2,1)} %gradients.7, bf16[7168,384]{1,0:T(8,128)(2,1)} %basis.9), custom_call_target="tpu_custom_call" | custom-call | flops 2818572288 | bytes 12845056 | tf_op jit(solution)/shard_map/pallas_call | solution.py:100
  20.0 1.1 %multiply_add_fusion = f32[384,512]{1,0:T(8,128)S(1)} fusion(f32[384,512]{1,0:T(8,128)S(1)} %shard_map.57, f16[384,512]{1,0:T(8,128)(2,1)} %collective-permute-done.4), kind=kLoop, calls=%fused_computation.4 | loop fusion | flops 589824 | bytes 1966080 | tf_op jit(solution)/shard_map/add | solution.py:218
  21.2 0.1 fusion.1
  21.3 2.7 %collective-permute-start.8 = (f16[192,512]{1,0:T(8,128)(2,1)S(1)}, f16[192,512]{1,0:T(8,128)(2,1)S(1)}, u32[]{:S(2)}, u32[]{:S(2)}) collective-permute-start(f16[192,512]{1,0:T(8,128)(2,1)S(1)} %get-tuple-element.66), channel_id=1, source_target_pairs={{0,8},{4,12},{8,0},{12,4},{1,9},{5,13},{9,1},{13,5},{2,10},{6,14},... | collective-permute-start | bytes 589832 | tf_op jit(solution)/shard_map/ppermute | solution.py:179
  24.0 0.5 collective-permute-start.5
  24.5 5.4 %shard_map.58 = f32[384,512]{1,0:T(8,128)S(1)} custom-call(s32[1]{0:T(128)} %bitcast.10.block, bf16[2048,7168]{1,0:T(8,128)(2,1)} %gradients.7, bf16[7168,384]{1,0:T(8,128)(2,1)} %basis.9), custom_call_target="tpu_custom_call" | custom-call | flops 2818572288 | bytes 12845056 | tf_op jit(solution)/shard_map/pallas_call | solution.py:100
  29.9 2.7 %collective-permute-done.5 = f16[128,512]{1,0:T(8,128)(2,1)S(1)} collective-permute-done((f16[128,512]{1,0:T(8,128)(2,1)S(1)}, f16[128,512]{1,0:T(8,128)(2,1)S(1)}, u32[]{:S(2)}, u32[]{:S(2)}) %collective-permute-start.5) | collective-permute-done | bytes 131104 | tf_op jit(solution)/shard_map/ppermute | solution.py:179
  32.6 0.2 bitcast_add_fusion
  32.8 0.2 collective-permute-start.6
  33.1 2.0 %collective-permute-start.11 = (f16[384,512]{1,0:T(8,128)(2,1)S(1)}, f16[384,512]{1,0:T(8,128)(2,1)S(1)}, u32[]{:S(2)}, u32[]{:S(2)}) collective-permute-start(f16[384,512]{1,0:T(8,128)(2,1)S(1)} %multiply_convert_fusion), channel_id=1, source_target_pairs={{0,4},{4,0},{8,12},{12,8},{1,5},{5,1},{9,13},{13,9},{2,6},{6,2},{1... | collective-permute-start | bytes 1179656 | tf_op jit(solution)/shard_map/ppermute | solution.py:179
  35.1 5.5 %shard_map.59 = f32[384,512]{1,0:T(8,128)S(1)} custom-call(s32[1]{0:T(128)} %bitcast.14.block, bf16[2048,7168]{1,0:T(8,128)(2,1)} %gradients.7, bf16[7168,384]{1,0:T(8,128)(2,1)} %basis.9), custom_call_target="tpu_custom_call" | custom-call | flops 2818572288 | bytes 12845056 | tf_op jit(solution)/shard_map/pallas_call | solution.py:100
  40.6 0.6 collective-permute-done.6
  41.2 2.0 %collective-permute-start.9 = (bf16[128,512]{1,0:T(8,128)(2,1)S(1)}, bf16[128,512]{1,0:T(8,128)(2,1)S(1)}, u32[]{:S(2)}, u32[]{:S(2)}) collective-permute-start(bf16[128,512]{1,0:T(8,128)(2,1)S(1)} %add_convert_fusion.1), channel_id=1, source_target_pairs={{0,2},{1,3},{2,0},{3,1},{4,6},{5,7},{6,4},{7,5},{8,10},{9,11},{10,... | collective-permute-start | bytes 393224 | tf_op jit(solution)/shard_map/ppermute | solution.py:179
  43.2 1.9 %collective-permute-start.12 = (f16[192,512]{1,0:T(8,128)(2,1)S(1)}, f16[192,512]{1,0:T(8,128)(2,1)S(1)}, u32[]{:S(2)}, u32[]{:S(2)}) collective-permute-start(f16[192,512]{1,0:T(8,128)(2,1)S(1)} %get-tuple-element.65), channel_id=1, source_target_pairs={{0,8},{4,12},{8,0},{12,4},{1,9},{5,13},{9,1},{13,5},{2,10},{6,14},... | collective-permute-start | bytes 589832 | tf_op jit(solution)/shard_map/ppermute | solution.py:179
  45.1 1.2 %collective-permute-done.9 = bf16[128,512]{1,0:T(8,128)(2,1)S(1)} collective-permute-done((bf16[128,512]{1,0:T(8,128)(2,1)S(1)}, bf16[128,512]{1,0:T(8,128)(2,1)S(1)}, u32[]{:S(2)}, u32[]{:S(2)}) %collective-permute-start.9) | collective-permute-done | bytes 131104 | tf_op jit(solution)/shard_map/ppermute | solution.py:179
  46.4 5.6 %collective-permute-done.12 = f16[192,512]{1,0:T(8,128)(2,1)S(1)} collective-permute-done((f16[192,512]{1,0:T(8,128)(2,1)S(1)}, f16[192,512]{1,0:T(8,128)(2,1)S(1)}, u32[]{:S(2)}, u32[]{:S(2)}) %collective-permute-start.12) | collective-permute-done | bytes 196640 | tf_op jit(solution)/shard_map/ppermute | solution.py:179
  52.0 0.2 add_convert_fusion.grad
  52.2 0.1 maximum_select_fusion
  52.3 1.1 %shard_map.60 = (f32[128,384]{1,0:T(8,128)S(1)}, bf16[128,384]{1,0:T(8,128)(2,1)S(1)}, bf16[128,384]{1,0:T(8,128)(2,1)S(1)}, bf16[128,384]{1,0:T(8,128)(2,1)S(1)}) custom-call(s32[4]{0:T(128)S(1)} %pad_add_fusion.order, s32[4,512]{1,0:T(4,128)S(1)} %copy-done.2, bf16[512,512]{1,0:T(8,128)(2,1)S(1)} %bitcast.34, bf16[384,512]{1,0:T(8,128)(2,1)S(1)} %add_convert_fusion.grad), custom_call_target="tpu_custom_call" | custom-call | flops 1 | bytes 1 | tf_op jit(solution)/shard_map/pallas_call | solution.py:167
  53.4 2.2 %collective-permute-start.13 = (bf16[128,384]{1,0:T(8,128)(2,1)S(1)}, bf16[128,384]{1,0:T(8,128)(2,1)S(1)}, u32[]{:S(2)}, u32[]{:S(2)}) collective-permute-start(bf16[128,384]{1,0:T(8,128)(2,1)S(1)} %get-tuple-element.62), channel_id=1, source_target_pairs={{0,12},{4,8},{8,4},{12,0},{1,13},{5,9},{9,5},{13,1},{2,14},{6,10},... | collective-permute-start | bytes 294920 | tf_op jit(solution)/shard_map/ppermute | solution.py:179
  55.6 2.3 %collective-permute-start.15 = (bf16[128,384]{1,0:T(8,128)(2,1)S(1)}, bf16[128,384]{1,0:T(8,128)(2,1)S(1)}, u32[]{:S(2)}, u32[]{:S(2)}) collective-permute-start(bf16[128,384]{1,0:T(8,128)(2,1)S(1)} %get-tuple-element.64), channel_id=1, source_target_pairs={{0,4},{4,0},{8,12},{12,8},{1,5},{5,1},{9,13},{13,9},{2,6},{6,2},{1... | collective-permute-start | bytes 294920 | tf_op jit(solution)/shard_map/ppermute | solution.py:179
  57.9 2.1 %collective-permute-done.13 = bf16[128,384]{1,0:T(8,128)(2,1)S(1)} collective-permute-done((bf16[128,384]{1,0:T(8,128)(2,1)S(1)}, bf16[128,384]{1,0:T(8,128)(2,1)S(1)}, u32[]{:S(2)}, u32[]{:S(2)}) %collective-permute-start.13) | collective-permute-done | bytes 98336 | tf_op jit(solution)/shard_map/ppermute | solution.py:179
  60.0 2.1 %collective-permute-done.14 = bf16[128,384]{1,0:T(8,128)(2,1)S(1)} collective-permute-done((bf16[128,384]{1,0:T(8,128)(2,1)S(1)}, bf16[128,384]{1,0:T(8,128)(2,1)S(1)}, u32[]{:S(2)}, u32[]{:S(2)}) %collective-permute-start.14) | collective-permute-done | bytes 98336 | tf_op jit(solution)/shard_map/ppermute | solution.py:179
  62.0 0.7 %convert_add_fusion = f32[128,384]{1,0:T(8,128)} fusion(bf16[128,384]{1,0:T(8,128)(2,1)S(1)} %collective-permute-done.15, bf16[128,384]{1,0:T(8,128)(2,1)S(1)} %collective-permute-done.14, f32[128,384]{1,0:T(8,128)S(1)} %get-tuple-element.61, bf16[128,384]{1,0:T(8,128)(2,1)S(1)} %collective-permute-done.13), kind=kLoop, calls=%fused_computation.23 | loop fusion | flops 294912 | bytes 688128 | tf_op jit(solution)/shard_map/add | solution.py:253
  (27 shorter events, 0.6 us)
Async XLA Ops:
  0.0 9.4 %collective-permute-start = (bf16[2048,512]{1,0:T(8,128)(2,1)}, bf16[2048,512]{1,0:T(8,128)(2,1)}, u32[]{:S(2)}, u32[]{:S(2)}) collective-permute-start(bf16[2048,512]{1,0:T(8,128)(2,1)} %act.1), channel_id=1, source_target_pairs={{0,1},{1,0},{2,3},{3,2},{4,5},{5,4},{6,7},{7,6},{8,9},{9,8},{10,11... | collective-permute-start | bytes 6291464 | tf_op jit(solution)/shard_map/ppermute | solution.py:179
  0.5 9.0 %collective-permute-start.1 = (bf16[512,512]{1,0:T(8,128)(2,1)}, bf16[512,512]{1,0:T(8,128)(2,1)S(1)}, u32[]{:S(2)}, u32[]{:S(2)}) collective-permute-start(bf16[512,512]{1,0:T(8,128)(2,1)} %basis.6), channel_id=1, source_target_pairs={{0,1},{1,0},{2,3},{3,2},{4,5},{5,4},{6,7},{7,6},{8,9},{9,8},{10,11... | collective-permute-start | bytes 1572872 | tf_op jit(solution)/shard_map/ppermute | solution.py:179
  0.5 8.9 %copy-start = (bf16[2048,512]{1,0:T(8,128)(2,1)S(1)}, bf16[2048,512]{1,0:T(8,128)(2,1)}, u32[]{:S(2)}) copy-start(bf16[2048,512]{1,0:T(8,128)(2,1)} %act.1) | copy-start | bytes 6291460
  0.5 8.9 %copy-start.1 = (bf16[512,512]{1,0:T(8,128)(2,1)S(1)}, bf16[512,512]{1,0:T(8,128)(2,1)}, u32[]{:S(2)}) copy-start(bf16[512,512]{1,0:T(8,128)(2,1)} %basis.6) | copy-start | bytes 1572868
  6.2 13.9 %collective-permute-start.4 = (f16[384,512]{1,0:T(8,128)(2,1)S(1)}, f16[384,512]{1,0:T(8,128)(2,1)}, u32[]{:S(2)}, u32[]{:S(2)}) collective-permute-start(f16[384,512]{1,0:T(8,128)(2,1)S(1)} %multiply_convert_fusion.1), channel_id=1, source_target_pairs={{0,4},{4,0},{8,12},{12,8},{1,5},{5,1},{9,13},{13,9},{2,6},{6,2},{1... | collective-permute-start | bytes 1179656 | tf_op jit(solution)/shard_map/ppermute | solution.py:179
  12.4 11.6 %collective-permute-start.3 = (f16[128,512]{1,0:T(8,128)(2,1)S(1)}, f16[128,512]{1,0:T(8,128)(2,1)S(1)}, u32[]{:S(2)}, u32[]{:S(2)}) collective-permute-start(f16[128,512]{1,0:T(8,128)(2,1)S(1)} %multiply_convert_fusion.3), channel_id=1, source_target_pairs={{0,2},{1,3},{2,0},{3,1},{4,6},{5,7},{6,4},{7,5},{8,10},{9,11},{10,... | collective-permute-start | bytes 393224 | tf_op jit(solution)/shard_map/ppermute | solution.py:179
  14.0 18.6 %collective-permute-start.2 = (f16[3,128,512]{2,1,0:T(8,128)(2,1)S(1)}, f16[3,128,512]{2,1,0:T(8,128)(2,1)S(1)}, u32[]{:S(2)}, u32[]{:S(2)}) collective-permute-start(f16[3,128,512]{2,1,0:T(8,128)(2,1)S(1)} %fusion), channel_id=1, source_target_pairs={{0,2},{1,3},{2,0},{3,1},{4,6},{5,7},{6,4},{7,5},{8,10},{9,11},{10,... | collective-permute-start | bytes 1179656 | tf_op jit(solution)/shard_map/ppermute | solution.py:179
  21.3 19.3 %collective-permute-start.8 = (f16[192,512]{1,0:T(8,128)(2,1)S(1)}, f16[192,512]{1,0:T(8,128)(2,1)S(1)}, u32[]{:S(2)}, u32[]{:S(2)}) collective-permute-start(f16[192,512]{1,0:T(8,128)(2,1)S(1)} %get-tuple-element.66), channel_id=1, source_target_pairs={{0,8},{4,12},{8,0},{12,4},{1,9},{5,13},{9,1},{13,5},{2,10},{6,14},... | collective-permute-start | bytes 589832 | tf_op jit(solution)/shard_map/ppermute | solution.py:179
  24.0 8.7 %collective-permute-start.5 = (f16[128,512]{1,0:T(8,128)(2,1)S(1)}, f16[128,512]{1,0:T(8,128)(2,1)S(1)}, u32[]{:S(2)}, u32[]{:S(2)}) collective-permute-start(f16[128,512]{1,0:T(8,128)(2,1)S(1)} %multiply_convert_fusion.2), channel_id=1, source_target_pairs={{0,4},{4,0},{8,12},{12,8},{1,5},{5,1},{9,13},{13,9},{2,6},{6,2},{1... | collective-permute-start | bytes 393224 | tf_op jit(solution)/shard_map/ppermute | solution.py:179
  32.8 8.3 %collective-permute-start.6 = (f16[128,512]{1,0:T(8,128)(2,1)S(1)}, f16[128,512]{1,0:T(8,128)(2,1)S(1)}, u32[]{:S(2)}, u32[]{:S(2)}) collective-permute-start(f16[128,512]{1,0:T(8,128)(2,1)S(1)} %get-tuple-element.68), channel_id=1, source_target_pairs={{0,4},{4,0},{8,12},{12,8},{1,5},{5,1},{9,13},{13,9},{2,6},{6,2},{1... | collective-permute-start | bytes 393224 | tf_op jit(solution)/shard_map/ppermute | solution.py:179
  33.0 8.2 %collective-permute-start.7 = (f16[128,512]{1,0:T(8,128)(2,1)S(1)}, f16[128,512]{1,0:T(8,128)(2,1)S(1)}, u32[]{:S(2)}, u32[]{:S(2)}) collective-permute-start(f16[128,512]{1,0:T(8,128)(2,1)S(1)} %get-tuple-element.69), channel_id=1, source_target_pairs={{0,8},{4,12},{8,0},{12,4},{1,9},{5,13},{9,1},{13,5},{2,10},{6,14},... | collective-permute-start | bytes 393224 | tf_op jit(solution)/shard_map/ppermute | solution.py:179
  33.1 18.9 %collective-permute-start.11 = (f16[384,512]{1,0:T(8,128)(2,1)S(1)}, f16[384,512]{1,0:T(8,128)(2,1)S(1)}, u32[]{:S(2)}, u32[]{:S(2)}) collective-permute-start(f16[384,512]{1,0:T(8,128)(2,1)S(1)} %multiply_convert_fusion), channel_id=1, source_target_pairs={{0,4},{4,0},{8,12},{12,8},{1,5},{5,1},{9,13},{13,9},{2,6},{6,2},{1... | collective-permute-start | bytes 1179656 | tf_op jit(solution)/shard_map/ppermute | solution.py:179
  35.1 17.2 %copy-start.2 = (s32[4,512]{1,0:T(4,128)S(1)}, s32[4,512]{1,0:T(4,128)}, u32[]{:S(2)}) copy-start(s32[4,512]{1,0:T(4,128)} %ids.1) | copy-start | bytes 24580
  41.2 5.0 %collective-permute-start.9 = (bf16[128,512]{1,0:T(8,128)(2,1)S(1)}, bf16[128,512]{1,0:T(8,128)(2,1)S(1)}, u32[]{:S(2)}, u32[]{:S(2)}) collective-permute-start(bf16[128,512]{1,0:T(8,128)(2,1)S(1)} %add_convert_fusion.1), channel_id=1, source_target_pairs={{0,2},{1,3},{2,0},{3,1},{4,6},{5,7},{6,4},{7,5},{8,10},{9,11},{10,... | collective-permute-start | bytes 393224 | tf_op jit(solution)/shard_map/ppermute | solution.py:179
  43.2 8.7 %collective-permute-start.12 = (f16[192,512]{1,0:T(8,128)(2,1)S(1)}, f16[192,512]{1,0:T(8,128)(2,1)S(1)}, u32[]{:S(2)}, u32[]{:S(2)}) collective-permute-start(f16[192,512]{1,0:T(8,128)(2,1)S(1)} %get-tuple-element.65), channel_id=1, source_target_pairs={{0,8},{4,12},{8,0},{12,4},{1,9},{5,13},{9,1},{13,5},{2,10},{6,14},... | collective-permute-start | bytes 589832 | tf_op jit(solution)/shard_map/ppermute | solution.py:179
  46.3 5.9 %collective-permute-start.10 = (bf16[256,512]{1,0:T(8,128)(2,1)S(1)}, bf16[256,512]{1,0:T(8,128)(2,1)S(1)}, u32[]{:S(2)}, u32[]{:S(2)}) collective-permute-start(bf16[256,512]{1,0:T(8,128)(2,1)S(1)} %bitcast.38), channel_id=1, source_target_pairs={{0,1},{1,0},{2,3},{3,2},{4,5},{5,4},{6,7},{7,6},{8,9},{9,8},{10,11... | collective-permute-start | bytes 786440 | tf_op jit(solution)/shard_map/ppermute | solution.py:179
  53.4 6.5 %collective-permute-start.13 = (bf16[128,384]{1,0:T(8,128)(2,1)S(1)}, bf16[128,384]{1,0:T(8,128)(2,1)S(1)}, u32[]{:S(2)}, u32[]{:S(2)}) collective-permute-start(bf16[128,384]{1,0:T(8,128)(2,1)S(1)} %get-tuple-element.62), channel_id=1, source_target_pairs={{0,12},{4,8},{8,4},{12,0},{1,13},{5,9},{9,5},{13,1},{2,14},{6,10},... | collective-permute-start | bytes 294920 | tf_op jit(solution)/shard_map/ppermute | solution.py:179
  55.6 6.4 %collective-permute-start.14 = (bf16[128,384]{1,0:T(8,128)(2,1)S(1)}, bf16[128,384]{1,0:T(8,128)(2,1)S(1)}, u32[]{:S(2)}, u32[]{:S(2)}) collective-permute-start(bf16[128,384]{1,0:T(8,128)(2,1)S(1)} %get-tuple-element.63), channel_id=1, source_target_pairs={{0,8},{4,12},{8,0},{12,4},{1,9},{5,13},{9,1},{13,5},{2,10},{6,14},... | collective-permute-start | bytes 294920 | tf_op jit(solution)/shard_map/ppermute | solution.py:179
  55.6 6.4 %collective-permute-start.15 = (bf16[128,384]{1,0:T(8,128)(2,1)S(1)}, bf16[128,384]{1,0:T(8,128)(2,1)S(1)}, u32[]{:S(2)}, u32[]{:S(2)}) collective-permute-start(bf16[128,384]{1,0:T(8,128)(2,1)S(1)} %get-tuple-element.64), channel_id=1, source_target_pairs={{0,4},{4,0},{8,12},{12,8},{1,5},{5,1},{9,13},{13,9},{2,6},{6,2},{1... | collective-permute-start | bytes 294920 | tf_op jit(solution)/shard_map/ppermute | solution.py:179

commit v4 on v3

--- a/solution.py
+++ b/solution.py
@@ -195,7 +195,7 @@
     quarter = basis_in.shape[1] // 4
     middle = basis_out.shape[1] // 2
     tie = lax.optimization_barrier
-    order = jnp.stack([z, z ^ 3, z ^ 2, z ^ 1])
+    order = jnp.stack([z, z ^ 2, z ^ 3, z ^ 1])
     where = jnp.stack([z, core, x])
 
     far_act, far_basis = swap(activations, "col", 1), swap(basis_in, "col", 1)
@@ -247,12 +247,14 @@
     whole = whole.reshape(4 * quarter, length)
     got_second = jnp.concatenate([got_upper_2, got_lower_2])
     grad = own + unpack(got_first, GRAD_UP) + unpack(got_second, GRAD_UP)
-    tile, to_3, to_2, to_1 = make_tile(order, token_ids, whole, grad.astype(jnp.bfloat16))
-    from_3, from_2, from_1 = swap(to_3, "row", 3), swap(to_2, "row", 2), swap(to_1, "row", 1)
+    tile, to_2, to_3, to_1 = make_tile(order, token_ids, whole, grad.astype(jnp.bfloat16))
+    from_2 = swap(to_2, "row", 2)
+    from_3 = swap(to_3, "row", 3)
+    from_1 = swap(to_1, "row", 1)
     return (
         tile
+        + from_2.astype(jnp.float32)
         + from_3.astype(jnp.float32)
-        + from_2.astype(jnp.float32)
         + from_1.astype(jnp.float32)
     )
 

time: 62.9 us -> 62.7 us (level)
  starting transfers between devices: 19.4 us -> 18.5 us
  waiting for transfers between devices: 14.2 us -> 14.9 us
    ppermute x16, starting transfers between devices: 19.4 us -> 18.5 us  [swap(): return lax.ppermute(value, axis, [(i, i ^ step) for i in range(size)])]
    ppermute x16, waiting for transfers between devices: 14.2 us -> 14.9 us  [swap(): return lax.ppermute(value, axis, [(i, i ^ step) for i in range(size)])]
  transfers between devices with their start and end apart: 16 -> 16, of which waited for: 6 -> 7; matrix products, arithmetic and copies ran while one was open for 3% -> 3% of each run, Pallas kernels for 40% -> 40%
where the time goes in v4:
time: 62.7 us; the launch traced here: 62.5 us
  Pallas kernels  26 us (41%)
  starting transfers between devices  18.5 us (30%)
  waiting for transfers between devices  14.9 us (24%)
  other arithmetic  2.95 us (5%)
    pallas_call x4, Pallas kernels, rotate_grad(): pl.pallas_call(grad_kernel, in_specs=[SMEM, HBM, HBM], out_specs=VMEM, ou...  21.9 us
    ppermute x16, starting transfers between devices, swap(): return lax.ppermute(value, axis, [(i, i ^ step) for i in range(size)])  18.5 us
    ppermute x16, waiting for transfers between devices, swap(): return lax.ppermute(value, axis, [(i, i ^ step) for i in range(size)])  14.9 us
    pallas_call x1, Pallas kernels, rotate_act(): pl.pallas_call(act_kernel, in_specs=[SMEM, VMEM, VMEM, VMEM, VMEM], out_s...  2.9 us
  transfers between devices with their start and end apart: 16, of which 7 were waited for; matrix products, arithmetic and copies ran while one was open for 3% of the time, Pallas kernels for 40%

profile of v4, /device:TPU:0, one launch (start us, length us, event | category | flops | bytes accessed | tf_op | source)
XLA Modules:
  0.0 62.5 jit_solution(12642733776974374635)
XLA Ops:
  0.0 0.5 collective-permute-start
  0.5 5.6 %shard_map.55 = f32[384,512]{1,0:T(8,128)S(1)} custom-call(s32[1]{0:T(128)} %bitcast.block, bf16[2048,7168]{1,0:T(8,128)(2,1)} %gradients.7, bf16[7168,384]{1,0:T(8,128)(2,1)} %basis.9), custom_call_target="tpu_custom_call" | custom-call | flops 2818572288 | bytes 12845056 | tf_op jit(solution)/shard_map/pallas_call | solution.py:100
  6.2 3.1 %collective-permute-start.4 = (f16[384,512]{1,0:T(8,128)(2,1)S(1)}, f16[384,512]{1,0:T(8,128)(2,1)}, u32[]{:S(2)}, u32[]{:S(2)}) collective-permute-start(f16[384,512]{1,0:T(8,128)(2,1)S(1)} %multiply_convert_fusion.1), channel_id=1, source_target_pairs={{0,4},{4,0},{8,12},{12,8},{1,5},{5,1},{9,13},{13,9},{2,6},{6,2},{1... | collective-permute-start | bytes 1179656 | tf_op jit(solution)/shard_map/ppermute | solution.py:179
  9.3 0.1 pad_add_fusion.order
  9.4 2.9 %shard_map.56 = (f32[128,512]{1,0:T(8,128)S(1)}, f32[128,512]{1,0:T(8,128)S(1)}, f32[128,512]{1,0:T(8,128)S(1)}, f32[128,512]{1,0:T(8,128)S(1)}, f32[128,512]{1,...) custom-call(s32[3]{0:T(128)S(1)} %pad_add_fusion.1.where, ...), custom_call_target="tpu_custom_call" | custom-call | flops 1073741824 | bytes 4194304 | tf_op jit(solution)/shard_map/pallas_call | solution.py:136
  12.4 1.6 %collective-permute-start.3 = (f16[128,512]{1,0:T(8,128)(2,1)S(1)}, f16[128,512]{1,0:T(8,128)(2,1)S(1)}, u32[]{:S(2)}, u32[]{:S(2)}) collective-permute-start(f16[128,512]{1,0:T(8,128)(2,1)S(1)} %multiply_convert_fusion.3), channel_id=1, source_target_pairs={{0,2},{1,3},{2,0},{3,1},{4,6},{5,7},{6,4},{7,5},{8,10},{9,11},{10,... | collective-permute-start | bytes 393224 | tf_op jit(solution)/shard_map/ppermute | solution.py:179
  14.0 0.6 collective-permute-start.2
  14.6 5.4 %shard_map.57 = f32[384,512]{1,0:T(8,128)S(1)} custom-call(s32[1]{0:T(128)} %bitcast.9.block, bf16[2048,7168]{1,0:T(8,128)(2,1)} %gradients.7, bf16[7168,384]{1,0:T(8,128)(2,1)} %basis.9), custom_call_target="tpu_custom_call" | custom-call | flops 2818572288 | bytes 12845056 | tf_op jit(solution)/shard_map/pallas_call | solution.py:100
  20.0 1.1 %multiply_add_fusion = f32[384,512]{1,0:T(8,128)S(1)} fusion(f32[384,512]{1,0:T(8,128)S(1)} %shard_map.57, f16[384,512]{1,0:T(8,128)(2,1)} %collective-permute-done.4), kind=kLoop, calls=%fused_computation.4 | loop fusion | flops 589824 | bytes 1966080 | tf_op jit(solution)/shard_map/add | solution.py:218
  21.3 2.7 %collective-permute-start.8 = (f16[192,512]{1,0:T(8,128)(2,1)S(1)}, f16[192,512]{1,0:T(8,128)(2,1)S(1)}, u32[]{:S(2)}, u32[]{:S(2)}) collective-permute-start(f16[192,512]{1,0:T(8,128)(2,1)S(1)} %get-tuple-element.66), channel_id=1, source_target_pairs={{0,8},{4,12},{8,0},{12,4},{1,9},{5,13},{9,1},{13,5},{2,10},{6,14},... | collective-permute-start | bytes 589832 | tf_op jit(solution)/shard_map/ppermute | solution.py:179
  24.0 0.5 collective-permute-start.5
  24.5 5.4 %shard_map.58 = f32[384,512]{1,0:T(8,128)S(1)} custom-call(s32[1]{0:T(128)} %bitcast.10.block, bf16[2048,7168]{1,0:T(8,128)(2,1)} %gradients.7, bf16[7168,384]{1,0:T(8,128)(2,1)} %basis.9), custom_call_target="tpu_custom_call" | custom-call | flops 2818572288 | bytes 12845056 | tf_op jit(solution)/shard_map/pallas_call | solution.py:100
  29.9 2.7 %collective-permute-done.5 = f16[128,512]{1,0:T(8,128)(2,1)S(1)} collective-permute-done((f16[128,512]{1,0:T(8,128)(2,1)S(1)}, f16[128,512]{1,0:T(8,128)(2,1)S(1)}, u32[]{:S(2)}, u32[]{:S(2)}) %collective-permute-start.5) | collective-permute-done | bytes 131104 | tf_op jit(solution)/shard_map/ppermute | solution.py:179
  32.6 0.2 bitcast_add_fusion
  32.8 0.2 collective-permute-start.6
  33.1 2.0 %collective-permute-start.11 = (f16[384,512]{1,0:T(8,128)(2,1)S(1)}, f16[384,512]{1,0:T(8,128)(2,1)S(1)}, u32[]{:S(2)}, u32[]{:S(2)}) collective-permute-start(f16[384,512]{1,0:T(8,128)(2,1)S(1)} %multiply_convert_fusion), channel_id=1, source_target_pairs={{0,4},{4,0},{8,12},{12,8},{1,5},{5,1},{9,13},{13,9},{2,6},{6,2},{1... | collective-permute-start | bytes 1179656 | tf_op jit(solution)/shard_map/ppermute | solution.py:179
  35.1 5.5 %shard_map.59 = f32[384,512]{1,0:T(8,128)S(1)} custom-call(s32[1]{0:T(128)} %bitcast.14.block, bf16[2048,7168]{1,0:T(8,128)(2,1)} %gradients.7, bf16[7168,384]{1,0:T(8,128)(2,1)} %basis.9), custom_call_target="tpu_custom_call" | custom-call | flops 2818572288 | bytes 12845056 | tf_op jit(solution)/shard_map/pallas_call | solution.py:100
  40.6 0.6 collective-permute-done.6
  41.2 2.0 %collective-permute-start.9 = (bf16[128,512]{1,0:T(8,128)(2,1)S(1)}, bf16[128,512]{1,0:T(8,128)(2,1)S(1)}, u32[]{:S(2)}, u32[]{:S(2)}) collective-permute-start(bf16[128,512]{1,0:T(8,128)(2,1)S(1)} %add_convert_fusion.1), channel_id=1, source_target_pairs={{0,2},{1,3},{2,0},{3,1},{4,6},{5,7},{6,4},{7,5},{8,10},{9,11},{10,... | collective-permute-start | bytes 393224 | tf_op jit(solution)/shard_map/ppermute | solution.py:179
  43.2 1.9 %collective-permute-start.12 = (f16[192,512]{1,0:T(8,128)(2,1)S(1)}, f16[192,512]{1,0:T(8,128)(2,1)S(1)}, u32[]{:S(2)}, u32[]{:S(2)}) collective-permute-start(f16[192,512]{1,0:T(8,128)(2,1)S(1)} %get-tuple-element.65), channel_id=1, source_target_pairs={{0,8},{4,12},{8,0},{12,4},{1,9},{5,13},{9,1},{13,5},{2,10},{6,14},... | collective-permute-start | bytes 589832 | tf_op jit(solution)/shard_map/ppermute | solution.py:179
  45.1 1.2 %collective-permute-done.9 = bf16[128,512]{1,0:T(8,128)(2,1)S(1)} collective-permute-done((bf16[128,512]{1,0:T(8,128)(2,1)S(1)}, bf16[128,512]{1,0:T(8,128)(2,1)S(1)}, u32[]{:S(2)}, u32[]{:S(2)}) %collective-permute-start.9) | collective-permute-done | bytes 131104 | tf_op jit(solution)/shard_map/ppermute | solution.py:179
  46.4 5.6 %collective-permute-done.12 = f16[192,512]{1,0:T(8,128)(2,1)S(1)} collective-permute-done((f16[192,512]{1,0:T(8,128)(2,1)S(1)}, f16[192,512]{1,0:T(8,128)(2,1)S(1)}, u32[]{:S(2)}, u32[]{:S(2)}) %collective-permute-start.12) | collective-permute-done | bytes 196640 | tf_op jit(solution)/shard_map/ppermute | solution.py:179
  52.0 0.2 add_convert_fusion.grad
  52.2 0.1 maximum_select_fusion
  52.3 1.1 %shard_map.60 = (f32[128,384]{1,0:T(8,128)S(1)}, bf16[128,384]{1,0:T(8,128)(2,1)S(1)}, bf16[128,384]{1,0:T(8,128)(2,1)S(1)}, bf16[128,384]{1,0:T(8,128)(2,1)S(1)}) custom-call(s32[4]{0:T(128)S(1)} %pad_add_fusion.order, s32[4,512]{1,0:T(4,128)S(1)} %copy-done.2, bf16[512,512]{1,0:T(8,128)(2,1)S(1)} %bitcast.34, bf16[384,512]{1,0:T(8,128)(2,1)S(1)} %add_convert_fusion.grad), custom_call_target="tpu_custom_call" | custom-call | flops 1 | bytes 1 | tf_op jit(solution)/shard_map/pallas_call | solution.py:167
  53.4 1.0 %collective-permute-start.13 = (bf16[128,384]{1,0:T(8,128)(2,1)S(1)}, bf16[128,384]{1,0:T(8,128)(2,1)S(1)}, u32[]{:S(2)}, u32[]{:S(2)}) collective-permute-start(bf16[128,384]{1,0:T(8,128)(2,1)S(1)} %get-tuple-element.62), channel_id=1, source_target_pairs={{0,8},{4,12},{8,0},{12,4},{1,9},{5,13},{9,1},{13,5},{2,10},{6,14},... | collective-permute-start | bytes 294920 | tf_op jit(solution)/shard_map/ppermute | solution.py:179
  54.4 1.3 %collective-permute-start.14 = (bf16[128,384]{1,0:T(8,128)(2,1)S(1)}, bf16[128,384]{1,0:T(8,128)(2,1)S(1)}, u32[]{:S(2)}, u32[]{:S(2)}) collective-permute-start(bf16[128,384]{1,0:T(8,128)(2,1)S(1)} %get-tuple-element.63), channel_id=1, source_target_pairs={{0,12},{4,8},{8,4},{12,0},{1,13},{5,9},{9,5},{13,1},{2,14},{6,10},... | collective-permute-start | bytes 294920 | tf_op jit(solution)/shard_map/ppermute | solution.py:179
  55.7 1.3 %collective-permute-start.15 = (bf16[128,384]{1,0:T(8,128)(2,1)S(1)}, bf16[128,384]{1,0:T(8,128)(2,1)S(1)}, u32[]{:S(2)}, u32[]{:S(2)}) collective-permute-start(bf16[128,384]{1,0:T(8,128)(2,1)S(1)} %get-tuple-element.64), channel_id=1, source_target_pairs={{0,4},{4,0},{8,12},{12,8},{1,5},{5,1},{9,13},{13,9},{2,6},{6,2},{1... | collective-permute-start | bytes 294920 | tf_op jit(solution)/shard_map/ppermute | solution.py:179
  57.0 2.8 %collective-permute-done.13 = bf16[128,384]{1,0:T(8,128)(2,1)S(1)} collective-permute-done((bf16[128,384]{1,0:T(8,128)(2,1)S(1)}, bf16[128,384]{1,0:T(8,128)(2,1)S(1)}, u32[]{:S(2)}, u32[]{:S(2)}) %collective-permute-start.13) | collective-permute-done | bytes 98336 | tf_op jit(solution)/shard_map/ppermute | solution.py:179
  59.8 1.2 %collective-permute-done.14 = bf16[128,384]{1,0:T(8,128)(2,1)S(1)} collective-permute-done((bf16[128,384]{1,0:T(8,128)(2,1)S(1)}, bf16[128,384]{1,0:T(8,128)(2,1)S(1)}, u32[]{:S(2)}, u32[]{:S(2)}) %collective-permute-start.14) | collective-permute-done | bytes 98336 | tf_op jit(solution)/shard_map/ppermute | solution.py:179
  61.0 0.8 %collective-permute-done.15 = bf16[128,384]{1,0:T(8,128)(2,1)S(1)} collective-permute-done((bf16[128,384]{1,0:T(8,128)(2,1)S(1)}, bf16[128,384]{1,0:T(8,128)(2,1)S(1)}, u32[]{:S(2)}, u32[]{:S(2)}) %collective-permute-start.15) | collective-permute-done | bytes 98336 | tf_op jit(solution)/shard_map/ppermute | solution.py:179
  61.8 0.7 %convert_add_fusion = f32[128,384]{1,0:T(8,128)} fusion(bf16[128,384]{1,0:T(8,128)(2,1)S(1)} %collective-permute-done.15, bf16[128,384]{1,0:T(8,128)(2,1)S(1)} %collective-permute-done.14, f32[128,384]{1,0:T(8,128)S(1)} %get-tuple-element.61, bf16[128,384]{1,0:T(8,128)(2,1)S(1)} %collective-permute-done.13), kind=kLoop, calls=%fused_computation.23 | loop fusion | flops 294912 | bytes 688128 | tf_op jit(solution)/shard_map/add | solution.py:255
  (27 shorter events, 0.7 us)
Async XLA Ops:
  0.0 9.4 %collective-permute-start = (bf16[2048,512]{1,0:T(8,128)(2,1)}, bf16[2048,512]{1,0:T(8,128)(2,1)}, u32[]{:S(2)}, u32[]{:S(2)}) collective-permute-start(bf16[2048,512]{1,0:T(8,128)(2,1)} %act.1), channel_id=1, source_target_pairs={{0,1},{1,0},{2,3},{3,2},{4,5},{5,4},{6,7},{7,6},{8,9},{9,8},{10,11... | collective-permute-start | bytes 6291464 | tf_op jit(solution)/shard_map/ppermute | solution.py:179
  0.5 9.0 %collective-permute-start.1 = (bf16[512,512]{1,0:T(8,128)(2,1)}, bf16[512,512]{1,0:T(8,128)(2,1)S(1)}, u32[]{:S(2)}, u32[]{:S(2)}) collective-permute-start(bf16[512,512]{1,0:T(8,128)(2,1)} %basis.6), channel_id=1, source_target_pairs={{0,1},{1,0},{2,3},{3,2},{4,5},{5,4},{6,7},{7,6},{8,9},{9,8},{10,11... | collective-permute-start | bytes 1572872 | tf_op jit(solution)/shard_map/ppermute | solution.py:179
  0.5 8.9 %copy-start = (bf16[2048,512]{1,0:T(8,128)(2,1)S(1)}, bf16[2048,512]{1,0:T(8,128)(2,1)}, u32[]{:S(2)}) copy-start(bf16[2048,512]{1,0:T(8,128)(2,1)} %act.1) | copy-start | bytes 6291460
  0.5 8.9 %copy-start.1 = (bf16[512,512]{1,0:T(8,128)(2,1)S(1)}, bf16[512,512]{1,0:T(8,128)(2,1)}, u32[]{:S(2)}) copy-start(bf16[512,512]{1,0:T(8,128)(2,1)} %basis.6) | copy-start | bytes 1572868
  6.2 13.9 %collective-permute-start.4 = (f16[384,512]{1,0:T(8,128)(2,1)S(1)}, f16[384,512]{1,0:T(8,128)(2,1)}, u32[]{:S(2)}, u32[]{:S(2)}) collective-permute-start(f16[384,512]{1,0:T(8,128)(2,1)S(1)} %multiply_convert_fusion.1), channel_id=1, source_target_pairs={{0,4},{4,0},{8,12},{12,8},{1,5},{5,1},{9,13},{13,9},{2,6},{6,2},{1... | collective-permute-start | bytes 1179656 | tf_op jit(solution)/shard_map/ppermute | solution.py:179
  12.4 11.6 %collective-permute-start.3 = (f16[128,512]{1,0:T(8,128)(2,1)S(1)}, f16[128,512]{1,0:T(8,128)(2,1)S(1)}, u32[]{:S(2)}, u32[]{:S(2)}) collective-permute-start(f16[128,512]{1,0:T(8,128)(2,1)S(1)} %multiply_convert_fusion.3), channel_id=1, source_target_pairs={{0,2},{1,3},{2,0},{3,1},{4,6},{5,7},{6,4},{7,5},{8,10},{9,11},{10,... | collective-permute-start | bytes 393224 | tf_op jit(solution)/shard_map/ppermute | solution.py:179
  14.0 18.6 %collective-permute-start.2 = (f16[3,128,512]{2,1,0:T(8,128)(2,1)S(1)}, f16[3,128,512]{2,1,0:T(8,128)(2,1)S(1)}, u32[]{:S(2)}, u32[]{:S(2)}) collective-permute-start(f16[3,128,512]{2,1,0:T(8,128)(2,1)S(1)} %fusion), channel_id=1, source_target_pairs={{0,2},{1,3},{2,0},{3,1},{4,6},{5,7},{6,4},{7,5},{8,10},{9,11},{10,... | collective-permute-start | bytes 1179656 | tf_op jit(solution)/shard_map/ppermute | solution.py:179
  21.3 19.3 %collective-permute-start.8 = (f16[192,512]{1,0:T(8,128)(2,1)S(1)}, f16[192,512]{1,0:T(8,128)(2,1)S(1)}, u32[]{:S(2)}, u32[]{:S(2)}) collective-permute-start(f16[192,512]{1,0:T(8,128)(2,1)S(1)} %get-tuple-element.66), channel_id=1, source_target_pairs={{0,8},{4,12},{8,0},{12,4},{1,9},{5,13},{9,1},{13,5},{2,10},{6,14},... | collective-permute-start | bytes 589832 | tf_op jit(solution)/shard_map/ppermute | solution.py:179
  24.0 8.7 %collective-permute-start.5 = (f16[128,512]{1,0:T(8,128)(2,1)S(1)}, f16[128,512]{1,0:T(8,128)(2,1)S(1)}, u32[]{:S(2)}, u32[]{:S(2)}) collective-permute-start(f16[128,512]{1,0:T(8,128)(2,1)S(1)} %multiply_convert_fusion.2), channel_id=1, source_target_pairs={{0,4},{4,0},{8,12},{12,8},{1,5},{5,1},{9,13},{13,9},{2,6},{6,2},{1... | collective-permute-start | bytes 393224 | tf_op jit(solution)/shard_map/ppermute | solution.py:179
  32.8 8.3 %collective-permute-start.6 = (f16[128,512]{1,0:T(8,128)(2,1)S(1)}, f16[128,512]{1,0:T(8,128)(2,1)S(1)}, u32[]{:S(2)}, u32[]{:S(2)}) collective-permute-start(f16[128,512]{1,0:T(8,128)(2,1)S(1)} %get-tuple-element.68), channel_id=1, source_target_pairs={{0,4},{4,0},{8,12},{12,8},{1,5},{5,1},{9,13},{13,9},{2,6},{6,2},{1... | collective-permute-start | bytes 393224 | tf_op jit(solution)/shard_map/ppermute | solution.py:179
  33.0 8.2 %collective-permute-start.7 = (f16[128,512]{1,0:T(8,128)(2,1)S(1)}, f16[128,512]{1,0:T(8,128)(2,1)S(1)}, u32[]{:S(2)}, u32[]{:S(2)}) collective-permute-start(f16[128,512]{1,0:T(8,128)(2,1)S(1)} %get-tuple-element.69), channel_id=1, source_target_pairs={{0,8},{4,12},{8,0},{12,4},{1,9},{5,13},{9,1},{13,5},{2,10},{6,14},... | collective-permute-start | bytes 393224 | tf_op jit(solution)/shard_map/ppermute | solution.py:179
  33.1 18.9 %collective-permute-start.11 = (f16[384,512]{1,0:T(8,128)(2,1)S(1)}, f16[384,512]{1,0:T(8,128)(2,1)S(1)}, u32[]{:S(2)}, u32[]{:S(2)}) collective-permute-start(f16[384,512]{1,0:T(8,128)(2,1)S(1)} %multiply_convert_fusion), channel_id=1, source_target_pairs={{0,4},{4,0},{8,12},{12,8},{1,5},{5,1},{9,13},{13,9},{2,6},{6,2},{1... | collective-permute-start | bytes 1179656 | tf_op jit(solution)/shard_map/ppermute | solution.py:179
  35.1 17.2 %copy-start.2 = (s32[4,512]{1,0:T(4,128)S(1)}, s32[4,512]{1,0:T(4,128)}, u32[]{:S(2)}) copy-start(s32[4,512]{1,0:T(4,128)} %ids.1) | copy-start | bytes 24580
  41.2 5.0 %collective-permute-start.9 = (bf16[128,512]{1,0:T(8,128)(2,1)S(1)}, bf16[128,512]{1,0:T(8,128)(2,1)S(1)}, u32[]{:S(2)}, u32[]{:S(2)}) collective-permute-start(bf16[128,512]{1,0:T(8,128)(2,1)S(1)} %add_convert_fusion.1), channel_id=1, source_target_pairs={{0,2},{1,3},{2,0},{3,1},{4,6},{5,7},{6,4},{7,5},{8,10},{9,11},{10,... | collective-permute-start | bytes 393224 | tf_op jit(solution)/shard_map/ppermute | solution.py:179
  43.2 8.7 %collective-permute-start.12 = (f16[192,512]{1,0:T(8,128)(2,1)S(1)}, f16[192,512]{1,0:T(8,128)(2,1)S(1)}, u32[]{:S(2)}, u32[]{:S(2)}) collective-permute-start(f16[192,512]{1,0:T(8,128)(2,1)S(1)} %get-tuple-element.65), channel_id=1, source_target_pairs={{0,8},{4,12},{8,0},{12,4},{1,9},{5,13},{9,1},{13,5},{2,10},{6,14},... | collective-permute-start | bytes 589832 | tf_op jit(solution)/shard_map/ppermute | solution.py:179
  46.3 5.9 %collective-permute-start.10 = (bf16[256,512]{1,0:T(8,128)(2,1)S(1)}, bf16[256,512]{1,0:T(8,128)(2,1)S(1)}, u32[]{:S(2)}, u32[]{:S(2)}) collective-permute-start(bf16[256,512]{1,0:T(8,128)(2,1)S(1)} %bitcast.38), channel_id=1, source_target_pairs={{0,1},{1,0},{2,3},{3,2},{4,5},{5,4},{6,7},{7,6},{8,9},{9,8},{10,11... | collective-permute-start | bytes 786440 | tf_op jit(solution)/shard_map/ppermute | solution.py:179
  53.4 6.3 %collective-permute-start.13 = (bf16[128,384]{1,0:T(8,128)(2,1)S(1)}, bf16[128,384]{1,0:T(8,128)(2,1)S(1)}, u32[]{:S(2)}, u32[]{:S(2)}) collective-permute-start(bf16[128,384]{1,0:T(8,128)(2,1)S(1)} %get-tuple-element.62), channel_id=1, source_target_pairs={{0,8},{4,12},{8,0},{12,4},{1,9},{5,13},{9,1},{13,5},{2,10},{6,14},... | collective-permute-start | bytes 294920 | tf_op jit(solution)/shard_map/ppermute | solution.py:179
  54.4 6.6 %collective-permute-start.14 = (bf16[128,384]{1,0:T(8,128)(2,1)S(1)}, bf16[128,384]{1,0:T(8,128)(2,1)S(1)}, u32[]{:S(2)}, u32[]{:S(2)}) collective-permute-start(bf16[128,384]{1,0:T(8,128)(2,1)S(1)} %get-tuple-element.63), channel_id=1, source_target_pairs={{0,12},{4,8},{8,4},{12,0},{1,13},{5,9},{9,5},{13,1},{2,14},{6,10},... | collective-permute-start | bytes 294920 | tf_op jit(solution)/shard_map/ppermute | solution.py:179
  55.7 6.1 %collective-permute-start.15 = (bf16[128,384]{1,0:T(8,128)(2,1)S(1)}, bf16[128,384]{1,0:T(8,128)(2,1)S(1)}, u32[]{:S(2)}, u32[]{:S(2)}) collective-permute-start(bf16[128,384]{1,0:T(8,128)(2,1)S(1)} %get-tuple-element.64), channel_id=1, source_target_pairs={{0,4},{4,0},{8,12},{12,8},{1,5},{5,1},{9,13},{13,9},{2,6},{6,2},{1... | collective-permute-start | bytes 294920 | tf_op jit(solution)/shard_map/ppermute | solution.py:179

commit v5 on v4

--- a/solution.py
+++ b/solution.py
@@ -215,9 +215,9 @@
     block, out_3, out_210 = tie((z ^ 2, out_3, out_210))
     second = rotate_grad(block, gradients, basis_out, length)
     got_third, second = tie((got_third, second))
-    second = second + unpack(got_third, GRAD_UP)
-    upper_2, lower_2 = pack(second[:middle], GRAD_UP), pack(second[middle:], GRAD_UP)
+    upper_2 = pack(second[:middle] + unpack(got_third[:middle], GRAD_UP), GRAD_UP)
     got_upper_2 = swap(upper_2, "row", 2)
+    got_third, second, upper_2 = tie((got_third, second, upper_2))
     got_3, upper_2 = tie((got_3, upper_2))
     act_3 = pack(mine_3 + unpack(got_3, ACT_UP), ACT_UP)
     over_3 = swap(act_3, "row", 1)
@@ -233,7 +233,9 @@
     first, act_2, act_1, act_0 = tie((first, act_2, act_1, act_0))
     first_out = pack(first, GRAD_UP)
     got_first = swap(first_out, "row", 1)
-    block, first_out = tie((z, first_out))
+    got_third, first_out = tie((got_third, first_out))
+    lower_2 = pack(second[middle:] + unpack(got_third[middle:], GRAD_UP), GRAD_UP)
+    block, first_out, lower_2 = tie((z, first_out, lower_2))
     own = rotate_grad(block, gradients, basis_out, length)
     over_1, over_2, got_upper_2, own = tie((over_1, over_2, got_upper_2, own))
     act = act_0 + unpack(over_1, ACT_UP) + unpack(over_2, ACT_UP)

time: 62.7 us -> 62.3 us (level)
    add x1 -> x0, other arithmetic: 1.13 us -> none  [line_shards(): second = second + unpack(got_third, GRAD_UP)]
    convert_element_type x6 -> x7, other arithmetic: 0.37 us -> 1.19 us  [pack(): return (value * up).astype(jnp.float16)]
where the time goes in v5:
time: 62.3 us; the launch traced here: 62.1 us
  Pallas kernels  25.9 us (42%)
  starting transfers between devices  18.5 us (30%)
  waiting for transfers between devices  14.8 us (24%)
  other arithmetic  2.65 us (4%)
    pallas_call x4, Pallas kernels, rotate_grad(): pl.pallas_call(grad_kernel, in_specs=[SMEM, HBM, HBM], out_specs=VMEM, ou...  21.9 us
    ppermute x16, starting transfers between devices, swap(): return lax.ppermute(value, axis, [(i, i ^ step) for i in range(size)])  18.5 us
    ppermute x16, waiting for transfers between devices, swap(): return lax.ppermute(value, axis, [(i, i ^ step) for i in range(size)])  14.8 us
    pallas_call x1, Pallas kernels, rotate_act(): pl.pallas_call(act_kernel, in_specs=[SMEM, VMEM, VMEM, VMEM, VMEM], out_s...  2.9 us
  transfers between devices with their start and end apart: 16, of which 7 were waited for; matrix products, arithmetic and copies ran while one was open for 3% of the time, Pallas kernels for 40%

profile of v5, /device:TPU:0, one launch (start us, length us, event | category | flops | bytes accessed | tf_op | source)
XLA Modules:
  0.0 62.1 jit_solution(12021279913865870282)
XLA Ops:
  0.0 0.5 collective-permute-start
  0.5 5.6 %shard_map.55 = f32[384,512]{1,0:T(8,128)S(1)} custom-call(s32[1]{0:T(128)} %bitcast.block, bf16[2048,7168]{1,0:T(8,128)(2,1)} %gradients.7, bf16[7168,384]{1,0:T(8,128)(2,1)} %basis.9), custom_call_target="tpu_custom_call" | custom-call | flops 2818572288 | bytes 12845056 | tf_op jit(solution)/shard_map/pallas_call | solution.py:100
  6.1 0.8 %multiply_convert_fusion.1 = f16[384,512]{1,0:T(8,128)(2,1)} fusion(f32[384,512]{1,0:T(8,128)S(1)} %shard_map.55), kind=kLoop, calls=%fused_computation.4 | loop fusion | flops 393216 | bytes 1179648 | tf_op jit(solution)/shard_map/convert_element_type | solution.py:183
  6.9 3.0 %collective-permute-start.7 = (f16[384,512]{1,0:T(8,128)(2,1)}, f16[384,512]{1,0:T(8,128)(2,1)S(1)}, u32[]{:S(2)}, u32[]{:S(2)}) collective-permute-start(f16[384,512]{1,0:T(8,128)(2,1)} %multiply_convert_fusion.1), channel_id=1, source_target_pairs={{0,4},{4,0},{8,12},{12,8},{1,5},{5,1},{9,13},{13,9},{2,6},{6,2},{1... | collective-permute-start | bytes 1179656 | tf_op jit(solution)/shard_map/ppermute | solution.py:179
  10.1 2.9 %shard_map.56 = (f32[128,512]{1,0:T(8,128)S(1)}, f32[128,512]{1,0:T(8,128)S(1)}, f32[128,512]{1,0:T(8,128)S(1)}, f32[128,512]{1,0:T(8,128)S(1)}, f32[128,512]{1,...) custom-call(s32[3]{0:T(128)S(1)} %pad_add_fusion.1.where, ...), custom_call_target="tpu_custom_call" | custom-call | flops 1073741824 | bytes 4194304 | tf_op jit(solution)/shard_map/pallas_call | solution.py:136
  13.0 1.6 %collective-permute-start.3 = (f16[128,512]{1,0:T(8,128)(2,1)S(1)}, f16[128,512]{1,0:T(8,128)(2,1)S(1)}, u32[]{:S(2)}, u32[]{:S(2)}) collective-permute-start(f16[128,512]{1,0:T(8,128)(2,1)S(1)} %multiply_convert_fusion.5), channel_id=1, source_target_pairs={{0,2},{1,3},{2,0},{3,1},{4,6},{5,7},{6,4},{7,5},{8,10},{9,11},{10,... | collective-permute-start | bytes 393224 | tf_op jit(solution)/shard_map/ppermute | solution.py:179
  14.7 0.6 collective-permute-start.2
  15.3 5.4 %shard_map.58 = f32[384,512]{1,0:T(8,128)S(1)} custom-call(s32[1]{0:T(128)} %bitcast.13.block, bf16[2048,7168]{1,0:T(8,128)(2,1)} %gradients.7, bf16[7168,384]{1,0:T(8,128)(2,1)} %basis.9), custom_call_target="tpu_custom_call" | custom-call | flops 2818572288 | bytes 12845056 | tf_op jit(solution)/shard_map/pallas_call | solution.py:100
  20.7 0.1 multiply_convert_fusion.3
  20.8 2.7 %collective-permute-start.8 = (f16[192,512]{1,0:T(8,128)(2,1)S(1)}, f16[192,512]{1,0:T(8,128)(2,1)S(1)}, u32[]{:S(2)}, u32[]{:S(2)}) collective-permute-start(f16[192,512]{1,0:T(8,128)(2,1)S(1)} %multiply_convert_fusion.3), channel_id=1, source_target_pairs={{0,8},{4,12},{8,0},{12,4},{1,9},{5,13},{9,1},{13,5},{2,10},{6,14},... | collective-permute-start | bytes 589832 | tf_op jit(solution)/shard_map/ppermute | solution.py:179
  23.5 0.5 collective-permute-start.4
  24.0 5.4 %shard_map.57 = f32[384,512]{1,0:T(8,128)S(1)} custom-call(s32[1]{0:T(128)} %bitcast.9.block, bf16[2048,7168]{1,0:T(8,128)(2,1)} %gradients.7, bf16[7168,384]{1,0:T(8,128)(2,1)} %basis.9), custom_call_target="tpu_custom_call" | custom-call | flops 2818572288 | bytes 12845056 | tf_op jit(solution)/shard_map/pallas_call | solution.py:100
  29.5 2.6 %collective-permute-done.4 = f16[128,512]{1,0:T(8,128)(2,1)S(1)} collective-permute-done((f16[128,512]{1,0:T(8,128)(2,1)S(1)}, f16[128,512]{1,0:T(8,128)(2,1)S(1)}, u32[]{:S(2)}, u32[]{:S(2)}) %collective-permute-start.4) | collective-permute-done | bytes 131104 | tf_op jit(solution)/shard_map/ppermute | solution.py:179
  32.1 0.2 bitcast_add_fusion
  32.3 0.2 collective-permute-start.5
  32.6 1.9 %collective-permute-start.11 = (f16[384,512]{1,0:T(8,128)(2,1)S(1)}, f16[384,512]{1,0:T(8,128)(2,1)S(1)}, u32[]{:S(2)}, u32[]{:S(2)}) collective-permute-start(f16[384,512]{1,0:T(8,128)(2,1)S(1)} %multiply_convert_fusion), channel_id=1, source_target_pairs={{0,4},{4,0},{8,12},{12,8},{1,5},{5,1},{9,13},{13,9},{2,6},{6,2},{1... | collective-permute-start | bytes 1179656 | tf_op jit(solution)/shard_map/ppermute | solution.py:179
  34.6 5.5 %shard_map.59 = f32[384,512]{1,0:T(8,128)S(1)} custom-call(s32[1]{0:T(128)} %bitcast.14.block, bf16[2048,7168]{1,0:T(8,128)(2,1)} %gradients.7, bf16[7168,384]{1,0:T(8,128)(2,1)} %basis.9), custom_call_target="tpu_custom_call" | custom-call | flops 2818572288 | bytes 12845056 | tf_op jit(solution)/shard_map/pallas_call | solution.py:100
  40.1 0.6 collective-permute-done.5
  40.8 2.0 %collective-permute-start.9 = (bf16[128,512]{1,0:T(8,128)(2,1)S(1)}, bf16[128,512]{1,0:T(8,128)(2,1)S(1)}, u32[]{:S(2)}, u32[]{:S(2)}) collective-permute-start(bf16[128,512]{1,0:T(8,128)(2,1)S(1)} %add_convert_fusion.1), channel_id=1, source_target_pairs={{0,2},{1,3},{2,0},{3,1},{4,6},{5,7},{6,4},{7,5},{8,10},{9,11},{10,... | collective-permute-start | bytes 393224 | tf_op jit(solution)/shard_map/ppermute | solution.py:179
  42.8 1.9 %collective-permute-start.12 = (f16[192,512]{1,0:T(8,128)(2,1)S(1)}, f16[192,512]{1,0:T(8,128)(2,1)S(1)}, u32[]{:S(2)}, u32[]{:S(2)}) collective-permute-start(f16[192,512]{1,0:T(8,128)(2,1)S(1)} %multiply_convert_fusion.2), channel_id=1, source_target_pairs={{0,8},{4,12},{8,0},{12,4},{1,9},{5,13},{9,1},{13,5},{2,10},{6,14},... | collective-permute-start | bytes 589832 | tf_op jit(solution)/shard_map/ppermute | solution.py:179
  44.7 1.1 %collective-permute-done.9 = bf16[128,512]{1,0:T(8,128)(2,1)S(1)} collective-permute-done((bf16[128,512]{1,0:T(8,128)(2,1)S(1)}, bf16[128,512]{1,0:T(8,128)(2,1)S(1)}, u32[]{:S(2)}, u32[]{:S(2)}) %collective-permute-start.9) | collective-permute-done | bytes 131104 | tf_op jit(solution)/shard_map/ppermute | solution.py:179
  45.9 5.5 %collective-permute-done.12 = f16[192,512]{1,0:T(8,128)(2,1)S(1)} collective-permute-done((f16[192,512]{1,0:T(8,128)(2,1)S(1)}, f16[192,512]{1,0:T(8,128)(2,1)S(1)}, u32[]{:S(2)}, u32[]{:S(2)}) %collective-permute-start.12) | collective-permute-done | bytes 196640 | tf_op jit(solution)/shard_map/ppermute | solution.py:179
  51.5 0.2 add_convert_fusion.grad
  51.7 0.1 maximum_select_fusion
  51.8 1.1 %shard_map.60 = (f32[128,384]{1,0:T(8,128)S(1)}, bf16[128,384]{1,0:T(8,128)(2,1)S(1)}, bf16[128,384]{1,0:T(8,128)(2,1)S(1)}, bf16[128,384]{1,0:T(8,128)(2,1)S(1)}) custom-call(s32[4]{0:T(128)S(1)} %pad_add_fusion.order, s32[4,512]{1,0:T(4,128)S(1)} %copy-done.2, bf16[512,512]{1,0:T(8,128)(2,1)S(1)} %bitcast.34, bf16[384,512]{1,0:T(8,128)(2,1)S(1)} %add_convert_fusion.grad), custom_call_target="tpu_custom_call" | custom-call | flops 1 | bytes 1 | tf_op jit(solution)/shard_map/pallas_call | solution.py:167
  53.0 1.0 %collective-permute-start.13 = (bf16[128,384]{1,0:T(8,128)(2,1)S(1)}, bf16[128,384]{1,0:T(8,128)(2,1)S(1)}, u32[]{:S(2)}, u32[]{:S(2)}) collective-permute-start(bf16[128,384]{1,0:T(8,128)(2,1)S(1)} %get-tuple-element.68), channel_id=1, source_target_pairs={{0,8},{4,12},{8,0},{12,4},{1,9},{5,13},{9,1},{13,5},{2,10},{6,14},... | collective-permute-start | bytes 294920 | tf_op jit(solution)/shard_map/ppermute | solution.py:179
  53.9 1.4 %collective-permute-start.14 = (bf16[128,384]{1,0:T(8,128)(2,1)S(1)}, bf16[128,384]{1,0:T(8,128)(2,1)S(1)}, u32[]{:S(2)}, u32[]{:S(2)}) collective-permute-start(bf16[128,384]{1,0:T(8,128)(2,1)S(1)} %get-tuple-element.69), channel_id=1, source_target_pairs={{0,12},{4,8},{8,4},{12,0},{1,13},{5,9},{9,5},{13,1},{2,14},{6,10},... | collective-permute-start | bytes 294920 | tf_op jit(solution)/shard_map/ppermute | solution.py:179
  55.3 1.2 %collective-permute-start.15 = (bf16[128,384]{1,0:T(8,128)(2,1)S(1)}, bf16[128,384]{1,0:T(8,128)(2,1)S(1)}, u32[]{:S(2)}, u32[]{:S(2)}) collective-permute-start(bf16[128,384]{1,0:T(8,128)(2,1)S(1)} %get-tuple-element.70), channel_id=1, source_target_pairs={{0,4},{4,0},{8,12},{12,8},{1,5},{5,1},{9,13},{13,9},{2,6},{6,2},{1... | collective-permute-start | bytes 294920 | tf_op jit(solution)/shard_map/ppermute | solution.py:179
  56.5 2.8 %collective-permute-done.13 = bf16[128,384]{1,0:T(8,128)(2,1)S(1)} collective-permute-done((bf16[128,384]{1,0:T(8,128)(2,1)S(1)}, bf16[128,384]{1,0:T(8,128)(2,1)S(1)}, u32[]{:S(2)}, u32[]{:S(2)}) %collective-permute-start.13) | collective-permute-done | bytes 98336 | tf_op jit(solution)/shard_map/ppermute | solution.py:179
  59.3 1.2 %collective-permute-done.14 = bf16[128,384]{1,0:T(8,128)(2,1)S(1)} collective-permute-done((bf16[128,384]{1,0:T(8,128)(2,1)S(1)}, bf16[128,384]{1,0:T(8,128)(2,1)S(1)}, u32[]{:S(2)}, u32[]{:S(2)}) %collective-permute-start.14) | collective-permute-done | bytes 98336 | tf_op jit(solution)/shard_map/ppermute | solution.py:179
  60.5 0.9 %collective-permute-done.15 = bf16[128,384]{1,0:T(8,128)(2,1)S(1)} collective-permute-done((bf16[128,384]{1,0:T(8,128)(2,1)S(1)}, bf16[128,384]{1,0:T(8,128)(2,1)S(1)}, u32[]{:S(2)}, u32[]{:S(2)}) %collective-permute-start.15) | collective-permute-done | bytes 98336 | tf_op jit(solution)/shard_map/ppermute | solution.py:179
  61.4 0.7 %convert_add_fusion = f32[128,384]{1,0:T(8,128)} fusion(bf16[128,384]{1,0:T(8,128)(2,1)S(1)} %collective-permute-done.15, bf16[128,384]{1,0:T(8,128)(2,1)S(1)} %collective-permute-done.14, f32[128,384]{1,0:T(8,128)S(1)} %get-tuple-element.67, bf16[128,384]{1,0:T(8,128)(2,1)S(1)} %collective-permute-done.13), kind=kLoop, calls=%fused_computation.20 | loop fusion | flops 294912 | bytes 688128 | tf_op jit(solution)/shard_map/add | solution.py:257
  (27 shorter events, 0.7 us)
Async XLA Ops:
  0.0 10.1 %collective-permute-start = (bf16[2048,512]{1,0:T(8,128)(2,1)}, bf16[2048,512]{1,0:T(8,128)(2,1)}, u32[]{:S(2)}, u32[]{:S(2)}) collective-permute-start(bf16[2048,512]{1,0:T(8,128)(2,1)} %act.1), channel_id=1, source_target_pairs={{0,1},{1,0},{2,3},{3,2},{4,5},{5,4},{6,7},{7,6},{8,9},{9,8},{10,11... | collective-permute-start | bytes 6291464 | tf_op jit(solution)/shard_map/ppermute | solution.py:179
  0.5 9.6 %collective-permute-start.1 = (bf16[512,512]{1,0:T(8,128)(2,1)}, bf16[512,512]{1,0:T(8,128)(2,1)S(1)}, u32[]{:S(2)}, u32[]{:S(2)}) collective-permute-start(bf16[512,512]{1,0:T(8,128)(2,1)} %basis.6), channel_id=1, source_target_pairs={{0,1},{1,0},{2,3},{3,2},{4,5},{5,4},{6,7},{7,6},{8,9},{9,8},{10,11... | collective-permute-start | bytes 1572872 | tf_op jit(solution)/shard_map/ppermute | solution.py:179
  0.5 9.6 %copy-start = (bf16[2048,512]{1,0:T(8,128)(2,1)S(1)}, bf16[2048,512]{1,0:T(8,128)(2,1)}, u32[]{:S(2)}) copy-start(bf16[2048,512]{1,0:T(8,128)(2,1)} %act.1) | copy-start | bytes 6291460
  0.5 9.6 %copy-start.1 = (bf16[512,512]{1,0:T(8,128)(2,1)S(1)}, bf16[512,512]{1,0:T(8,128)(2,1)}, u32[]{:S(2)}) copy-start(bf16[512,512]{1,0:T(8,128)(2,1)} %basis.6) | copy-start | bytes 1572868
  6.9 13.8 %collective-permute-start.7 = (f16[384,512]{1,0:T(8,128)(2,1)}, f16[384,512]{1,0:T(8,128)(2,1)S(1)}, u32[]{:S(2)}, u32[]{:S(2)}) collective-permute-start(f16[384,512]{1,0:T(8,128)(2,1)} %multiply_convert_fusion.1), channel_id=1, source_target_pairs={{0,4},{4,0},{8,12},{12,8},{1,5},{5,1},{9,13},{13,9},{2,6},{6,2},{1... | collective-permute-start | bytes 1179656 | tf_op jit(solution)/shard_map/ppermute | solution.py:179
  13.0 10.4 %collective-permute-start.3 = (f16[128,512]{1,0:T(8,128)(2,1)S(1)}, f16[128,512]{1,0:T(8,128)(2,1)S(1)}, u32[]{:S(2)}, u32[]{:S(2)}) collective-permute-start(f16[128,512]{1,0:T(8,128)(2,1)S(1)} %multiply_convert_fusion.5), channel_id=1, source_target_pairs={{0,2},{1,3},{2,0},{3,1},{4,6},{5,7},{6,4},{7,5},{8,10},{9,11},{10,... | collective-permute-start | bytes 393224 | tf_op jit(solution)/shard_map/ppermute | solution.py:179
  14.7 17.4 %collective-permute-start.2 = (f16[3,128,512]{2,1,0:T(8,128)(2,1)S(1)}, f16[3,128,512]{2,1,0:T(8,128)(2,1)S(1)}, u32[]{:S(2)}, u32[]{:S(2)}) collective-permute-start(f16[3,128,512]{2,1,0:T(8,128)(2,1)S(1)} %fusion), channel_id=1, source_target_pairs={{0,2},{1,3},{2,0},{3,1},{4,6},{5,7},{6,4},{7,5},{8,10},{9,11},{10,... | collective-permute-start | bytes 1179656 | tf_op jit(solution)/shard_map/ppermute | solution.py:179
  20.8 19.3 %collective-permute-start.8 = (f16[192,512]{1,0:T(8,128)(2,1)S(1)}, f16[192,512]{1,0:T(8,128)(2,1)S(1)}, u32[]{:S(2)}, u32[]{:S(2)}) collective-permute-start(f16[192,512]{1,0:T(8,128)(2,1)S(1)} %multiply_convert_fusion.3), channel_id=1, source_target_pairs={{0,8},{4,12},{8,0},{12,4},{1,9},{5,13},{9,1},{13,5},{2,10},{6,14},... | collective-permute-start | bytes 589832 | tf_op jit(solution)/shard_map/ppermute | solution.py:179
  23.5 8.6 %collective-permute-start.4 = (f16[128,512]{1,0:T(8,128)(2,1)S(1)}, f16[128,512]{1,0:T(8,128)(2,1)S(1)}, u32[]{:S(2)}, u32[]{:S(2)}) collective-permute-start(f16[128,512]{1,0:T(8,128)(2,1)S(1)} %multiply_convert_fusion.4), channel_id=1, source_target_pairs={{0,4},{4,0},{8,12},{12,8},{1,5},{5,1},{9,13},{13,9},{2,6},{6,2},{1... | collective-permute-start | bytes 393224 | tf_op jit(solution)/shard_map/ppermute | solution.py:179
  32.3 8.4 %collective-permute-start.5 = (f16[128,512]{1,0:T(8,128)(2,1)S(1)}, f16[128,512]{1,0:T(8,128)(2,1)S(1)}, u32[]{:S(2)}, u32[]{:S(2)}) collective-permute-start(f16[128,512]{1,0:T(8,128)(2,1)S(1)} %get-tuple-element.72), channel_id=1, source_target_pairs={{0,4},{4,0},{8,12},{12,8},{1,5},{5,1},{9,13},{13,9},{2,6},{6,2},{1... | collective-permute-start | bytes 393224 | tf_op jit(solution)/shard_map/ppermute | solution.py:179
  32.5 8.2 %collective-permute-start.6 = (f16[128,512]{1,0:T(8,128)(2,1)S(1)}, f16[128,512]{1,0:T(8,128)(2,1)S(1)}, u32[]{:S(2)}, u32[]{:S(2)}) collective-permute-start(f16[128,512]{1,0:T(8,128)(2,1)S(1)} %get-tuple-element.73), channel_id=1, source_target_pairs={{0,8},{4,12},{8,0},{12,4},{1,9},{5,13},{9,1},{13,5},{2,10},{6,14},... | collective-permute-start | bytes 393224 | tf_op jit(solution)/shard_map/ppermute | solution.py:179
  32.6 18.9 %collective-permute-start.11 = (f16[384,512]{1,0:T(8,128)(2,1)S(1)}, f16[384,512]{1,0:T(8,128)(2,1)S(1)}, u32[]{:S(2)}, u32[]{:S(2)}) collective-permute-start(f16[384,512]{1,0:T(8,128)(2,1)S(1)} %multiply_convert_fusion), channel_id=1, source_target_pairs={{0,4},{4,0},{8,12},{12,8},{1,5},{5,1},{9,13},{13,9},{2,6},{6,2},{1... | collective-permute-start | bytes 1179656 | tf_op jit(solution)/shard_map/ppermute | solution.py:179
  34.6 17.2 %copy-start.2 = (s32[4,512]{1,0:T(4,128)S(1)}, s32[4,512]{1,0:T(4,128)}, u32[]{:S(2)}) copy-start(s32[4,512]{1,0:T(4,128)} %ids.1) | copy-start | bytes 24580
  40.8 5.0 %collective-permute-start.9 = (bf16[128,512]{1,0:T(8,128)(2,1)S(1)}, bf16[128,512]{1,0:T(8,128)(2,1)S(1)}, u32[]{:S(2)}, u32[]{:S(2)}) collective-permute-start(bf16[128,512]{1,0:T(8,128)(2,1)S(1)} %add_convert_fusion.1), channel_id=1, source_target_pairs={{0,2},{1,3},{2,0},{3,1},{4,6},{5,7},{6,4},{7,5},{8,10},{9,11},{10,... | collective-permute-start | bytes 393224 | tf_op jit(solution)/shard_map/ppermute | solution.py:179
  42.8 8.7 %collective-permute-start.12 = (f16[192,512]{1,0:T(8,128)(2,1)S(1)}, f16[192,512]{1,0:T(8,128)(2,1)S(1)}, u32[]{:S(2)}, u32[]{:S(2)}) collective-permute-start(f16[192,512]{1,0:T(8,128)(2,1)S(1)} %multiply_convert_fusion.2), channel_id=1, source_target_pairs={{0,8},{4,12},{8,0},{12,4},{1,9},{5,13},{9,1},{13,5},{2,10},{6,14},... | collective-permute-start | bytes 589832 | tf_op jit(solution)/shard_map/ppermute | solution.py:179
  45.9 5.9 %collective-permute-start.10 = (bf16[256,512]{1,0:T(8,128)(2,1)S(1)}, bf16[256,512]{1,0:T(8,128)(2,1)S(1)}, u32[]{:S(2)}, u32[]{:S(2)}) collective-permute-start(bf16[256,512]{1,0:T(8,128)(2,1)S(1)} %bitcast.38), channel_id=1, source_target_pairs={{0,1},{1,0},{2,3},{3,2},{4,5},{5,4},{6,7},{7,6},{8,9},{9,8},{10,11... | collective-permute-start | bytes 786440 | tf_op jit(solution)/shard_map/ppermute | solution.py:179
  53.0 6.3 %collective-permute-start.13 = (bf16[128,384]{1,0:T(8,128)(2,1)S(1)}, bf16[128,384]{1,0:T(8,128)(2,1)S(1)}, u32[]{:S(2)}, u32[]{:S(2)}) collective-permute-start(bf16[128,384]{1,0:T(8,128)(2,1)S(1)} %get-tuple-element.68), channel_id=1, source_target_pairs={{0,8},{4,12},{8,0},{12,4},{1,9},{5,13},{9,1},{13,5},{2,10},{6,14},... | collective-permute-start | bytes 294920 | tf_op jit(solution)/shard_map/ppermute | solution.py:179
  53.9 6.6 %collective-permute-start.14 = (bf16[128,384]{1,0:T(8,128)(2,1)S(1)}, bf16[128,384]{1,0:T(8,128)(2,1)S(1)}, u32[]{:S(2)}, u32[]{:S(2)}) collective-permute-start(bf16[128,384]{1,0:T(8,128)(2,1)S(1)} %get-tuple-element.69), channel_id=1, source_target_pairs={{0,12},{4,8},{8,4},{12,0},{1,13},{5,9},{9,5},{13,1},{2,14},{6,10},... | collective-permute-start | bytes 294920 | tf_op jit(solution)/shard_map/ppermute | solution.py:179
  55.3 6.1 %collective-permute-start.15 = (bf16[128,384]{1,0:T(8,128)(2,1)S(1)}, bf16[128,384]{1,0:T(8,128)(2,1)S(1)}, u32[]{:S(2)}, u32[]{:S(2)}) collective-permute-start(bf16[128,384]{1,0:T(8,128)(2,1)S(1)} %get-tuple-element.70), channel_id=1, source_target_pairs={{0,4},{4,0},{8,12},{12,8},{1,5},{5,1},{9,13},{13,9},{2,6},{6,2},{1... | collective-permute-start | bytes 294920 | tf_op jit(solution)/shard_map/ppermute | solution.py:179

commit v6 on v5

--- a/solution.py
+++ b/solution.py
@@ -119,7 +119,7 @@
 
 def act_kernel(where, act, basis, far_act, far_basis, *outs):
     quarter, length = outs[0].shape
-    z, core, x = where[0], where[1], where[2]
+    z, core, x = where[0], where[4], where[5]
     span = pl.ds(pl.multiple_of(core * 2 * quarter, 2 * quarter), 2 * quarter)
     near = basis[:, span]
     far = far_basis[:, span]
@@ -195,8 +195,7 @@
     quarter = basis_in.shape[1] // 4
     middle = basis_out.shape[1] // 2
     tie = lax.optimization_barrier
-    order = jnp.stack([z, z ^ 2, z ^ 3, z ^ 1])
-    where = jnp.stack([z, core, x])
+    order = jnp.stack([z, z ^ 2, z ^ 3, z ^ 1, core, x])
 
     far_act, far_basis = swap(activations, "col", 1), swap(basis_in, "col", 1)
     third = rotate_grad(z ^ 3, gradients, basis_out, length)
@@ -205,7 +204,7 @@
 
     far_act, far_basis, third, order = tie((far_act, far_basis, third, order))
     mine_3, other_3, mine_2, other_2, mine_1, other_1, mine_0, other_0 = rotate_act(
-        where, activations, basis_in, far_act, far_basis, length
+        order, activations, basis_in, far_act, far_basis, length
     )
     out_3 = pack(other_3, ACT_UP)
     out_210 = pack(jnp.stack([other_2, other_1, other_0]), ACT_UP)

time: 62.3 us -> 62.1 us (level)
  no operation moved by 1% of the time
where the time goes in v6:
time: 62.1 us; the launch traced here: 62 us
  Pallas kernels  25.9 us (42%)
  starting transfers between devices  18.6 us (30%)
  waiting for transfers between devices  14.7 us (24%)
  other arithmetic  2.5 us (4%)
    pallas_call x4, Pallas kernels, rotate_grad(): pl.pallas_call(grad_kernel, in_specs=[SMEM, HBM, HBM], out_specs=VMEM, ou...  21.9 us
    ppermute x16, starting transfers between devices, swap(): return lax.ppermute(value, axis, [(i, i ^ step) for i in range(size)])  18.6 us
    ppermute x16, waiting for transfers between devices, swap(): return lax.ppermute(value, axis, [(i, i ^ step) for i in range(size)])  14.7 us
    pallas_call x1, Pallas kernels, rotate_act(): pl.pallas_call(act_kernel, in_specs=[SMEM, VMEM, VMEM, VMEM, VMEM], out_s...  2.9 us
  transfers between devices with their start and end apart: 16, of which 7 were waited for; matrix products, arithmetic and copies ran while one was open for 3% of the time, Pallas kernels for 40%

profile of v6, /device:TPU:0, one launch (start us, length us, event | category | flops | bytes accessed | tf_op | source)
XLA Modules:
  0.0 62.0 jit_solution(8768338257637609156)
XLA Ops:
  0.0 0.5 collective-permute-start
  0.5 5.6 %shard_map.55 = f32[384,512]{1,0:T(8,128)S(1)} custom-call(s32[1]{0:T(128)} %bitcast.block, bf16[2048,7168]{1,0:T(8,128)(2,1)} %gradients.7, bf16[7168,384]{1,0:T(8,128)(2,1)} %basis.9), custom_call_target="tpu_custom_call" | custom-call | flops 2818572288 | bytes 12845056 | tf_op jit(solution)/shard_map/pallas_call | solution.py:100
  6.1 0.8 %multiply_convert_fusion.1 = f16[384,512]{1,0:T(8,128)(2,1)} fusion(f32[384,512]{1,0:T(8,128)S(1)} %shard_map.55), kind=kLoop, calls=%fused_computation.4 | loop fusion | flops 393216 | bytes 1179648 | tf_op jit(solution)/shard_map/convert_element_type | solution.py:183
  6.9 3.0 %collective-permute-start.7 = (f16[384,512]{1,0:T(8,128)(2,1)}, f16[384,512]{1,0:T(8,128)(2,1)S(1)}, u32[]{:S(2)}, u32[]{:S(2)}) collective-permute-start(f16[384,512]{1,0:T(8,128)(2,1)} %multiply_convert_fusion.1), channel_id=1, source_target_pairs={{0,4},{4,0},{8,12},{12,8},{1,5},{5,1},{9,13},{13,9},{2,6},{6,2},{1... | collective-permute-start | bytes 1179656 | tf_op jit(solution)/shard_map/ppermute | solution.py:179
  9.9 0.1 stack.60.where.order
  10.0 2.9 %shard_map.56 = (f32[128,512]{1,0:T(8,128)S(1)}, f32[128,512]{1,0:T(8,128)S(1)}, f32[128,512]{1,0:T(8,128)S(1)}, f32[128,512]{1,0:T(8,128)S(1)}, f32[128,512]{1,...) custom-call(s32[6]{0:T(128)S(1)} %stack.60.where.order, ...), custom_call_target="tpu_custom_call" | custom-call | flops 1073741824 | bytes 4194304 | tf_op jit(solution)/shard_map/pallas_call | solution.py:136
  13.0 1.6 %collective-permute-start.3 = (f16[128,512]{1,0:T(8,128)(2,1)S(1)}, f16[128,512]{1,0:T(8,128)(2,1)S(1)}, u32[]{:S(2)}, u32[]{:S(2)}) collective-permute-start(f16[128,512]{1,0:T(8,128)(2,1)S(1)} %multiply_convert_fusion.5), channel_id=1, source_target_pairs={{0,2},{1,3},{2,0},{3,1},{4,6},{5,7},{6,4},{7,5},{8,10},{9,11},{10,... | collective-permute-start | bytes 393224 | tf_op jit(solution)/shard_map/ppermute | solution.py:179
  14.6 0.6 collective-permute-start.2
  15.2 5.4 %shard_map.58 = f32[384,512]{1,0:T(8,128)S(1)} custom-call(s32[1]{0:T(128)} %bitcast.13.block, bf16[2048,7168]{1,0:T(8,128)(2,1)} %gradients.7, bf16[7168,384]{1,0:T(8,128)(2,1)} %basis.9), custom_call_target="tpu_custom_call" | custom-call | flops 2818572288 | bytes 12845056 | tf_op jit(solution)/shard_map/pallas_call | solution.py:100
  20.7 2.7 %collective-permute-start.8 = (f16[192,512]{1,0:T(8,128)(2,1)S(1)}, f16[192,512]{1,0:T(8,128)(2,1)S(1)}, u32[]{:S(2)}, u32[]{:S(2)}) collective-permute-start(f16[192,512]{1,0:T(8,128)(2,1)S(1)} %multiply_convert_fusion.3), channel_id=1, source_target_pairs={{0,8},{4,12},{8,0},{12,4},{1,9},{5,13},{9,1},{13,5},{2,10},{6,14},... | collective-permute-start | bytes 589832 | tf_op jit(solution)/shard_map/ppermute | solution.py:179
  23.5 0.6 collective-permute-start.4
  24.0 5.4 %shard_map.57 = f32[384,512]{1,0:T(8,128)S(1)} custom-call(s32[1]{0:T(128)} %bitcast.9.block, bf16[2048,7168]{1,0:T(8,128)(2,1)} %gradients.7, bf16[7168,384]{1,0:T(8,128)(2,1)} %basis.9), custom_call_target="tpu_custom_call" | custom-call | flops 2818572288 | bytes 12845056 | tf_op jit(solution)/shard_map/pallas_call | solution.py:100
  29.5 2.6 %collective-permute-done.4 = f16[128,512]{1,0:T(8,128)(2,1)S(1)} collective-permute-done((f16[128,512]{1,0:T(8,128)(2,1)S(1)}, f16[128,512]{1,0:T(8,128)(2,1)S(1)}, u32[]{:S(2)}, u32[]{:S(2)}) %collective-permute-start.4) | collective-permute-done | bytes 131104 | tf_op jit(solution)/shard_map/ppermute | solution.py:179
  32.1 0.2 bitcast_add_fusion
  32.2 0.2 collective-permute-start.5
  32.6 1.9 %collective-permute-start.11 = (f16[384,512]{1,0:T(8,128)(2,1)S(1)}, f16[384,512]{1,0:T(8,128)(2,1)S(1)}, u32[]{:S(2)}, u32[]{:S(2)}) collective-permute-start(f16[384,512]{1,0:T(8,128)(2,1)S(1)} %multiply_convert_fusion), channel_id=1, source_target_pairs={{0,4},{4,0},{8,12},{12,8},{1,5},{5,1},{9,13},{13,9},{2,6},{6,2},{1... | collective-permute-start | bytes 1179656 | tf_op jit(solution)/shard_map/ppermute | solution.py:179
  34.6 5.5 %shard_map.59 = f32[384,512]{1,0:T(8,128)S(1)} custom-call(s32[1]{0:T(128)} %bitcast.14.block, bf16[2048,7168]{1,0:T(8,128)(2,1)} %gradients.7, bf16[7168,384]{1,0:T(8,128)(2,1)} %basis.9), custom_call_target="tpu_custom_call" | custom-call | flops 2818572288 | bytes 12845056 | tf_op jit(solution)/shard_map/pallas_call | solution.py:100
  40.1 0.6 collective-permute-done.5
  40.7 1.9 %collective-permute-start.9 = (bf16[128,512]{1,0:T(8,128)(2,1)S(1)}, bf16[128,512]{1,0:T(8,128)(2,1)S(1)}, u32[]{:S(2)}, u32[]{:S(2)}) collective-permute-start(bf16[128,512]{1,0:T(8,128)(2,1)S(1)} %add_convert_fusion.1), channel_id=1, source_target_pairs={{0,2},{1,3},{2,0},{3,1},{4,6},{5,7},{6,4},{7,5},{8,10},{9,11},{10,... | collective-permute-start | bytes 393224 | tf_op jit(solution)/shard_map/ppermute | solution.py:179
  42.6 2.0 %collective-permute-start.12 = (f16[192,512]{1,0:T(8,128)(2,1)S(1)}, f16[192,512]{1,0:T(8,128)(2,1)S(1)}, u32[]{:S(2)}, u32[]{:S(2)}) collective-permute-start(f16[192,512]{1,0:T(8,128)(2,1)S(1)} %multiply_convert_fusion.2), channel_id=1, source_target_pairs={{0,8},{4,12},{8,0},{12,4},{1,9},{5,13},{9,1},{13,5},{2,10},{6,14},... | collective-permute-start | bytes 589832 | tf_op jit(solution)/shard_map/ppermute | solution.py:179
  44.6 1.1 %collective-permute-done.9 = bf16[128,512]{1,0:T(8,128)(2,1)S(1)} collective-permute-done((bf16[128,512]{1,0:T(8,128)(2,1)S(1)}, bf16[128,512]{1,0:T(8,128)(2,1)S(1)}, u32[]{:S(2)}, u32[]{:S(2)}) %collective-permute-start.9) | collective-permute-done | bytes 131104 | tf_op jit(solution)/shard_map/ppermute | solution.py:179
  45.9 5.5 %collective-permute-done.12 = f16[192,512]{1,0:T(8,128)(2,1)S(1)} collective-permute-done((f16[192,512]{1,0:T(8,128)(2,1)S(1)}, f16[192,512]{1,0:T(8,128)(2,1)S(1)}, u32[]{:S(2)}, u32[]{:S(2)}) %collective-permute-start.12) | collective-permute-done | bytes 196640 | tf_op jit(solution)/shard_map/ppermute | solution.py:179
  51.3 0.2 add_convert_fusion.grad
  51.6 0.1 maximum_select_fusion
  51.7 1.1 %shard_map.60 = (f32[128,384]{1,0:T(8,128)S(1)}, bf16[128,384]{1,0:T(8,128)(2,1)S(1)}, bf16[128,384]{1,0:T(8,128)(2,1)S(1)}, bf16[128,384]{1,0:T(8,128)(2,1)S(1)}) custom-call(s32[6]{0:T(128)S(1)} %stack.60.where.order, s32[4,512]{1,0:T(4,128)S(1)} %copy-done.2, bf16[512,512]{1,0:T(8,128)(2,1)S(1)} %bitcast.34, bf16[384,512]{1,0:T(8,128)(2,1)S(1)} %add_convert_fusion.grad), custom_call_target="tpu_custom_call" | custom-call | flops 1 | bytes 1 | tf_op jit(solution)/shard_map/pallas_call | solution.py:167
  52.8 1.1 %collective-permute-start.13 = (bf16[128,384]{1,0:T(8,128)(2,1)S(1)}, bf16[128,384]{1,0:T(8,128)(2,1)S(1)}, u32[]{:S(2)}, u32[]{:S(2)}) collective-permute-start(bf16[128,384]{1,0:T(8,128)(2,1)S(1)} %get-tuple-element.68), channel_id=1, source_target_pairs={{0,8},{4,12},{8,0},{12,4},{1,9},{5,13},{9,1},{13,5},{2,10},{6,14},... | collective-permute-start | bytes 294920 | tf_op jit(solution)/shard_map/ppermute | solution.py:179
  53.9 1.4 %collective-permute-start.14 = (bf16[128,384]{1,0:T(8,128)(2,1)S(1)}, bf16[128,384]{1,0:T(8,128)(2,1)S(1)}, u32[]{:S(2)}, u32[]{:S(2)}) collective-permute-start(bf16[128,384]{1,0:T(8,128)(2,1)S(1)} %get-tuple-element.69), channel_id=1, source_target_pairs={{0,12},{4,8},{8,4},{12,0},{1,13},{5,9},{9,5},{13,1},{2,14},{6,10},... | collective-permute-start | bytes 294920 | tf_op jit(solution)/shard_map/ppermute | solution.py:179
  55.2 1.1 %collective-permute-start.15 = (bf16[128,384]{1,0:T(8,128)(2,1)S(1)}, bf16[128,384]{1,0:T(8,128)(2,1)S(1)}, u32[]{:S(2)}, u32[]{:S(2)}) collective-permute-start(bf16[128,384]{1,0:T(8,128)(2,1)S(1)} %get-tuple-element.70), channel_id=1, source_target_pairs={{0,4},{4,0},{8,12},{12,8},{1,5},{5,1},{9,13},{13,9},{2,6},{6,2},{1... | collective-permute-start | bytes 294920 | tf_op jit(solution)/shard_map/ppermute | solution.py:179
  56.4 2.8 %collective-permute-done.13 = bf16[128,384]{1,0:T(8,128)(2,1)S(1)} collective-permute-done((bf16[128,384]{1,0:T(8,128)(2,1)S(1)}, bf16[128,384]{1,0:T(8,128)(2,1)S(1)}, u32[]{:S(2)}, u32[]{:S(2)}) %collective-permute-start.13) | collective-permute-done | bytes 98336 | tf_op jit(solution)/shard_map/ppermute | solution.py:179
  59.2 1.3 %collective-permute-done.14 = bf16[128,384]{1,0:T(8,128)(2,1)S(1)} collective-permute-done((bf16[128,384]{1,0:T(8,128)(2,1)S(1)}, bf16[128,384]{1,0:T(8,128)(2,1)S(1)}, u32[]{:S(2)}, u32[]{:S(2)}) %collective-permute-start.14) | collective-permute-done | bytes 98336 | tf_op jit(solution)/shard_map/ppermute | solution.py:179
  60.5 0.8 %collective-permute-done.15 = bf16[128,384]{1,0:T(8,128)(2,1)S(1)} collective-permute-done((bf16[128,384]{1,0:T(8,128)(2,1)S(1)}, bf16[128,384]{1,0:T(8,128)(2,1)S(1)}, u32[]{:S(2)}, u32[]{:S(2)}) %collective-permute-start.15) | collective-permute-done | bytes 98336 | tf_op jit(solution)/shard_map/ppermute | solution.py:179
  61.3 0.7 %convert_add_fusion = f32[128,384]{1,0:T(8,128)} fusion(bf16[128,384]{1,0:T(8,128)(2,1)S(1)} %collective-permute-done.15, bf16[128,384]{1,0:T(8,128)(2,1)S(1)} %collective-permute-done.14, f32[128,384]{1,0:T(8,128)S(1)} %get-tuple-element.67, bf16[128,384]{1,0:T(8,128)(2,1)S(1)} %collective-permute-done.13), kind=kLoop, calls=%fused_computation.20 | loop fusion | flops 294912 | bytes 688128 | tf_op jit(solution)/shard_map/add | solution.py:256
  (26 shorter events, 0.6 us)
Async XLA Ops:
  0.0 10.0 %collective-permute-start = (bf16[2048,512]{1,0:T(8,128)(2,1)}, bf16[2048,512]{1,0:T(8,128)(2,1)}, u32[]{:S(2)}, u32[]{:S(2)}) collective-permute-start(bf16[2048,512]{1,0:T(8,128)(2,1)} %act.1), channel_id=1, source_target_pairs={{0,1},{1,0},{2,3},{3,2},{4,5},{5,4},{6,7},{7,6},{8,9},{9,8},{10,11... | collective-permute-start | bytes 6291464 | tf_op jit(solution)/shard_map/ppermute | solution.py:179
  0.5 9.6 %collective-permute-start.1 = (bf16[512,512]{1,0:T(8,128)(2,1)}, bf16[512,512]{1,0:T(8,128)(2,1)S(1)}, u32[]{:S(2)}, u32[]{:S(2)}) collective-permute-start(bf16[512,512]{1,0:T(8,128)(2,1)} %basis.6), channel_id=1, source_target_pairs={{0,1},{1,0},{2,3},{3,2},{4,5},{5,4},{6,7},{7,6},{8,9},{9,8},{10,11... | collective-permute-start | bytes 1572872 | tf_op jit(solution)/shard_map/ppermute | solution.py:179
  0.5 9.5 %copy-start = (bf16[2048,512]{1,0:T(8,128)(2,1)S(1)}, bf16[2048,512]{1,0:T(8,128)(2,1)}, u32[]{:S(2)}) copy-start(bf16[2048,512]{1,0:T(8,128)(2,1)} %act.1) | copy-start | bytes 6291460
  0.5 9.5 %copy-start.1 = (bf16[512,512]{1,0:T(8,128)(2,1)S(1)}, bf16[512,512]{1,0:T(8,128)(2,1)}, u32[]{:S(2)}) copy-start(bf16[512,512]{1,0:T(8,128)(2,1)} %basis.6) | copy-start | bytes 1572868
  6.9 13.7 %collective-permute-start.7 = (f16[384,512]{1,0:T(8,128)(2,1)}, f16[384,512]{1,0:T(8,128)(2,1)S(1)}, u32[]{:S(2)}, u32[]{:S(2)}) collective-permute-start(f16[384,512]{1,0:T(8,128)(2,1)} %multiply_convert_fusion.1), channel_id=1, source_target_pairs={{0,4},{4,0},{8,12},{12,8},{1,5},{5,1},{9,13},{13,9},{2,6},{6,2},{1... | collective-permute-start | bytes 1179656 | tf_op jit(solution)/shard_map/ppermute | solution.py:179
  13.0 10.4 %collective-permute-start.3 = (f16[128,512]{1,0:T(8,128)(2,1)S(1)}, f16[128,512]{1,0:T(8,128)(2,1)S(1)}, u32[]{:S(2)}, u32[]{:S(2)}) collective-permute-start(f16[128,512]{1,0:T(8,128)(2,1)S(1)} %multiply_convert_fusion.5), channel_id=1, source_target_pairs={{0,2},{1,3},{2,0},{3,1},{4,6},{5,7},{6,4},{7,5},{8,10},{9,11},{10,... | collective-permute-start | bytes 393224 | tf_op jit(solution)/shard_map/ppermute | solution.py:179
  14.6 17.4 %collective-permute-start.2 = (f16[3,128,512]{2,1,0:T(8,128)(2,1)S(1)}, f16[3,128,512]{2,1,0:T(8,128)(2,1)S(1)}, u32[]{:S(2)}, u32[]{:S(2)}) collective-permute-start(f16[3,128,512]{2,1,0:T(8,128)(2,1)S(1)} %fusion), channel_id=1, source_target_pairs={{0,2},{1,3},{2,0},{3,1},{4,6},{5,7},{6,4},{7,5},{8,10},{9,11},{10,... | collective-permute-start | bytes 1179656 | tf_op jit(solution)/shard_map/ppermute | solution.py:179
  20.7 19.3 %collective-permute-start.8 = (f16[192,512]{1,0:T(8,128)(2,1)S(1)}, f16[192,512]{1,0:T(8,128)(2,1)S(1)}, u32[]{:S(2)}, u32[]{:S(2)}) collective-permute-start(f16[192,512]{1,0:T(8,128)(2,1)S(1)} %multiply_convert_fusion.3), channel_id=1, source_target_pairs={{0,8},{4,12},{8,0},{12,4},{1,9},{5,13},{9,1},{13,5},{2,10},{6,14},... | collective-permute-start | bytes 589832 | tf_op jit(solution)/shard_map/ppermute | solution.py:179
  23.5 8.6 %collective-permute-start.4 = (f16[128,512]{1,0:T(8,128)(2,1)S(1)}, f16[128,512]{1,0:T(8,128)(2,1)S(1)}, u32[]{:S(2)}, u32[]{:S(2)}) collective-permute-start(f16[128,512]{1,0:T(8,128)(2,1)S(1)} %multiply_convert_fusion.4), channel_id=1, source_target_pairs={{0,4},{4,0},{8,12},{12,8},{1,5},{5,1},{9,13},{13,9},{2,6},{6,2},{1... | collective-permute-start | bytes 393224 | tf_op jit(solution)/shard_map/ppermute | solution.py:179
  32.2 8.4 %collective-permute-start.5 = (f16[128,512]{1,0:T(8,128)(2,1)S(1)}, f16[128,512]{1,0:T(8,128)(2,1)S(1)}, u32[]{:S(2)}, u32[]{:S(2)}) collective-permute-start(f16[128,512]{1,0:T(8,128)(2,1)S(1)} %get-tuple-element.72), channel_id=1, source_target_pairs={{0,4},{4,0},{8,12},{12,8},{1,5},{5,1},{9,13},{13,9},{2,6},{6,2},{1... | collective-permute-start | bytes 393224 | tf_op jit(solution)/shard_map/ppermute | solution.py:179
  32.5 8.2 %collective-permute-start.6 = (f16[128,512]{1,0:T(8,128)(2,1)S(1)}, f16[128,512]{1,0:T(8,128)(2,1)S(1)}, u32[]{:S(2)}, u32[]{:S(2)}) collective-permute-start(f16[128,512]{1,0:T(8,128)(2,1)S(1)} %get-tuple-element.73), channel_id=1, source_target_pairs={{0,8},{4,12},{8,0},{12,4},{1,9},{5,13},{9,1},{13,5},{2,10},{6,14},... | collective-permute-start | bytes 393224 | tf_op jit(solution)/shard_map/ppermute | solution.py:179
  32.6 18.8 %collective-permute-start.11 = (f16[384,512]{1,0:T(8,128)(2,1)S(1)}, f16[384,512]{1,0:T(8,128)(2,1)S(1)}, u32[]{:S(2)}, u32[]{:S(2)}) collective-permute-start(f16[384,512]{1,0:T(8,128)(2,1)S(1)} %multiply_convert_fusion), channel_id=1, source_target_pairs={{0,4},{4,0},{8,12},{12,8},{1,5},{5,1},{9,13},{13,9},{2,6},{6,2},{1... | collective-permute-start | bytes 1179656 | tf_op jit(solution)/shard_map/ppermute | solution.py:179
  34.5 17.1 %copy-start.2 = (s32[4,512]{1,0:T(4,128)S(1)}, s32[4,512]{1,0:T(4,128)}, u32[]{:S(2)}) copy-start(s32[4,512]{1,0:T(4,128)} %ids.1) | copy-start | bytes 24580
  40.7 5.0 %collective-permute-start.9 = (bf16[128,512]{1,0:T(8,128)(2,1)S(1)}, bf16[128,512]{1,0:T(8,128)(2,1)S(1)}, u32[]{:S(2)}, u32[]{:S(2)}) collective-permute-start(bf16[128,512]{1,0:T(8,128)(2,1)S(1)} %add_convert_fusion.1), channel_id=1, source_target_pairs={{0,2},{1,3},{2,0},{3,1},{4,6},{5,7},{6,4},{7,5},{8,10},{9,11},{10,... | collective-permute-start | bytes 393224 | tf_op jit(solution)/shard_map/ppermute | solution.py:179
  42.6 8.7 %collective-permute-start.12 = (f16[192,512]{1,0:T(8,128)(2,1)S(1)}, f16[192,512]{1,0:T(8,128)(2,1)S(1)}, u32[]{:S(2)}, u32[]{:S(2)}) collective-permute-start(f16[192,512]{1,0:T(8,128)(2,1)S(1)} %multiply_convert_fusion.2), channel_id=1, source_target_pairs={{0,8},{4,12},{8,0},{12,4},{1,9},{5,13},{9,1},{13,5},{2,10},{6,14},... | collective-permute-start | bytes 589832 | tf_op jit(solution)/shard_map/ppermute | solution.py:179
  45.8 5.8 %collective-permute-start.10 = (bf16[256,512]{1,0:T(8,128)(2,1)S(1)}, bf16[256,512]{1,0:T(8,128)(2,1)S(1)}, u32[]{:S(2)}, u32[]{:S(2)}) collective-permute-start(bf16[256,512]{1,0:T(8,128)(2,1)S(1)} %bitcast.38), channel_id=1, source_target_pairs={{0,1},{1,0},{2,3},{3,2},{4,5},{5,4},{6,7},{7,6},{8,9},{9,8},{10,11... | collective-permute-start | bytes 786440 | tf_op jit(solution)/shard_map/ppermute | solution.py:179
  52.8 6.4 %collective-permute-start.13 = (bf16[128,384]{1,0:T(8,128)(2,1)S(1)}, bf16[128,384]{1,0:T(8,128)(2,1)S(1)}, u32[]{:S(2)}, u32[]{:S(2)}) collective-permute-start(bf16[128,384]{1,0:T(8,128)(2,1)S(1)} %get-tuple-element.68), channel_id=1, source_target_pairs={{0,8},{4,12},{8,0},{12,4},{1,9},{5,13},{9,1},{13,5},{2,10},{6,14},... | collective-permute-start | bytes 294920 | tf_op jit(solution)/shard_map/ppermute | solution.py:179
  53.9 6.6 %collective-permute-start.14 = (bf16[128,384]{1,0:T(8,128)(2,1)S(1)}, bf16[128,384]{1,0:T(8,128)(2,1)S(1)}, u32[]{:S(2)}, u32[]{:S(2)}) collective-permute-start(bf16[128,384]{1,0:T(8,128)(2,1)S(1)} %get-tuple-element.69), channel_id=1, source_target_pairs={{0,12},{4,8},{8,4},{12,0},{1,13},{5,9},{9,5},{13,1},{2,14},{6,10},... | collective-permute-start | bytes 294920 | tf_op jit(solution)/shard_map/ppermute | solution.py:179
  55.2 6.0 %collective-permute-start.15 = (bf16[128,384]{1,0:T(8,128)(2,1)S(1)}, bf16[128,384]{1,0:T(8,128)(2,1)S(1)}, u32[]{:S(2)}, u32[]{:S(2)}) collective-permute-start(bf16[128,384]{1,0:T(8,128)(2,1)S(1)} %get-tuple-element.70), channel_id=1, source_target_pairs={{0,4},{4,0},{8,12},{12,8},{1,5},{5,1},{9,13},{13,9},{2,6},{6,2},{1... | collective-permute-start | bytes 294920 | tf_op jit(solution)/shard_map/ppermute | solution.py:179

commit v7 on v6

--- a/solution.py
+++ b/solution.py
@@ -202,7 +202,7 @@
     third = pack(third, GRAD_UP)
     got_third = swap(third, "row", 1)
 
-    far_act, far_basis, third, order = tie((far_act, far_basis, third, order))
+    far_act, far_basis, third = tie((far_act, far_basis, third))
     mine_3, other_3, mine_2, other_2, mine_1, other_1, mine_0, other_0 = rotate_act(
         order, activations, basis_in, far_act, far_basis, length
     )

time: 62.1 us -> 62.1 us (level)
  no operation moved by 1% of the time
where the time goes in v7:
time: 62.1 us; the launch traced here: 62 us
  Pallas kernels  25.9 us (42%)
  starting transfers between devices  18.6 us (30%)
  waiting for transfers between devices  14.7 us (24%)
  other arithmetic  2.5 us (4%)
    pallas_call x4, Pallas kernels, rotate_grad(): pl.pallas_call(grad_kernel, in_specs=[SMEM, HBM, HBM], out_specs=VMEM, ou...  21.9 us
    ppermute x16, starting transfers between devices, swap(): return lax.ppermute(value, axis, [(i, i ^ step) for i in range(size)])  18.6 us
    ppermute x16, waiting for transfers between devices, swap(): return lax.ppermute(value, axis, [(i, i ^ step) for i in range(size)])  14.7 us
    pallas_call x1, Pallas kernels, rotate_act(): pl.pallas_call(act_kernel, in_specs=[SMEM, VMEM, VMEM, VMEM, VMEM], out_s...  2.9 us
  transfers between devices with their start and end apart: 16, of which 7 were waited for; matrix products, arithmetic and copies ran while one was open for 3% of the time, Pallas kernels for 40%

profile of v7, /device:TPU:0, one launch (start us, length us, event | category | flops | bytes accessed | tf_op | source)
XLA Modules:
  0.0 62.0 jit_solution(8768338257637609156)
XLA Ops:
  0.0 0.5 collective-permute-start
  0.5 5.6 %shard_map.55 = f32[384,512]{1,0:T(8,128)S(1)} custom-call(s32[1]{0:T(128)} %bitcast.2.block, bf16[2048,7168]{1,0:T(8,128)(2,1)} %gradients.7, bf16[7168,384]{1,0:T(8,128)(2,1)} %basis.9), custom_call_target="tpu_custom_call" | custom-call | flops 2818572288 | bytes 12845056 | tf_op jit(solution)/shard_map/pallas_call | solution.py:100
  6.1 0.8 %multiply_convert_fusion.1 = f16[384,512]{1,0:T(8,128)(2,1)} fusion(f32[384,512]{1,0:T(8,128)S(1)} %shard_map.55), kind=kLoop, calls=%fused_computation.4 | loop fusion | flops 393216 | bytes 1179648 | tf_op jit(solution)/shard_map/convert_element_type | solution.py:183
  6.9 3.0 %collective-permute-start.7 = (f16[384,512]{1,0:T(8,128)(2,1)}, f16[384,512]{1,0:T(8,128)(2,1)S(1)}, u32[]{:S(2)}, u32[]{:S(2)}) collective-permute-start(f16[384,512]{1,0:T(8,128)(2,1)} %multiply_convert_fusion.1), channel_id=1, source_target_pairs={{0,4},{4,0},{8,12},{12,8},{1,5},{5,1},{9,13},{13,9},{2,6},{6,2},{1... | collective-permute-start | bytes 1179656 | tf_op jit(solution)/shard_map/ppermute | solution.py:179
  9.9 0.1 stack.63.where.order
  10.0 2.9 %shard_map.56 = (f32[128,512]{1,0:T(8,128)S(1)}, f32[128,512]{1,0:T(8,128)S(1)}, f32[128,512]{1,0:T(8,128)S(1)}, f32[128,512]{1,0:T(8,128)S(1)}, f32[128,512]{1,...) custom-call(s32[6]{0:T(128)S(1)} %stack.63.where.order, ...), custom_call_target="tpu_custom_call" | custom-call | flops 1073741824 | bytes 4194304 | tf_op jit(solution)/shard_map/pallas_call | solution.py:136
  13.0 1.6 %collective-permute-start.3 = (f16[128,512]{1,0:T(8,128)(2,1)S(1)}, f16[128,512]{1,0:T(8,128)(2,1)S(1)}, u32[]{:S(2)}, u32[]{:S(2)}) collective-permute-start(f16[128,512]{1,0:T(8,128)(2,1)S(1)} %multiply_convert_fusion.5), channel_id=1, source_target_pairs={{0,2},{1,3},{2,0},{3,1},{4,6},{5,7},{6,4},{7,5},{8,10},{9,11},{10,... | collective-permute-start | bytes 393224 | tf_op jit(solution)/shard_map/ppermute | solution.py:179
  14.6 0.6 collective-permute-start.2
  15.2 5.4 %shard_map.58 = f32[384,512]{1,0:T(8,128)S(1)} custom-call(s32[1]{0:T(128)} %bitcast.13.block, bf16[2048,7168]{1,0:T(8,128)(2,1)} %gradients.7, bf16[7168,384]{1,0:T(8,128)(2,1)} %basis.9), custom_call_target="tpu_custom_call" | custom-call | flops 2818572288 | bytes 12845056 | tf_op jit(solution)/shard_map/pallas_call | solution.py:100
  20.7 2.7 %collective-permute-start.8 = (f16[192,512]{1,0:T(8,128)(2,1)S(1)}, f16[192,512]{1,0:T(8,128)(2,1)S(1)}, u32[]{:S(2)}, u32[]{:S(2)}) collective-permute-start(f16[192,512]{1,0:T(8,128)(2,1)S(1)} %multiply_convert_fusion.3), channel_id=1, source_target_pairs={{0,8},{4,12},{8,0},{12,4},{1,9},{5,13},{9,1},{13,5},{2,10},{6,14},... | collective-permute-start | bytes 589832 | tf_op jit(solution)/shard_map/ppermute | solution.py:179
  23.5 0.6 collective-permute-start.4
  24.0 5.4 %shard_map.57 = f32[384,512]{1,0:T(8,128)S(1)} custom-call(s32[1]{0:T(128)} %bitcast.9.block, bf16[2048,7168]{1,0:T(8,128)(2,1)} %gradients.7, bf16[7168,384]{1,0:T(8,128)(2,1)} %basis.9), custom_call_target="tpu_custom_call" | custom-call | flops 2818572288 | bytes 12845056 | tf_op jit(solution)/shard_map/pallas_call | solution.py:100
  29.5 2.6 %collective-permute-done.4 = f16[128,512]{1,0:T(8,128)(2,1)S(1)} collective-permute-done((f16[128,512]{1,0:T(8,128)(2,1)S(1)}, f16[128,512]{1,0:T(8,128)(2,1)S(1)}, u32[]{:S(2)}, u32[]{:S(2)}) %collective-permute-start.4) | collective-permute-done | bytes 131104 | tf_op jit(solution)/shard_map/ppermute | solution.py:179
  32.1 0.2 bitcast_add_fusion
  32.2 0.2 collective-permute-start.5
  32.6 1.9 %collective-permute-start.11 = (f16[384,512]{1,0:T(8,128)(2,1)S(1)}, f16[384,512]{1,0:T(8,128)(2,1)S(1)}, u32[]{:S(2)}, u32[]{:S(2)}) collective-permute-start(f16[384,512]{1,0:T(8,128)(2,1)S(1)} %multiply_convert_fusion), channel_id=1, source_target_pairs={{0,4},{4,0},{8,12},{12,8},{1,5},{5,1},{9,13},{13,9},{2,6},{6,2},{1... | collective-permute-start | bytes 1179656 | tf_op jit(solution)/shard_map/ppermute | solution.py:179
  34.6 5.5 %shard_map.59 = f32[384,512]{1,0:T(8,128)S(1)} custom-call(s32[1]{0:T(128)} %bitcast.14.block, bf16[2048,7168]{1,0:T(8,128)(2,1)} %gradients.7, bf16[7168,384]{1,0:T(8,128)(2,1)} %basis.9), custom_call_target="tpu_custom_call" | custom-call | flops 2818572288 | bytes 12845056 | tf_op jit(solution)/shard_map/pallas_call | solution.py:100
  40.1 0.6 collective-permute-done.5
  40.7 1.9 %collective-permute-start.9 = (bf16[128,512]{1,0:T(8,128)(2,1)S(1)}, bf16[128,512]{1,0:T(8,128)(2,1)S(1)}, u32[]{:S(2)}, u32[]{:S(2)}) collective-permute-start(bf16[128,512]{1,0:T(8,128)(2,1)S(1)} %add_convert_fusion.1), channel_id=1, source_target_pairs={{0,2},{1,3},{2,0},{3,1},{4,6},{5,7},{6,4},{7,5},{8,10},{9,11},{10,... | collective-permute-start | bytes 393224 | tf_op jit(solution)/shard_map/ppermute | solution.py:179
  42.6 2.0 %collective-permute-start.12 = (f16[192,512]{1,0:T(8,128)(2,1)S(1)}, f16[192,512]{1,0:T(8,128)(2,1)S(1)}, u32[]{:S(2)}, u32[]{:S(2)}) collective-permute-start(f16[192,512]{1,0:T(8,128)(2,1)S(1)} %multiply_convert_fusion.2), channel_id=1, source_target_pairs={{0,8},{4,12},{8,0},{12,4},{1,9},{5,13},{9,1},{13,5},{2,10},{6,14},... | collective-permute-start | bytes 589832 | tf_op jit(solution)/shard_map/ppermute | solution.py:179
  44.6 1.1 %collective-permute-done.9 = bf16[128,512]{1,0:T(8,128)(2,1)S(1)} collective-permute-done((bf16[128,512]{1,0:T(8,128)(2,1)S(1)}, bf16[128,512]{1,0:T(8,128)(2,1)S(1)}, u32[]{:S(2)}, u32[]{:S(2)}) %collective-permute-start.9) | collective-permute-done | bytes 131104 | tf_op jit(solution)/shard_map/ppermute | solution.py:179
  45.9 5.5 %collective-permute-done.12 = f16[192,512]{1,0:T(8,128)(2,1)S(1)} collective-permute-done((f16[192,512]{1,0:T(8,128)(2,1)S(1)}, f16[192,512]{1,0:T(8,128)(2,1)S(1)}, u32[]{:S(2)}, u32[]{:S(2)}) %collective-permute-start.12) | collective-permute-done | bytes 196640 | tf_op jit(solution)/shard_map/ppermute | solution.py:179
  51.3 0.2 add_convert_fusion.grad
  51.6 0.1 maximum_select_fusion
  51.7 1.1 %shard_map.60 = (f32[128,384]{1,0:T(8,128)S(1)}, bf16[128,384]{1,0:T(8,128)(2,1)S(1)}, bf16[128,384]{1,0:T(8,128)(2,1)S(1)}, bf16[128,384]{1,0:T(8,128)(2,1)S(1)}) custom-call(s32[6]{0:T(128)S(1)} %stack.63.where.order, s32[4,512]{1,0:T(4,128)S(1)} %copy-done.2, bf16[512,512]{1,0:T(8,128)(2,1)S(1)} %bitcast.34, bf16[384,512]{1,0:T(8,128)(2,1)S(1)} %add_convert_fusion.grad), custom_call_target="tpu_custom_call" | custom-call | flops 1 | bytes 1 | tf_op jit(solution)/shard_map/pallas_call | solution.py:167
  52.8 1.1 %collective-permute-start.13 = (bf16[128,384]{1,0:T(8,128)(2,1)S(1)}, bf16[128,384]{1,0:T(8,128)(2,1)S(1)}, u32[]{:S(2)}, u32[]{:S(2)}) collective-permute-start(bf16[128,384]{1,0:T(8,128)(2,1)S(1)} %get-tuple-element.66), channel_id=1, source_target_pairs={{0,8},{4,12},{8,0},{12,4},{1,9},{5,13},{9,1},{13,5},{2,10},{6,14},... | collective-permute-start | bytes 294920 | tf_op jit(solution)/shard_map/ppermute | solution.py:179
  53.9 1.4 %collective-permute-start.14 = (bf16[128,384]{1,0:T(8,128)(2,1)S(1)}, bf16[128,384]{1,0:T(8,128)(2,1)S(1)}, u32[]{:S(2)}, u32[]{:S(2)}) collective-permute-start(bf16[128,384]{1,0:T(8,128)(2,1)S(1)} %get-tuple-element.67), channel_id=1, source_target_pairs={{0,12},{4,8},{8,4},{12,0},{1,13},{5,9},{9,5},{13,1},{2,14},{6,10},... | collective-permute-start | bytes 294920 | tf_op jit(solution)/shard_map/ppermute | solution.py:179
  55.2 1.1 %collective-permute-start.15 = (bf16[128,384]{1,0:T(8,128)(2,1)S(1)}, bf16[128,384]{1,0:T(8,128)(2,1)S(1)}, u32[]{:S(2)}, u32[]{:S(2)}) collective-permute-start(bf16[128,384]{1,0:T(8,128)(2,1)S(1)} %get-tuple-element.68), channel_id=1, source_target_pairs={{0,4},{4,0},{8,12},{12,8},{1,5},{5,1},{9,13},{13,9},{2,6},{6,2},{1... | collective-permute-start | bytes 294920 | tf_op jit(solution)/shard_map/ppermute | solution.py:179
  56.4 2.8 %collective-permute-done.13 = bf16[128,384]{1,0:T(8,128)(2,1)S(1)} collective-permute-done((bf16[128,384]{1,0:T(8,128)(2,1)S(1)}, bf16[128,384]{1,0:T(8,128)(2,1)S(1)}, u32[]{:S(2)}, u32[]{:S(2)}) %collective-permute-start.13) | collective-permute-done | bytes 98336 | tf_op jit(solution)/shard_map/ppermute | solution.py:179
  59.2 1.3 %collective-permute-done.14 = bf16[128,384]{1,0:T(8,128)(2,1)S(1)} collective-permute-done((bf16[128,384]{1,0:T(8,128)(2,1)S(1)}, bf16[128,384]{1,0:T(8,128)(2,1)S(1)}, u32[]{:S(2)}, u32[]{:S(2)}) %collective-permute-start.14) | collective-permute-done | bytes 98336 | tf_op jit(solution)/shard_map/ppermute | solution.py:179
  60.5 0.8 %collective-permute-done.15 = bf16[128,384]{1,0:T(8,128)(2,1)S(1)} collective-permute-done((bf16[128,384]{1,0:T(8,128)(2,1)S(1)}, bf16[128,384]{1,0:T(8,128)(2,1)S(1)}, u32[]{:S(2)}, u32[]{:S(2)}) %collective-permute-start.15) | collective-permute-done | bytes 98336 | tf_op jit(solution)/shard_map/ppermute | solution.py:179
  61.3 0.7 %convert_add_fusion = f32[128,384]{1,0:T(8,128)} fusion(bf16[128,384]{1,0:T(8,128)(2,1)S(1)} %collective-permute-done.15, bf16[128,384]{1,0:T(8,128)(2,1)S(1)} %collective-permute-done.14, f32[128,384]{1,0:T(8,128)S(1)} %get-tuple-element.65, bf16[128,384]{1,0:T(8,128)(2,1)S(1)} %collective-permute-done.13), kind=kLoop, calls=%fused_computation.20 | loop fusion | flops 294912 | bytes 688128 | tf_op jit(solution)/shard_map/add | solution.py:256
  (26 shorter events, 0.6 us)
Async XLA Ops:
  0.0 10.0 %collective-permute-start = (bf16[2048,512]{1,0:T(8,128)(2,1)}, bf16[2048,512]{1,0:T(8,128)(2,1)}, u32[]{:S(2)}, u32[]{:S(2)}) collective-permute-start(bf16[2048,512]{1,0:T(8,128)(2,1)} %act.1), channel_id=1, source_target_pairs={{0,1},{1,0},{2,3},{3,2},{4,5},{5,4},{6,7},{7,6},{8,9},{9,8},{10,11... | collective-permute-start | bytes 6291464 | tf_op jit(solution)/shard_map/ppermute | solution.py:179
  0.5 9.6 %collective-permute-start.1 = (bf16[512,512]{1,0:T(8,128)(2,1)}, bf16[512,512]{1,0:T(8,128)(2,1)S(1)}, u32[]{:S(2)}, u32[]{:S(2)}) collective-permute-start(bf16[512,512]{1,0:T(8,128)(2,1)} %basis.6), channel_id=1, source_target_pairs={{0,1},{1,0},{2,3},{3,2},{4,5},{5,4},{6,7},{7,6},{8,9},{9,8},{10,11... | collective-permute-start | bytes 1572872 | tf_op jit(solution)/shard_map/ppermute | solution.py:179
  0.5 9.5 %copy-start = (bf16[2048,512]{1,0:T(8,128)(2,1)S(1)}, bf16[2048,512]{1,0:T(8,128)(2,1)}, u32[]{:S(2)}) copy-start(bf16[2048,512]{1,0:T(8,128)(2,1)} %act.1) | copy-start | bytes 6291460
  0.5 9.5 %copy-start.1 = (bf16[512,512]{1,0:T(8,128)(2,1)S(1)}, bf16[512,512]{1,0:T(8,128)(2,1)}, u32[]{:S(2)}) copy-start(bf16[512,512]{1,0:T(8,128)(2,1)} %basis.6) | copy-start | bytes 1572868
  6.9 13.7 %collective-permute-start.7 = (f16[384,512]{1,0:T(8,128)(2,1)}, f16[384,512]{1,0:T(8,128)(2,1)S(1)}, u32[]{:S(2)}, u32[]{:S(2)}) collective-permute-start(f16[384,512]{1,0:T(8,128)(2,1)} %multiply_convert_fusion.1), channel_id=1, source_target_pairs={{0,4},{4,0},{8,12},{12,8},{1,5},{5,1},{9,13},{13,9},{2,6},{6,2},{1... | collective-permute-start | bytes 1179656 | tf_op jit(solution)/shard_map/ppermute | solution.py:179
  13.0 10.4 %collective-permute-start.3 = (f16[128,512]{1,0:T(8,128)(2,1)S(1)}, f16[128,512]{1,0:T(8,128)(2,1)S(1)}, u32[]{:S(2)}, u32[]{:S(2)}) collective-permute-start(f16[128,512]{1,0:T(8,128)(2,1)S(1)} %multiply_convert_fusion.5), channel_id=1, source_target_pairs={{0,2},{1,3},{2,0},{3,1},{4,6},{5,7},{6,4},{7,5},{8,10},{9,11},{10,... | collective-permute-start | bytes 393224 | tf_op jit(solution)/shard_map/ppermute | solution.py:179
  14.6 17.4 %collective-permute-start.2 = (f16[3,128,512]{2,1,0:T(8,128)(2,1)S(1)}, f16[3,128,512]{2,1,0:T(8,128)(2,1)S(1)}, u32[]{:S(2)}, u32[]{:S(2)}) collective-permute-start(f16[3,128,512]{2,1,0:T(8,128)(2,1)S(1)} %fusion), channel_id=1, source_target_pairs={{0,2},{1,3},{2,0},{3,1},{4,6},{5,7},{6,4},{7,5},{8,10},{9,11},{10,... | collective-permute-start | bytes 1179656 | tf_op jit(solution)/shard_map/ppermute | solution.py:179
  20.7 19.3 %collective-permute-start.8 = (f16[192,512]{1,0:T(8,128)(2,1)S(1)}, f16[192,512]{1,0:T(8,128)(2,1)S(1)}, u32[]{:S(2)}, u32[]{:S(2)}) collective-permute-start(f16[192,512]{1,0:T(8,128)(2,1)S(1)} %multiply_convert_fusion.3), channel_id=1, source_target_pairs={{0,8},{4,12},{8,0},{12,4},{1,9},{5,13},{9,1},{13,5},{2,10},{6,14},... | collective-permute-start | bytes 589832 | tf_op jit(solution)/shard_map/ppermute | solution.py:179
  23.5 8.6 %collective-permute-start.4 = (f16[128,512]{1,0:T(8,128)(2,1)S(1)}, f16[128,512]{1,0:T(8,128)(2,1)S(1)}, u32[]{:S(2)}, u32[]{:S(2)}) collective-permute-start(f16[128,512]{1,0:T(8,128)(2,1)S(1)} %multiply_convert_fusion.4), channel_id=1, source_target_pairs={{0,4},{4,0},{8,12},{12,8},{1,5},{5,1},{9,13},{13,9},{2,6},{6,2},{1... | collective-permute-start | bytes 393224 | tf_op jit(solution)/shard_map/ppermute | solution.py:179
  32.2 8.4 %collective-permute-start.5 = (f16[128,512]{1,0:T(8,128)(2,1)S(1)}, f16[128,512]{1,0:T(8,128)(2,1)S(1)}, u32[]{:S(2)}, u32[]{:S(2)}) collective-permute-start(f16[128,512]{1,0:T(8,128)(2,1)S(1)} %get-tuple-element.70), channel_id=1, source_target_pairs={{0,4},{4,0},{8,12},{12,8},{1,5},{5,1},{9,13},{13,9},{2,6},{6,2},{1... | collective-permute-start | bytes 393224 | tf_op jit(solution)/shard_map/ppermute | solution.py:179
  32.5 8.2 %collective-permute-start.6 = (f16[128,512]{1,0:T(8,128)(2,1)S(1)}, f16[128,512]{1,0:T(8,128)(2,1)S(1)}, u32[]{:S(2)}, u32[]{:S(2)}) collective-permute-start(f16[128,512]{1,0:T(8,128)(2,1)S(1)} %get-tuple-element.71), channel_id=1, source_target_pairs={{0,8},{4,12},{8,0},{12,4},{1,9},{5,13},{9,1},{13,5},{2,10},{6,14},... | collective-permute-start | bytes 393224 | tf_op jit(solution)/shard_map/ppermute | solution.py:179
  32.6 18.8 %collective-permute-start.11 = (f16[384,512]{1,0:T(8,128)(2,1)S(1)}, f16[384,512]{1,0:T(8,128)(2,1)S(1)}, u32[]{:S(2)}, u32[]{:S(2)}) collective-permute-start(f16[384,512]{1,0:T(8,128)(2,1)S(1)} %multiply_convert_fusion), channel_id=1, source_target_pairs={{0,4},{4,0},{8,12},{12,8},{1,5},{5,1},{9,13},{13,9},{2,6},{6,2},{1... | collective-permute-start | bytes 1179656 | tf_op jit(solution)/shard_map/ppermute | solution.py:179
  34.5 17.1 %copy-start.2 = (s32[4,512]{1,0:T(4,128)S(1)}, s32[4,512]{1,0:T(4,128)}, u32[]{:S(2)}) copy-start(s32[4,512]{1,0:T(4,128)} %ids.1) | copy-start | bytes 24580
  40.7 5.0 %collective-permute-start.9 = (bf16[128,512]{1,0:T(8,128)(2,1)S(1)}, bf16[128,512]{1,0:T(8,128)(2,1)S(1)}, u32[]{:S(2)}, u32[]{:S(2)}) collective-permute-start(bf16[128,512]{1,0:T(8,128)(2,1)S(1)} %add_convert_fusion.1), channel_id=1, source_target_pairs={{0,2},{1,3},{2,0},{3,1},{4,6},{5,7},{6,4},{7,5},{8,10},{9,11},{10,... | collective-permute-start | bytes 393224 | tf_op jit(solution)/shard_map/ppermute | solution.py:179
  42.6 8.7 %collective-permute-start.12 = (f16[192,512]{1,0:T(8,128)(2,1)S(1)}, f16[192,512]{1,0:T(8,128)(2,1)S(1)}, u32[]{:S(2)}, u32[]{:S(2)}) collective-permute-start(f16[192,512]{1,0:T(8,128)(2,1)S(1)} %multiply_convert_fusion.2), channel_id=1, source_target_pairs={{0,8},{4,12},{8,0},{12,4},{1,9},{5,13},{9,1},{13,5},{2,10},{6,14},... | collective-permute-start | bytes 589832 | tf_op jit(solution)/shard_map/ppermute | solution.py:179
  45.8 5.8 %collective-permute-start.10 = (bf16[256,512]{1,0:T(8,128)(2,1)S(1)}, bf16[256,512]{1,0:T(8,128)(2,1)S(1)}, u32[]{:S(2)}, u32[]{:S(2)}) collective-permute-start(bf16[256,512]{1,0:T(8,128)(2,1)S(1)} %bitcast.38), channel_id=1, source_target_pairs={{0,1},{1,0},{2,3},{3,2},{4,5},{5,4},{6,7},{7,6},{8,9},{9,8},{10,11... | collective-permute-start | bytes 786440 | tf_op jit(solution)/shard_map/ppermute | solution.py:179
  52.8 6.4 %collective-permute-start.13 = (bf16[128,384]{1,0:T(8,128)(2,1)S(1)}, bf16[128,384]{1,0:T(8,128)(2,1)S(1)}, u32[]{:S(2)}, u32[]{:S(2)}) collective-permute-start(bf16[128,384]{1,0:T(8,128)(2,1)S(1)} %get-tuple-element.66), channel_id=1, source_target_pairs={{0,8},{4,12},{8,0},{12,4},{1,9},{5,13},{9,1},{13,5},{2,10},{6,14},... | collective-permute-start | bytes 294920 | tf_op jit(solution)/shard_map/ppermute | solution.py:179
  53.9 6.6 %collective-permute-start.14 = (bf16[128,384]{1,0:T(8,128)(2,1)S(1)}, bf16[128,384]{1,0:T(8,128)(2,1)S(1)}, u32[]{:S(2)}, u32[]{:S(2)}) collective-permute-start(bf16[128,384]{1,0:T(8,128)(2,1)S(1)} %get-tuple-element.67), channel_id=1, source_target_pairs={{0,12},{4,8},{8,4},{12,0},{1,13},{5,9},{9,5},{13,1},{2,14},{6,10},... | collective-permute-start | bytes 294920 | tf_op jit(solution)/shard_map/ppermute | solution.py:179
  55.2 6.0 %collective-permute-start.15 = (bf16[128,384]{1,0:T(8,128)(2,1)S(1)}, bf16[128,384]{1,0:T(8,128)(2,1)S(1)}, u32[]{:S(2)}, u32[]{:S(2)}) collective-permute-start(bf16[128,384]{1,0:T(8,128)(2,1)S(1)} %get-tuple-element.68), channel_id=1, source_target_pairs={{0,4},{4,0},{8,12},{12,8},{1,5},{5,1},{9,13},{13,9},{2,6},{6,2},{1... | collective-permute-start | bytes 294920 | tf_op jit(solution)/shard_map/ppermute | solution.py:179
